TPU v7x, 128 devices: a whole 4x4x4 slice. The times are simulated.
128 devices in a mesh: fsdp: 8 (over x_hi, z), seq: 2 (over x_lo), tp: 8 (over y, core).
Axes of the slice: x: 4 (x_hi: 2, x_lo: 2; x = x_hi * 2 + x_lo), y: 4, z: 4, core: 2. Of those that a mesh axis runs over, the one named last changes fastest.
Arguments:
- hidden_in: bfloat16 [24, 256, 1280], P('fsdp', 'seq'), may hold values from -6 to 6
- cotangent: bfloat16 [24, 256, 1280], P('fsdp', 'seq'), may hold values from -6 to 6
- lengths: int32 [24], P('fsdp'), may hold values from 1 to 256, as said below
- qkv_weight: bfloat16 [2, 3, 1280, 1280], P(None, None, ('fsdp', 'seq'), 'tp'), may hold values from -0.15625 to 0.15625
- qv_bias: bfloat16 [2, 2, 1280], P(None, None, 'tp'), may hold values from -4 to 4
- out_weight: bfloat16 [2, 1280, 1280], P(None, 'tp', ('fsdp', 'seq')), may hold values from -1 to 1
- out_bias: bfloat16 [2, 1280], P(None, ('fsdp', 'seq')), may hold values from -4 to 4
- up_weight: bfloat16 [2, 1280, 5120], P(None, ('fsdp', 'seq'), 'tp'), may hold values from -0.15625 to 0.15625
- up_bias: bfloat16 [2, 5120], P(None, 'tp'), may hold values from -6 to 6
- down_weight: bfloat16 [2, 5120, 1280], P(None, 'tp', ('fsdp', 'seq')), may hold values from -0.078125 to 0.078125
- down_bias: bfloat16 [2, 1280], P(None, ('fsdp', 'seq')), may hold values from -4 to 4
- ln_gain: bfloat16 [2, 2, 1280], P(None, None, ('fsdp', 'seq')), may hold values from 0.5 to 1.5
- ln_bias: bfloat16 [2, 2, 1280], P(None, None, ('fsdp', 'seq')), may hold values from -4 to 4
Outputs:
- out_hidden: float32 [24, 256, 1280], P('fsdp', 'seq')
- in_grad: float32 [24, 256, 1280], P('fsdp', 'seq')
- qkv_grad: float32 [2, 3, 1280, 1280], P(None, None, ('fsdp', 'seq'), 'tp')
- qv_bias_grad: float32 [2, 2, 1280], P(None, None, 'tp')
- out_weight_grad: float32 [2, 1280, 1280], P(None, 'tp', ('fsdp', 'seq'))
- out_bias_grad: float32 [2, 1280], P(None, ('fsdp', 'seq'))
- up_weight_grad: float32 [2, 1280, 5120], P(None, ('fsdp', 'seq'), 'tp')
- up_bias_grad: float32 [2, 5120], P(None, 'tp')
- down_weight_grad: float32 [2, 5120, 1280], P(None, 'tp', ('fsdp', 'seq'))
- down_bias_grad: float32 [2, 1280], P(None, ('fsdp', 'seq'))
- ln_gain_grad: float32 [2, 2, 1280], P(None, None, ('fsdp', 'seq'))
- ln_bias_grad: float32 [2, 2, 1280], P(None, None, ('fsdp', 'seq'))
Inputs may be any that keep to these rules, and one draw needn't show every extreme that they name: `lengths`: clip c is on index c // 3 of fsdp, as micro-batch c % 3; among the 3 clips of each index of fsdp one has 256 valid tokens.
All inputs are finite; a program needn't handle non-finite values.
Results may differ from a plain program's by a relative error of at most 0.024.
Values may be sent and summed in bfloat16 or wider, within the bound.
A program may use at most 128 MiB of HBM per device.

v0:
```python
from functools import partial
import math

import jax
import jax.numpy as jnp
from jax import lax
from jax.sharding import PartitionSpec as P

HD = 80


EPSILON = 1e-05
MASKED = -1000000000.0


def layer_norm(values, gain_vec, shift_vec):
    row_mean = jnp.mean(values, axis=-1, keepdims=True)
    centred = values - row_mean
    row_var = jnp.mean(centred * centred, axis=-1, keepdims=True)
    return centred * lax.rsqrt(row_var + EPSILON) * gain_vec + shift_vec


def branch_total(partial_sum):
    return lax.psum(partial_sum.astype(jnp.bfloat16), "tp").astype(jnp.float32)


def input_total(partial_sum):
    return lax.psum(partial_sum.astype(jnp.bfloat16), "tp").astype(jnp.float32)


def forward_layer(hidden, weights, biases, length):
    w_qkv, w_out, w_up, w_down, b_out, b_down, gain_rows, shift_rows = weights
    b_qv, b_up = biases
    gain_rows = gain_rows.astype(jnp.float32)
    shift_rows = shift_rows.astype(jnp.float32)
    normed = layer_norm(hidden, gain_rows[0], shift_rows[0]).astype(jnp.bfloat16)
    projected = jnp.einsum("cd,jde->jce", normed, w_qkv, preferred_element_type=jnp.float32)
    queries = (projected[0] + b_qv[0]).astype(jnp.bfloat16)
    keys_own = projected[1].astype(jnp.bfloat16)
    values_own = (projected[2] + b_qv[1]).astype(jnp.bfloat16)
    keys_all, values_all = (
        lax.all_gather(keys_own, "seq", axis=0, tiled=True),
        lax.all_gather(values_own, "seq", axis=0, tiled=True),
    )
    row_count, local_width = queries.shape
    head_count = local_width // HD
    key_count = keys_all.shape[0]
    scaling = 1.0 / math.sqrt(HD)
    query_heads = queries.reshape(row_count, head_count, HD)
    key_heads = keys_all.reshape(key_count, head_count, HD)
    value_heads = values_all.reshape(key_count, head_count, HD)
    scores = (
        jnp.einsum("qhe,khe->hqk", query_heads, key_heads, preferred_element_type=jnp.float32)
        * scaling
    )
    key_live = jnp.arange(key_count) < length
    scores = jnp.where(key_live[None, None, :], scores, MASKED)
    soft_probs = jax.nn.softmax(scores, axis=-1)
    probs_low = soft_probs.astype(jnp.bfloat16)
    attended = jnp.einsum(
        "hqk,khe->qhe", probs_low, value_heads, preferred_element_type=jnp.float32
    )
    attended = attended.reshape(row_count, local_width).astype(jnp.bfloat16)
    attn_out = branch_total(
        jnp.dot(attended, w_out, preferred_element_type=jnp.float32)
    ) + b_out.astype(jnp.float32)
    middle = hidden + attn_out
    normed_two = layer_norm(middle, gain_rows[1], shift_rows[1]).astype(jnp.bfloat16)
    pre_act = jnp.dot(normed_two, w_up, preferred_element_type=jnp.float32) + b_up
    activated = jax.nn.gelu(pre_act, approximate=False).astype(jnp.bfloat16)
    mlp_out = branch_total(
        jnp.dot(activated, w_down, preferred_element_type=jnp.float32)
    ) + b_down.astype(jnp.float32)
    saved = (
        normed,
        query_heads,
        key_heads,
        value_heads,
        soft_probs,
        probs_low,
        attended,
        middle,
        normed_two,
        pre_act,
        activated,
    )
    return (middle + mlp_out, saved)


def backward_layer(hidden, weights, biases, length, grad_out):
    w_qkv, w_out, w_up, w_down, b_out, b_down, gain_rows, shift_rows = weights
    gain_f = gain_rows.astype(jnp.float32)
    shift_f = shift_rows.astype(jnp.float32)
    _, saved = forward_layer(hidden, weights, biases, length)
    (
        normed,
        query_heads,
        key_heads,
        value_heads,
        soft_probs,
        probs_low,
        attended,
        middle,
        normed_two,
        pre_act,
        activated,
    ) = saved
    row_count, local_width = attended.shape
    head_count = local_width // HD
    key_count = key_heads.shape[0]
    scaling = 1.0 / math.sqrt(HD)
    grad_bdown = jnp.sum(grad_out, axis=0)
    grad_y = grad_out.astype(jnp.bfloat16)
    grad_wdown = jnp.einsum("cf,cd->fd", activated, grad_y, preferred_element_type=jnp.float32)
    grad_act = jnp.einsum("cd,fd->cf", grad_y, w_down, preferred_element_type=jnp.float32)
    _, gelu_back = jax.vjp(partial(jax.nn.gelu, approximate=False), pre_act)
    grad_pre = gelu_back(grad_act)[0].astype(jnp.bfloat16)
    grad_bup = jnp.sum(grad_pre.astype(jnp.float32), axis=0)
    grad_wup = jnp.einsum("cd,cf->df", normed_two, grad_pre, preferred_element_type=jnp.float32)
    grad_norm_two = input_total(
        jnp.einsum("cf,df->cd", grad_pre, w_up, preferred_element_type=jnp.float32)
    )
    _, norm_back_two = jax.vjp(layer_norm, middle, gain_f[1], shift_f[1])
    grad_mid, gain_grad_two, shift_grad_two = norm_back_two(grad_norm_two)
    grad_mid = grad_out + grad_mid
    grad_bout = jnp.sum(grad_mid, axis=0)
    grad_mid_low = grad_mid.astype(jnp.bfloat16)
    grad_wout = jnp.einsum("cq,cd->qd", attended, grad_mid_low, preferred_element_type=jnp.float32)
    grad_att = jnp.einsum(
        "cd,qd->cq", grad_mid_low, w_out, preferred_element_type=jnp.float32
    ).astype(jnp.bfloat16)
    grad_att = grad_att.reshape(row_count, head_count, HD)
    grad_probs = jnp.einsum(
        "qhe,khe->hqk", grad_att, value_heads, preferred_element_type=jnp.float32
    )
    grad_values = jnp.einsum(
        "hqk,qhe->khe", probs_low, grad_att, preferred_element_type=jnp.float32
    )
    grad_scores = soft_probs * (
        grad_probs - jnp.sum(soft_probs * grad_probs, axis=-1, keepdims=True)
    )
    grad_scores = grad_scores.astype(jnp.bfloat16)
    grad_queries = (
        jnp.einsum("hqk,khe->qhe", grad_scores, key_heads, preferred_element_type=jnp.float32)
        * scaling
    )
    grad_keys = (
        jnp.einsum("hqk,qhe->khe", grad_scores, query_heads, preferred_element_type=jnp.float32)
        * scaling
    )
    own_keys, own_values = (
        lax.psum_scatter(
            grad_keys.reshape(key_count, local_width).astype(jnp.bfloat16),
            "seq",
            scatter_dimension=0,
            tiled=True,
        ).astype(jnp.float32),
        lax.psum_scatter(
            grad_values.reshape(key_count, local_width).astype(jnp.bfloat16),
            "seq",
            scatter_dimension=0,
            tiled=True,
        ).astype(jnp.float32),
    )
    grad_proj = jnp.stack(
        [grad_queries.reshape(row_count, local_width), own_keys, own_values]
    ).astype(jnp.bfloat16)
    grad_proj_f = grad_proj.astype(jnp.float32)
    grad_bqv = jnp.stack([jnp.sum(grad_proj_f[0], axis=0), jnp.sum(grad_proj_f[2], axis=0)])
    grad_wqkv = jnp.einsum("cd,jce->jde", normed, grad_proj, preferred_element_type=jnp.float32)
    grad_norm = input_total(
        jnp.einsum("jce,jde->cd", grad_proj, w_qkv, preferred_element_type=jnp.float32)
    )
    _, norm_back_one = jax.vjp(layer_norm, hidden, gain_f[0], shift_f[0])
    grad_input, gain_grad_one, shift_grad_one = norm_back_one(grad_norm)
    layer_grads = (
        grad_wqkv,
        grad_bqv,
        grad_wout,
        grad_bout,
        grad_wup,
        grad_bup,
        grad_wdown,
        grad_bdown,
        jnp.stack([gain_grad_one, gain_grad_two]),
        jnp.stack([shift_grad_one, shift_grad_two]),
    )
    return (grad_mid + grad_input, layer_grads)


def body(
    hidden_in,
    cotangent,
    lengths,
    qkv_weight,
    qv_bias,
    out_weight,
    out_bias,
    up_weight,
    up_bias,
    down_weight,
    down_bias,
    ln_gain,
    ln_bias,
):
    layer_count = qkv_weight.shape[0]
    micro_count = hidden_in.shape[0]
    row_count = hidden_in.shape[1]

    def fetch_layer(layer_idx):
        return (
            lax.all_gather(qkv_weight[layer_idx], ("fsdp", "seq"), axis=1, tiled=True),
            lax.all_gather(out_weight[layer_idx], ("fsdp", "seq"), axis=1, tiled=True),
            lax.all_gather(up_weight[layer_idx], ("fsdp", "seq"), axis=0, tiled=True),
            lax.all_gather(down_weight[layer_idx], ("fsdp", "seq"), axis=1, tiled=True),
            lax.all_gather(out_bias[layer_idx], ("fsdp", "seq"), axis=0, tiled=True),
            lax.all_gather(down_bias[layer_idx], ("fsdp", "seq"), axis=0, tiled=True),
            lax.all_gather(ln_gain[layer_idx], ("fsdp", "seq"), axis=1, tiled=True),
            lax.all_gather(ln_bias[layer_idx], ("fsdp", "seq"), axis=1, tiled=True),
        )

    def local_biases(layer_idx):
        return (qv_bias[layer_idx].astype(jnp.float32), up_bias[layer_idx].astype(jnp.float32))

    positions = lax.axis_index("seq") * row_count + jnp.arange(row_count)
    totals = [None] * layer_count
    outputs = []
    input_grads = []
    for micro_idx in range(micro_count):
        length = lengths[micro_idx]
        hidden = hidden_in[micro_idx].astype(jnp.float32)
        layer_inputs = []
        for layer_idx in range(layer_count):
            layer_inputs.append(hidden)
            hidden, _ = forward_layer(
                hidden, fetch_layer(layer_idx), local_biases(layer_idx), length
            )
        outputs.append(hidden)
        grad_flow = (
            cotangent[micro_idx].astype(jnp.float32)
            * (positions < length).astype(jnp.float32)[:, None]
        )
        for layer_idx in reversed(range(layer_count)):
            grad_flow, layer_grads = backward_layer(
                layer_inputs[layer_idx],
                fetch_layer(layer_idx),
                local_biases(layer_idx),
                length,
                grad_flow,
            )
            if totals[layer_idx] is None:
                totals[layer_idx] = layer_grads
            else:
                totals[layer_idx] = jax.tree.map(jnp.add, totals[layer_idx], layer_grads)
        input_grads.append(grad_flow)
    stacked = [
        jnp.stack([totals[layer_idx][member] for layer_idx in range(layer_count)])
        for member in range(10)
    ]
    (
        grad_wqkv,
        grad_bqv,
        grad_wout,
        grad_bout,
        grad_wup,
        grad_bup,
        grad_wdown,
        grad_bdown,
        grad_gain,
        grad_shift,
    ) = stacked
    shards = (
        lax.psum_scatter(
            grad_wqkv.astype(jnp.bfloat16), ("fsdp", "seq"), scatter_dimension=2, tiled=True
        ).astype(jnp.float32),
        lax.psum_scatter(
            grad_wout.astype(jnp.bfloat16), ("fsdp", "seq"), scatter_dimension=2, tiled=True
        ).astype(jnp.float32),
        lax.psum_scatter(
            grad_wup.astype(jnp.bfloat16), ("fsdp", "seq"), scatter_dimension=1, tiled=True
        ).astype(jnp.float32),
        lax.psum_scatter(
            grad_wdown.astype(jnp.bfloat16), ("fsdp", "seq"), scatter_dimension=2, tiled=True
        ).astype(jnp.float32),
        lax.psum_scatter(
            grad_bout.astype(jnp.bfloat16), ("fsdp", "seq"), scatter_dimension=1, tiled=True
        ).astype(jnp.float32),
        lax.psum_scatter(
            grad_bdown.astype(jnp.bfloat16), ("fsdp", "seq"), scatter_dimension=1, tiled=True
        ).astype(jnp.float32),
        lax.psum_scatter(
            grad_gain.astype(jnp.bfloat16), ("fsdp", "seq"), scatter_dimension=2, tiled=True
        ).astype(jnp.float32),
        lax.psum_scatter(
            grad_shift.astype(jnp.bfloat16), ("fsdp", "seq"), scatter_dimension=2, tiled=True
        ).astype(jnp.float32),
    )
    bias_sums = lax.psum((grad_bqv, grad_bup), ("fsdp", "seq"))
    return (
        jnp.stack(outputs),
        jnp.stack(input_grads),
        shards[0],
        bias_sums[0],
        shards[1],
        shards[4],
        shards[2],
        bias_sums[1],
        shards[3],
        shards[5],
        shards[6],
        shards[7],
    )


def solution(mesh):
    placed = (
        P("fsdp", "seq", None),
        P("fsdp", "seq", None),
        P("fsdp"),
        P(None, None, ("fsdp", "seq"), "tp"),
        P(None, None, "tp"),
        P(None, "tp", ("fsdp", "seq")),
        P(None, ("fsdp", "seq")),
        P(None, ("fsdp", "seq"), "tp"),
        P(None, "tp"),
        P(None, "tp", ("fsdp", "seq")),
        P(None, ("fsdp", "seq")),
        P(None, None, ("fsdp", "seq")),
        P(None, None, ("fsdp", "seq")),
    )
    return jax.shard_map(
        body,
        mesh=mesh,
        in_specs=placed,
        out_specs=(
            P("fsdp", "seq", None),
            P("fsdp", "seq", None),
            P(None, None, ("fsdp", "seq"), "tp"),
            P(None, None, "tp"),
            P(None, "tp", ("fsdp", "seq")),
            P(None, ("fsdp", "seq")),
            P(None, ("fsdp", "seq"), "tp"),
            P(None, "tp"),
            P(None, "tp", ("fsdp", "seq")),
            P(None, ("fsdp", "seq")),
            P(None, None, ("fsdp", "seq")),
            P(None, None, ("fsdp", "seq")),
        ),
        check_vma=False,
    )
```

profile of v0, /device:TPU:0, one launch (start us, length us, event | category | flops | bytes accessed | tf_op | source)
XLA Modules:
  0.0 2356.8 jit_solution(8872836746268542872)
XLA Ops:
  13.4 47.6 %all-gather = bf16[1,2,1280]{1,0,2:T(2,128)(2,1)S(1)} all-gather(bf16[1,2,80]{1,0,2:T(2,128)(2,1)S(1)} %copy.93), channel_id=2, replica_groups=mesh['fsdp'=8,'seq'=2,'tp'=8] {'fsdp','seq'}, dimensions={2}, use_global_device_ids=true | all-gather | bytes 5440 | tf_op jit(solution)/shard_map/all_gather | solution.py:218
  61.9 44.4 %all-gather.1 = bf16[1,2,1280]{1,0,2:T(2,128)(2,1)S(1)} all-gather(bf16[1,2,80]{1,0,2:T(2,128)(2,1)S(1)} %copy.94), channel_id=3, replica_groups=mesh['fsdp'=8,'seq'=2,'tp'=8] {'fsdp','seq'}, dimensions={2}, use_global_device_ids=true | all-gather | bytes 5440 | tf_op jit(solution)/shard_map/all_gather | solution.py:219
  108.4 44.5 %all-gather.4 = bf16[1,160,1280]{1,0,2:T(2,128)(2,1)} all-gather(bf16[1,160,80]{1,0,2:T(2,128)(2,1)S(1)} %copy.96), channel_id=6, replica_groups=mesh['fsdp'=8,'seq'=2,'tp'=8] {'fsdp','seq'}, dimensions={2}, use_global_device_ids=true | all-gather | bytes 435200 | tf_op jit(solution)/shard_map/all_gather | solution.py:213
  160.0 21.0 slice_reduce_fusion.5
  181.0 21.7 slice_reduce_fusion.4
  238.0 71.4 %all-reduce.6 = (bf16[1280]{0:T(1024)(128)(2,1)S(1)}, bf16[1280]{0:T(1024)(128)(2,1)S(1)}, bf16[1280]{0:T(1024)(128)(2,1)}, bf16[1280]{0:T(1024)(128)(2,1)}) all-reduce(bf16[1280]{0:T(1024)(128)(2,1)S(1)} %dynamic-update-slice, bf16[1280]{0:T(1024)(128)(2,1)S(1)} %dynamic-update-slice.1, ...), channel_id=7, replica_groups=mesh['fsdp'=8,'seq'=2,'tp'=8] {'fsdp','seq'}, use_global_device_ids=true, to_apply=%add | all-reduce | flops 5120 | bytes 20480
  310.2 41.8 %all-gather.9 = bf16[1,2,1280]{1,0,2:T(2,128)(2,1)S(1)} all-gather(bf16[1,2,80]{1,0,2:T(2,128)(2,1)S(1)} %copy.97), channel_id=11, replica_groups=mesh['fsdp'=8,'seq'=2,'tp'=8] {'fsdp','seq'}, dimensions={2}, use_global_device_ids=true | all-gather | bytes 5440 | tf_op jit(solution)/shard_map/all_gather | solution.py:218
  352.9 41.5 %all-gather.10 = bf16[1,2,1280]{1,0,2:T(2,128)(2,1)S(1)} all-gather(bf16[1,2,80]{1,0,2:T(2,128)(2,1)S(1)} %copy.98), channel_id=12, replica_groups=mesh['fsdp'=8,'seq'=2,'tp'=8] {'fsdp','seq'}, dimensions={2}, use_global_device_ids=true | all-gather | bytes 5440 | tf_op jit(solution)/shard_map/all_gather | solution.py:219
  396.1 51.3 %all-gather.13 = bf16[1,160,1280]{1,0,2:T(2,128)(2,1)} all-gather(bf16[1,160,80]{1,0,2:T(2,128)(2,1)S(1)} %copy.100), channel_id=15, replica_groups=mesh['fsdp'=8,'seq'=2,'tp'=8] {'fsdp','seq'}, dimensions={2}, use_global_device_ids=true | all-gather | bytes 435200 | tf_op jit(solution)/shard_map/all_gather | solution.py:213
  479.6 22.0 slice_reduce_fusion
  501.6 25.9 %all-gather.35.cloned.1.call-done = bf16[1,3,1280,160]{3,1,0,2:T(4,128)(2,1)} async-done(((bf16[1,3,80,160]{3,1,0,2:T(4,128)(2,1)}), bf16[1,3,1280,160]{3,1,0,2:T(4,128)(2,1)}) %all-gather.35.cloned.1.call-update) | async-done | bytes 1228816 | tf_op jit(solution)/shard_map/all_gather | solution.py:212
  531.4 59.9 %all-reduce.29.cloned.1.call-done = bf16[128,1280]{1,0:T(8,128)(2,1)} async-done(((bf16[128,1280]{1,0:T(8,128)(2,1)}), bf16[128,1280]{1,0:T(8,128)(2,1)}) %all-reduce.29.cloned.1.call-update) | async-done | bytes 327696 | tf_op jit(solution)/shard_map/psum | solution.py:24
  627.7 39.7 %all-reduce.31.cloned.1.call-done = bf16[128,1280]{1,0:T(8,128)(2,1)} async-done(((bf16[128,1280]{1,0:T(8,128)(2,1)}), bf16[128,1280]{1,0:T(8,128)(2,1)}) %all-reduce.31.cloned.1.call-update) | async-done | bytes 327696 | tf_op jit(solution)/shard_map/psum | solution.py:24
  670.5 73.6 %all-gather.37.cloned.1.call-done = bf16[1,1280,640]{2,1,0:T(8,128)(2,1)} async-done(((bf16[1,80,640]{2,1,0:T(8,128)(2,1)}), bf16[1,1280,640]{2,1,0:T(8,128)(2,1)}) %all-gather.37.cloned.1.call-update) | async-done | bytes 1638416 | tf_op jit(solution)/shard_map/all_gather | solution.py:214
  746.8 74.9 %all-gather.39.cloned.1.call-done = bf16[1,640,1280]{1,2,0:T(8,128)(2,1)} async-done(((bf16[1,640,80]{1,2,0:T(8,128)(2,1)}), bf16[1,640,1280]{1,2,0:T(8,128)(2,1)}) %all-gather.39.cloned.1.call-update) | async-done | bytes 1638416 | tf_op jit(solution)/shard_map/all_gather | solution.py:215
  829.5 58.0 %all-reduce.33.cloned.1.call-done = bf16[128,1280]{1,0:T(8,128)(2,1)} async-done(((bf16[128,1280]{1,0:T(8,128)(2,1)}), bf16[128,1280]{1,0:T(8,128)(2,1)}) %all-reduce.33.cloned.1.call-update) | async-done | bytes 327696 | tf_op jit(solution)/shard_map/psum | solution.py:28
  928.1 60.2 %all-reduce.35.cloned.1.call-done = bf16[128,1280]{1,0:T(8,128)(2,1)} async-done(((bf16[128,1280]{1,0:T(8,128)(2,1)}), bf16[128,1280]{1,0:T(8,128)(2,1)}) %all-reduce.35.cloned.1.call-update) | async-done | bytes 327696 | tf_op jit(solution)/shard_map/psum | solution.py:28
  998.8 59.3 %all-reduce.51.cloned.1.call-done = (bf16[128,1280]{1,0:T(8,128)(2,1)}, bf16[128,1280]{1,0:T(8,128)(2,1)}) async-done(((bf16[128,1280]{1,0:T(8,128)(2,1)}, bf16[128,1280]{1,0:T(8,128)(2,1)}), (bf16[128,1280]{1,0:T(8,128)(2,1)}, bf16[128,1280]{1,0:T(8,128)(2,1)})) %all-reduce.51.cloned.1.call-update) | async-done | bytes 655376 | tf_op jit(solution)/shard_map/psum | solution.py:28
  1071.1 57.1 %all-reduce.49.cloned.1.call-done = (bf16[128,1280]{1,0:T(8,128)(2,1)}, bf16[128,1280]{1,0:T(8,128)(2,1)}) async-done(((bf16[128,1280]{1,0:T(8,128)(2,1)}, bf16[128,1280]{1,0:T(8,128)(2,1)}), (bf16[128,1280]{1,0:T(8,128)(2,1)}, bf16[128,1280]{1,0:T(8,128)(2,1)})) %all-reduce.49.cloned.1.call-update) | async-done | bytes 655376 | tf_op jit(solution)/shard_map/psum | solution.py:24
  1169.3 56.0 %all-reduce.47.cloned.1.call-done = (bf16[128,1280]{1,0:T(8,128)(2,1)}, bf16[128,1280]{1,0:T(8,128)(2,1)}) async-done(((bf16[128,1280]{1,0:T(8,128)(2,1)}, bf16[128,1280]{1,0:T(8,128)(2,1)}), (bf16[128,1280]{1,0:T(8,128)(2,1)}, bf16[128,1280]{1,0:T(8,128)(2,1)})) %all-reduce.47.cloned.1.call-update) | async-done | bytes 655376 | tf_op jit(solution)/shard_map/psum | solution.py:24
  1245.2 55.2 %all-reduce.45.cloned.1.call-done = (bf16[128,1280]{1,0:T(8,128)(2,1)}, bf16[128,1280]{1,0:T(8,128)(2,1)}) async-done(((bf16[128,1280]{1,0:T(8,128)(2,1)}, bf16[128,1280]{1,0:T(8,128)(2,1)}), (bf16[128,1280]{1,0:T(8,128)(2,1)}, bf16[128,1280]{1,0:T(8,128)(2,1)})) %all-reduce.45.cloned.1.call-update) | async-done | bytes 655376 | tf_op jit(solution)/shard_map/psum | solution.py:28
  1382.9 58.9 %all-reduce.43.cloned.1.call-done = (bf16[128,1280]{1,0:T(8,128)(2,1)}, bf16[128,1280]{1,0:T(8,128)(2,1)}) async-done(((bf16[128,1280]{1,0:T(8,128)(2,1)}, bf16[128,1280]{1,0:T(8,128)(2,1)}), (bf16[128,1280]{1,0:T(8,128)(2,1)}, bf16[128,1280]{1,0:T(8,128)(2,1)})) %all-reduce.43.cloned.1.call-update) | async-done | bytes 655376 | tf_op jit(solution)/shard_map/psum | solution.py:28
  1458.0 55.8 %all-reduce.41.cloned.1.call-done = (bf16[128,1280]{1,0:T(8,128)(2,1)}, bf16[128,1280]{1,0:T(8,128)(2,1)}) async-done(((bf16[128,1280]{1,0:T(8,128)(2,1)}, bf16[128,1280]{1,0:T(8,128)(2,1)}), (bf16[128,1280]{1,0:T(8,128)(2,1)}, bf16[128,1280]{1,0:T(8,128)(2,1)})) %all-reduce.41.cloned.1.call-update) | async-done | bytes 655376 | tf_op jit(solution)/shard_map/psum | solution.py:28
  1639.3 58.0 %all-reduce.39.cloned.1.call-done = (bf16[128,1280]{1,0:T(8,128)(2,1)}, bf16[128,1280]{1,0:T(8,128)(2,1)}, bf16[128,1280]{1,0:T(8,128)(2,1)}, bf16[128,1280]{1,0...) async-done(((bf16[128,1280]{1,0:T(8,128)(2,1)}, bf16[128,1280]{1,0:T(8,128)(2,1)}, bf16[128,1280]{1,0:T(8,128)(2,1)}, bf16[128,1280]{1,0:T(8,128)(2,1)}, ...) | async-done | bytes 1966096 | tf_op jit(solution)/shard_map/psum | solution.py:24
  1781.8 71.0 %reduce-scatter.86.cloned.1.call-done = bf16[80,2]{1,0:T(8,128)(2,1)} async-done(((bf16[1280,2]{1,0:T(8,128)(2,1)}), bf16[80,2]{1,0:T(8,128)(2,1)}) %reduce-scatter.86.cloned.1.call-update) | async-done | bytes 336
  1856.3 38.5 %all-reduce.5 = (f32[2,2,160]{2,1,0:T(2,128)}, f32[2,640]{1,0:T(2,128)}) all-reduce(f32[2,2,160]{2,1,0:T(2,128)S(1)} %pad_maximum_fusion.17, f32[2,640]{1,0:T(2,128)S(1)} %pad_maximum_fusion.15), channel_id=1, replica_groups=mesh['fsdp'=8,'seq'=2,'tp'=8] {'fsdp','seq'}, use_global_device_ids=true, to_apply=%region_115.116 | all-reduce | flops 1920 | bytes 15360 | tf_op jit(solution)/shard_map/psum | solution.py:298
  1902.8 26.5 %reduce-scatter.92.cloned.1.call-done = bf16[80,4]{1,0:T(8,128)(2,1)} async-done(((bf16[1280,4]{1,0:T(8,128)(2,1)}), bf16[80,4]{1,0:T(8,128)(2,1)}) %reduce-scatter.92.cloned.1.call-update) | async-done | bytes 656
  1930.8 74.6 %reduce-scatter.90.cloned.1.call-done = bf16[80,4]{1,0:T(8,128)(2,1)} async-done(((bf16[1280,4]{1,0:T(8,128)(2,1)}), bf16[80,4]{1,0:T(8,128)(2,1)}) %reduce-scatter.90.cloned.1.call-update) | async-done | bytes 656
  2006.9 76.3 %reduce-scatter.84.cloned.1.call-done = bf16[80,320]{1,0:T(8,128)(2,1)} async-done(((bf16[1280,320]{1,0:T(8,128)(2,1)}), bf16[80,320]{1,0:T(8,128)(2,1)}) %reduce-scatter.84.cloned.1.call-update) | async-done | bytes 51216
  2085.0 95.2 %all-reduce.37.cloned.1.call-done = bf16[2,640,1280]{1,0,2:T(2,128)(2,1)} async-done(((bf16[2,640,1280]{1,0,2:T(2,128)(2,1)}), bf16[2,640,1280]{1,0,2:T(2,128)(2,1)}) %all-reduce.37.cloned.1.call-update) | async-done | bytes 3276816
  2182.1 81.3 %reduce-scatter.82.cloned.1.call-done = bf16[80,960]{1,0:T(8,128)(2,1)} async-done(((bf16[1280,960]{1,0:T(8,128)(2,1)}), bf16[80,960]{1,0:T(8,128)(2,1)}) %reduce-scatter.82.cloned.1.call-update) | async-done | bytes 153616
  2265.8 82.2 %reduce-scatter.56.cloned.1.call-done = bf16[2,80,640]{2,1,0:T(8,128)(2,1)} async-done(((bf16[2,1280,640]{2,1,0:T(8,128)(2,1)}), bf16[2,80,640]{2,1,0:T(8,128)(2,1)}) %reduce-scatter.56.cloned.1.call-update) | async-done | bytes 204816 | tf_op jit(solution)/shard_map/reduce_scatter | solution.py:279
  (1265 shorter events, 590.5 us)
Async XLA Ops:
  7.2 195.5 %all-gather.29.cloned.1.call-start = ((), (), s32[]{:S(2)}) async-start(), calls=%async_computation.24 | async-start | bytes 2785280 | tf_op jit(solution)/shard_map/all_gather | solution.py:212
  9.0 462.7 %all-reduce.53.cloned.1.call-start = ((), (), s32[]{:S(2)}) async-start(), calls=%async_computation.56 | async-start | bytes 1310720 | tf_op jit(solution)/shard_map/psum | solution.py:24
  233.4 240.7 %all-gather.31.cloned.1.call-start = ((), (), s32[]{:S(2)}) async-start(), calls=%async_computation.25 | async-start | bytes 1740800 | tf_op jit(solution)/shard_map/all_gather | solution.py:214
  234.1 241.9 %all-gather.33.cloned.1.call-start = ((), (), s32[]{:S(2)}) async-start(), calls=%async_computation.26 | async-start | bytes 1740800 | tf_op jit(solution)/shard_map/all_gather | solution.py:215
  234.9 292.5 %all-gather.35.cloned.1.call-start = ((), (), s32[]{:S(2)}) async-start(), calls=%async_computation.27 | async-start | bytes 2785280 | tf_op jit(solution)/shard_map/all_gather | solution.py:212
  235.7 355.5 %all-reduce.29.cloned.1.call-start = ((), (), s32[]{:S(2)}) async-start(), calls=%async_computation.19 | async-start | bytes 655360 | tf_op jit(solution)/shard_map/psum | solution.py:24
  479.5 187.9 %all-reduce.31.cloned.1.call-start = ((), (), s32[]{:S(2)}) async-start(), calls=%async_computation.20 | async-start | bytes 655360 | tf_op jit(solution)/shard_map/psum | solution.py:24
  608.2 135.9 %all-gather.37.cloned.1.call-start = ((), (), s32[]{:S(2)}) async-start(), calls=%async_computation.28 | async-start | bytes 1740800 | tf_op jit(solution)/shard_map/all_gather | solution.py:214
  609.0 212.7 %all-gather.39.cloned.1.call-start = ((), (), s32[]{:S(2)}) async-start(), calls=%async_computation.29 | async-start | bytes 1740800 | tf_op jit(solution)/shard_map/all_gather | solution.py:215
  609.7 277.7 %all-reduce.33.cloned.1.call-start = ((), (), s32[]{:S(2)}) async-start(), calls=%async_computation.21 | async-start | bytes 655360 | tf_op jit(solution)/shard_map/psum | solution.py:28
  827.1 80.5 %reduce-scatter.66.cloned.1.call-start = ((), (), s32[]{:S(2)}) async-start(), calls=%async_computation.34 | async-start | bytes 196608
  898.6 89.8 %all-reduce.35.cloned.1.call-start = ((), (), s32[]{:S(2)}) async-start(), calls=%async_computation.22 | async-start | bytes 655360 | tf_op jit(solution)/shard_map/psum | solution.py:28
  926.3 131.9 %all-reduce.51.cloned.1.call-start = ((), (), s32[]{:S(2)}) async-start(), calls=%async_computation.55 | async-start | bytes 1310720 | tf_op jit(solution)/shard_map/psum | solution.py:28
  997.5 130.8 %all-reduce.49.cloned.1.call-start = ((), (), s32[]{:S(2)}) async-start(), calls=%async_computation.54 | async-start | bytes 1310720 | tf_op jit(solution)/shard_map/psum | solution.py:24
  1067.5 157.8 %all-reduce.47.cloned.1.call-start = ((), (), s32[]{:S(2)}) async-start(), calls=%async_computation.53 | async-start | bytes 1310720 | tf_op jit(solution)/shard_map/psum | solution.py:24
  1165.1 135.3 %all-reduce.45.cloned.1.call-start = ((), (), s32[]{:S(2)}) async-start(), calls=%async_computation.52 | async-start | bytes 1310720 | tf_op jit(solution)/shard_map/psum | solution.py:28
  1239.6 90.7 %reduce-scatter.74.cloned.1.call-start = ((), (), s32[]{:S(2)}) async-start(), calls=%async_computation.38 | async-start | bytes 196608
  1328.4 47.4 %reduce-scatter.60.cloned.1.call-start = ((), (), s32[]{:S(2)}) async-start(), calls=%async_computation.31 | async-start | bytes 196608
  1330.2 111.6 %all-reduce.43.cloned.1.call-start = ((), (), s32[]{:S(2)}) async-start(), calls=%async_computation.51 | async-start | bytes 1310720 | tf_op jit(solution)/shard_map/psum | solution.py:28
  1379.3 134.5 %all-reduce.41.cloned.1.call-start = ((), (), s32[]{:S(2)}) async-start(), calls=%async_computation.50 | async-start | bytes 1310720 | tf_op jit(solution)/shard_map/psum | solution.py:28
  1453.0 103.5 %reduce-scatter.70.cloned.1.call-start = ((), (), s32[]{:S(2)}) async-start(), calls=%async_computation.36 | async-start | bytes 196608
  1554.2 56.2 %reduce-scatter.78.cloned.1.call-start = ((), (), s32[]{:S(2)}) async-start(), calls=%async_computation.40 | async-start | bytes 196608
  1555.3 71.7 %reduce-scatter.80.cloned.1.call-start = ((), (), s32[]{:S(2)}) async-start(), calls=%async_computation.41 | async-start | bytes 196608
  1556.5 140.8 %all-reduce.39.cloned.1.call-start = ((), (), s32[]{:S(2)}) async-start(), calls=%async_computation.49 | async-start | bytes 3932160 | tf_op jit(solution)/shard_map/psum | solution.py:24
  1630.6 149.7 %reduce-scatter.88.cloned.1.call-start = ((), (), s32[]{:S(2)}) async-start(), calls=%async_computation.45 | async-start | bytes 348160
  1634.8 217.9 %reduce-scatter.86.cloned.1.call-start = ((), (), s32[]{:S(2)}) async-start(), calls=%async_computation.44 | async-start | bytes 348160
  1639.1 290.2 %reduce-scatter.92.cloned.1.call-start = ((), (), s32[]{:S(2)}) async-start(), calls=%async_computation.47 | async-start | bytes 348160
  1704.5 300.9 %reduce-scatter.90.cloned.1.call-start = ((), (), s32[]{:S(2)}) async-start(), calls=%async_computation.46 | async-start | bytes 348160
  1708.0 375.2 %reduce-scatter.84.cloned.1.call-start = ((), (), s32[]{:S(2)}) async-start(), calls=%async_computation.43 | async-start | bytes 1044480
  1718.4 461.8 %all-reduce.37.cloned.1.call-start = ((), (), s32[]{:S(2)}) async-start(), calls=%async_computation.48 | async-start | bytes 6553600
  1738.4 525.1 %reduce-scatter.82.cloned.1.call-start = ((), (), s32[]{:S(2)}) async-start(), calls=%async_computation.42 | async-start | bytes 2785280
  1766.8 581.2 %reduce-scatter.56.cloned.1.call-start = ((), (), s32[]{:S(2)}) async-start(), calls=%async_computation.23 | async-start | bytes 3481600 | tf_op jit(solution)/shard_map/reduce_scatter | solution.py:279
  (392 other events, 5866.8 us)
Sparse Core Ops, SparseCore 0:
  10.2 91.5 all-gather.28
  233.5 59.5 all-reduce.52
  294.8 76.6 all-gather.30
  372.9 75.0 all-gather.32
  450.1 77.2 all-gather.34
  530.2 61.0 all-reduce.28
  608.3 59.0 all-reduce.30
  669.1 74.9 all-gather.36
  745.8 75.8 all-gather.38
  827.2 60.1 all-reduce.32
  927.2 61.1 all-reduce.34
  997.6 60.4 all-reduce.50
  1067.6 60.6 all-reduce.48
  1165.2 60.0 all-reduce.46
  1239.7 60.6 all-reduce.44
  1329.4 13.7 reduce-scatter.75
  1345.3 13.7 reduce-scatter.57
  1362.0 13.7 reduce-scatter.59
  1379.4 62.3 all-reduce.42
  1453.1 60.6 all-reduce.40
  1579.9 13.7 reduce-scatter.63
  1596.6 13.7 reduce-scatter.77
  1613.3 13.7 reduce-scatter.79
  1630.7 66.5 all-reduce.38
  1699.8 76.6 reduce-scatter.87
  1778.8 73.8 reduce-scatter.85
  1855.1 74.1 reduce-scatter.91
  1931.7 73.7 reduce-scatter.89
  2007.9 75.2 reduce-scatter.83
  2086.5 93.6 all-reduce.36
  2182.6 80.7 reduce-scatter.81
  2266.0 82.0 reduce-scatter.55
  (6 shorter events, 75.0 us)
where the time goes:
time: 2370 us; the launch traced here: 2360 us
  waiting for transfers between devices  1430 us (60%)
  blocking collectives  439 us (19%)
  local copies, waits for them, and re-layouts  222 us (9%)
  matrix products  153 us (6%)
  other arithmetic  92.5 us (4%)
    unnamed x57, waiting for transfers between devices  551 us
    psum x6, waiting for transfers between devices, input_total(): return lax.psum(partial_sum.astype(jnp.bfloat16), 'tp').astype(jnp.float32)  347 us
    psum x6, waiting for transfers between devices, branch_total(): return lax.psum(partial_sum.astype(jnp.bfloat16), 'tp').astype(jnp.float32)  271 us
    unnamed x837, local copies, waits for them, and re-layouts  100 us
    all_gather x2, blocking collectives, fetch_layer(): lax.all_gather(out_weight[layer_idx], ('fsdp', 'seq'), axis=1, tiled=True)  95.8 us
    all_gather x2, blocking collectives, fetch_layer(): lax.all_gather(ln_gain[layer_idx], ('fsdp', 'seq'), axis=1, tiled=True)  89.5 us
    all_gather x2, blocking collectives, fetch_layer(): lax.all_gather(ln_bias[layer_idx], ('fsdp', 'seq'), axis=1, tiled=True)  85.9 us
    reduce_scatter x1, waiting for transfers between devices, body(): lax.psum_scatter(grad_wup.astype(jnp.bfloat16), ('fsdp', 'seq'), scatter_...  82.2 us
  transfers between devices with their start and end apart: 38, of which 31 were waited for; matrix products, arithmetic and copies ran while one was open for 14% of the time, Pallas kernels for 0%

commit v1 on v0

v1 whole, which is shorter than its diff:
```python
from functools import partial
import math

import jax
import jax.numpy as jnp
from jax import lax
from jax.experimental import pallas as pl
from jax.experimental.pallas import tpu as pltpu
from jax.sharding import PartitionSpec as P

HD = 80
EPSILON = 1e-05
MASKED = -1000000000.0
MESH = pl.DeviceIdType.MESH
BF = jnp.bfloat16
F32 = jnp.float32
SCALING = 1.0 / math.sqrt(HD)

D = 1280
MICRO = 3
ROWS = 128
PART = 640
SHARDS = 16
SHARD = 80
WIDTH = 160


def dot_nn(a, b):
    return lax.dot_general(a, b, (((1,), (0,)), ((), ())), preferred_element_type=F32)


def dot_nt(a, b):
    return lax.dot_general(a, b, (((1,), (1,)), ((), ())), preferred_element_type=F32)


def dot_tn(a, b):
    return lax.dot_general(a, b, (((0,), (0,)), ((), ())), preferred_element_type=F32)


def norm_parts(values):
    row_mean = jnp.mean(values, axis=-1, keepdims=True)
    centred = values - row_mean
    row_var = jnp.mean(centred * centred, axis=-1, keepdims=True)
    inv = lax.rsqrt(row_var + EPSILON)
    return centred * inv, inv


def norm_back(grad, gain, unit, inv):
    scaled = grad * gain
    return inv * (
        scaled
        - jnp.mean(scaled, axis=-1, keepdims=True)
        - unit * jnp.mean(scaled * unit, axis=-1, keepdims=True)
    )


def split_heads(x):
    first = lax.broadcasted_iota(jnp.int32, x.shape, 1) < HD
    return jnp.concatenate([jnp.where(first, x, 0.0), jnp.where(first, 0.0, x)], axis=0)


def kernel(
    hid_ref, cot_ref, wown_ref, vec_ref, bqkv_ref, bup_ref, live_ref,
    out_ref, ingrad_ref, dwo_ref, vout_ref, bout_ref,
    W, dW, rsb, FB, BB, dr, yr, part, sb,
    qkv, kvo, prob, att, xrow, midrow, slope, act,
    gpre, gkeep, gproj, gks, gkr, gyrow, gmidrow,
    VG, V, GV, GT, vr, vr2, gb, br,
    gss, grs, rss, rrs, s1, r1, s2, r2, s3, r3, s4, r4, ks, kr, gs_s, gs_r, vs, vrs, es, er, lsem,
):
    f, s, t = lax.axis_index("fsdp"), lax.axis_index("seq"), lax.axis_index("tp")
    me = f * 2 + s
    y, core = t // 2, t % 2
    other = 1 - core

    def shard_dev(k):
        j = (me + k) % SHARDS
        return j, (j // 2, j % 2, t)

    def y_dev(k):
        j = (y + k) % 4
        return j, (f, s, j * 2 + core)

    core_dev = (f, s, y * 2 + other)
    seq_dev = (f, 1 - s, t)

    def remote(src, dst, ss, rs, dev):
        return pltpu.make_async_remote_copy(
            src_ref=src, dst_ref=dst, send_sem=ss, recv_sem=rs, device_id=dev, device_id_type=MESH
        )

    def wait_bytes(ref, sem):
        pltpu.make_async_copy(ref, ref, sem).wait()

    cp_h = pltpu.make_async_copy(hid_ref, FB.at[0], lsem.at[0])
    cp_c = pltpu.make_async_copy(cot_ref, BB.at[0], lsem.at[1])
    cp_h.start()
    cp_c.start()

    barrier = pltpu.get_barrier_semaphore()

    @pl.loop(1, SHARDS)
    def _(k):
        pl.semaphore_signal(barrier, inc=1, device_id=shard_dev(k)[1], device_id_type=MESH)

    @pl.loop(1, 8)
    def _(k):
        pl.semaphore_signal(barrier, inc=1, device_id=(f, s, (t + k) % 8), device_id_type=MESH)

    pl.semaphore_wait(barrier, 22)

    @pl.loop(1, SHARDS)
    def _(k):
        remote(vec_ref, VG.at[me], vs.at[0], vrs.at[0], shard_dev(k)[1]).start()

    VG[me] = vec_ref[...]

    def gather_start(l, p):
        @pl.loop(1, SHARDS)
        def _(k):
            remote(wown_ref.at[l, p], W.at[l, p, me], gss.at[l, p], grs.at[l, p], shard_dev(k)[1]).start()

        W[l, p, me] = wown_ref[l, p]

    def gather_wait(l, p):
        wait_bytes(W.at[l, p, pl.ds(0, SHARDS - 1)], grs.at[l, p])
        wait_bytes(W.at[l, p, pl.ds(0, SHARDS - 1)], gss.at[l, p])

    gather_start(0, 0)
    wait_bytes(VG.at[pl.ds(0, SHARDS - 1)], vrs.at[0])
    wait_bytes(VG.at[pl.ds(0, SHARDS - 1)], vs.at[0])
    V[...] = jnp.zeros_like(V)
    for i in range(SHARDS):
        low = SHARD * i // 128 * 128
        piece = VG[i].astype(F32)
        V[0, :, low : low + 256] += piece[0:8]
        V[1, :, low : low + 256] += piece[8:16]
    GV[...] = jnp.zeros_like(GV)
    gb[...] = jnp.zeros_like(gb)

    def vec(l, r):
        return V[l, r : r + 1, 0:D]

    cp_h.wait()
    cp_c.wait()
    for c in range(MICRO):
        whole = FB[0, c].reshape(ROWS, D).astype(F32)
        unit, _ = norm_parts(whole)
        xrow[0, c] = FB[0, c, y, core].astype(F32)
        FB[0, c] = (unit * vec(0, 0) + vec(0, 2)).astype(BF).reshape(4, 2, 16, D)
        gyrow[c] = BB[0, c, y, core].astype(F32)

    def rs_start(a, c, value):
        part[c] = value.astype(BF).reshape(4, 2, 16, D)
        remote(part.at[c, :, other], dr.at[a, c], s1.at[c], r1.at[a, c], core_dev).start()

    def rs_mid(a, c):
        wait_bytes(dr.at[a, c], r1.at[a, c])
        wait_bytes(dr.at[a, c], s1.at[c])
        sb[c] = (part[c, :, core].astype(F32) + dr[a, c].astype(F32)).astype(BF)
        for k in range(1, 4):
            j, dev = y_dev(k)
            remote(sb.at[c, j], yr.at[a, c, k - 1], s2.at[c], r2.at[a, c], dev).start()

    def rs_end(a, c):
        wait_bytes(yr.at[a, c], r2.at[a, c])
        wait_bytes(yr.at[a, c], s2.at[c])
        total = sb[c, y].astype(F32)
        for k in range(3):
            total = total + yr[a, c, k].astype(F32)
        return total

    def ag_start(buf, i, a, c, value):
        buf[i, c, y, core] = value.astype(BF)
        for k in range(1, 4):
            _, dev = y_dev(k)
            remote(buf.at[i, c, y, core], buf.at[i, c, y, core], s3.at[c], r3.at[a, c], dev).start()

    def ag_mid(buf, i, a, c):
        wait_bytes(yr.at[a, c], r3.at[a, c])
        wait_bytes(yr.at[a, c], s3.at[c])
        remote(buf.at[i, c, :, core], buf.at[i, c, :, core], s4.at[c], r4.at[a, c], core_dev).start()

    def ag_end(buf, i, a, c):
        wait_bytes(dr.at[a, c], r4.at[a, c])
        wait_bytes(dr.at[a, c], s4.at[c])

    def heads_of(l, c):
        own = qkv[l, c].astype(F32)
        far = kvo[l, c].astype(F32)
        q = own[:, 0:160]
        k = jnp.concatenate([own[:, 160:320], far[:, 32:192]], axis=0)
        v = jnp.concatenate([own[:, 320:480], far[:, 192:352]], axis=0)
        return split_heads(q).astype(BF), k, v

    def forward(l, carry):
        a0, a1 = 2 * l, 2 * l + 1

        @pl.when(l > 0)
        def _():
            gather_start(l, 0)

        gather_wait(l, 0)
        gather_start(l, 1)
        for c in range(MICRO):
            normed = FB[2 * l, c].reshape(ROWS, D)
            proj = dot_nn(normed, W[l, 0, :, :, 0:512].reshape(D, 512)) + bqkv_ref[l]
            qkv[l, c] = proj.astype(BF)
            remote(qkv.at[l, c, :, 128:512], kvo.at[l, c], ks.at[l, c], kr.at[l, c], seq_dev).start()
        for c in range(MICRO):
            wait_bytes(kvo.at[l, c], kr.at[l, c])
            wait_bytes(kvo.at[l, c], ks.at[l, c])
            q2, k, v = heads_of(l, c)
            scores = dot_nt(q2, k.astype(BF)) * SCALING
            scores = jnp.where(live_ref[c] > 0.0, scores, MASKED)
            top = jnp.max(scores, axis=-1, keepdims=True)
            powers = jnp.exp(scores - top)
            probs = powers / jnp.sum(powers, axis=-1, keepdims=True)
            prob[l, c] = probs
            low = probs.astype(BF)
            attended = dot_nn(
                jnp.concatenate([low[0:ROWS], low[ROWS:]], axis=1), split_heads(v).astype(BF)
            )
            wide = jnp.concatenate([jnp.zeros((ROWS, 96), F32), attended], axis=1).astype(BF)
            att[l, c] = wide
            rs_start(a0, c, dot_nt(wide, W[l, 0, :, :, 384:640].reshape(D, 256)))
        gather_wait(l, 1)
        gather_start(l, 2)
        for c in range(MICRO):
            rs_mid(a0, c)
        for c in range(MICRO):
            middle = xrow[l, c] + rs_end(a0, c) + vec(l, 4)
            midrow[l, c] = middle
            unit, _ = norm_parts(middle)
            ag_start(FB, 2 * l + 1, a0, c, unit * vec(l, 1) + vec(l, 3))
        for c in range(MICRO):
            ag_mid(FB, 2 * l + 1, a0, c)
        gather_wait(l, 2)
        for c in range(MICRO):
            ag_end(FB, 2 * l + 1, a0, c)
            normed = FB[2 * l + 1, c].reshape(ROWS, D)
            pre = dot_nn(normed, W[l, 1].reshape(D, PART)) + bup_ref[l]
            cdf = 0.5 * (1.0 + lax.erf(pre * math.sqrt(0.5)))
            activated = (pre * cdf).astype(BF)
            act[l, c] = activated
            slope[l, c] = cdf + pre * jnp.exp(-0.5 * pre * pre) * (1.0 / math.sqrt(2.0 * math.pi))
            rs_start(a1, c, dot_nt(activated, W[l, 2].reshape(D, PART)))
        for c in range(MICRO):
            rs_mid(a1, c)
        following = lax.rem(l + 1, 2)
        for c in range(MICRO):
            hidden = midrow[l, c] + rs_end(a1, c) + vec(l, 5)
            xrow[l + 1, c] = hidden
            unit, _ = norm_parts(hidden)
            normed = unit * vec(following, 0) + vec(following, 2)
            ag_start(FB, 2 * l + 2, a1, c, jnp.where(l == 1, hidden, normed))
        for c in range(MICRO):
            ag_mid(FB, 2 * l + 2, a1, c)
        for c in range(MICRO):
            ag_end(FB, 2 * l + 2, a1, c)
        return carry

    lax.fori_loop(0, 2, forward, 0)
    cp_o = pltpu.make_async_copy(FB.at[4], out_ref, lsem.at[0])
    cp_o.start()

    def send_part(l, p):
        @pl.loop(1, SHARDS)
        def _(k):
            j, dev = shard_dev(k)
            remote(dW.at[l, p, j], rsb.at[l, p, k - 1], rss.at[l, p], rrs.at[l, p], dev).start()

    def weight_grad(l, p, buf, i, right):
        @pl.loop(0, 2)
        def _(m):
            left = buf[i, :, :, :, :, pl.ds(pl.multiple_of(m * 640, 128), 640)].reshape(MICRO * ROWS, 640)
            dW[l, p, pl.ds(m * 8, 8)] = dot_tn(left, right).astype(BF).reshape(8, SHARD, PART)

        send_part(l, p)

    def backward(j, carry):
        l = 1 - j
        a0, a1 = 4 + 2 * j, 5 + 2 * j
        b0, b1, b2 = 2 * j, 2 * j + 1, 2 * j + 2
        for c in range(MICRO):
            grad_act = dot_nn(BB[b0, c].reshape(ROWS, D), W[l, 2].reshape(D, PART))
            grad_pre = (grad_act * slope[l, c]).astype(BF)
            gpre[c] = grad_pre
            gb[pl.ds(2 + l, 1), :] += jnp.sum(grad_pre.astype(F32), axis=0, keepdims=True)
            rs_start(a0, c, dot_nt(grad_pre, W[l, 1].reshape(D, PART)))
        weight_grad(l, 2, BB, b0, act[l].reshape(MICRO * ROWS, PART))
        for c in range(MICRO):
            rs_mid(a0, c)
        for c in range(MICRO):
            grad_norm = rs_end(a0, c)
            unit, inv = norm_parts(midrow[l, c])
            gy = gyrow[c]
            grad_mid = gy + norm_back(grad_norm, vec(l, 1), unit, inv)
            gmidrow[c] = grad_mid
            GV[l, 1:2, 0:D] += jnp.sum(grad_norm * unit, axis=0, keepdims=True)
            GV[l, 3:4, 0:D] += jnp.sum(grad_norm, axis=0, keepdims=True)
            GV[l, 4:5, 0:D] += jnp.sum(grad_mid, axis=0, keepdims=True)
            GV[l, 5:6, 0:D] += jnp.sum(gy, axis=0, keepdims=True)
            ag_start(BB, b1, a0, c, grad_mid)
        weight_grad(l, 1, FB, 2 * l + 1, gpre[...].reshape(MICRO * ROWS, PART))
        for c in range(MICRO):
            ag_mid(BB, b1, a0, c)
        for c in range(MICRO):
            ag_end(BB, b1, a0, c)
            wide = dot_nn(BB[b1, c].reshape(ROWS, D), W[l, 0, :, :, 384:640].reshape(D, 256))
            ga2 = split_heads(wide[:, 96:256]).astype(BF)
            q2, k, v = heads_of(l, c)
            probs = prob[l, c]
            grad_probs = dot_nt(ga2, v.astype(BF))
            grad_scores = probs * (
                grad_probs - jnp.sum(probs * grad_probs, axis=-1, keepdims=True)
            )
            low = grad_scores.astype(BF)
            grad_v = dot_tn(probs.astype(BF), ga2)
            grad_k = dot_tn(low, q2) * SCALING
            grad_q = (
                dot_nn(
                    jnp.concatenate([low[0:ROWS], low[ROWS:]], axis=1), split_heads(k).astype(BF)
                )
                * SCALING
            )
            pad = jnp.zeros((ROWS, 64), F32)
            gks[c] = jnp.concatenate([grad_k[ROWS:], grad_v[ROWS:], pad], axis=1).astype(BF)
            remote(gks.at[c], gkr.at[l, c], gs_s.at[c], gs_r.at[l, c], seq_dev).start()
            gkeep[c, :, 0:160] = grad_q
            gkeep[c, :, 160:320] = grad_k[0:ROWS]
            gkeep[c, :, 320:480] = grad_v[0:ROWS]
            gkeep[c, :, 480:512] = jnp.zeros((ROWS, 32), F32)
        for c in range(MICRO):
            wait_bytes(gkr.at[l, c], gs_r.at[l, c])
            wait_bytes(gkr.at[l, c], gs_s.at[c])
            far = gkr[l, c].astype(F32)
            gkeep[c, :, 160:480] += far[:, 0:320]
            grads = gkeep[c].astype(BF)
            gproj[c] = grads
            gb[pl.ds(l, 1), 0:512] += jnp.sum(grads.astype(F32), axis=0, keepdims=True)
            rs_start(a1, c, dot_nt(grads, W[l, 0, :, :, 0:512].reshape(D, 512)))

        @pl.loop(0, 2)
        def _(m):
            lanes = pl.ds(pl.multiple_of(m * 640, 128), 640)
            left = FB[2 * l, :, :, :, :, lanes].reshape(MICRO * ROWS, 640)
            first = dot_tn(left, gproj[...].reshape(MICRO * ROWS, 512))
            left_two = BB[b1, :, :, :, :, lanes].reshape(MICRO * ROWS, 640)
            second = dot_tn(left_two, att[l].reshape(MICRO * ROWS, 256))
            rows = pl.ds(m * 8, 8)
            dW[l, 0, rows, :, 0:384] = first[:, 0:384].astype(BF).reshape(8, SHARD, 384)
            dW[l, 0, rows, :, 384:512] = (first[:, 384:512] + second[:, 0:128]).astype(BF).reshape(8, SHARD, 128)
            dW[l, 0, rows, :, 512:640] = second[:, 128:256].astype(BF).reshape(8, SHARD, 128)

        send_part(l, 0)
        for c in range(MICRO):
            rs_mid(a1, c)
        for c in range(MICRO):
            grad_norm = rs_end(a1, c)
            unit, inv = norm_parts(xrow[l, c])
            gy = gmidrow[c] + norm_back(grad_norm, vec(l, 0), unit, inv)
            gyrow[c] = gy
            GV[l, 0:1, 0:D] += jnp.sum(grad_norm * unit, axis=0, keepdims=True)
            GV[l, 2:3, 0:D] += jnp.sum(grad_norm, axis=0, keepdims=True)
            ag_start(BB, b2, a1, c, gy)
        for c in range(MICRO):
            ag_mid(BB, b2, a1, c)
        for c in range(MICRO):
            ag_end(BB, b2, a1, c)
        return carry

    lax.fori_loop(0, 2, backward, 0)
    cp_g = pltpu.make_async_copy(BB.at[4], ingrad_ref, lsem.at[1])
    cp_g.start()

    for i in range(11):
        GT[i, 0:8] = GV[0, :, 128 * i : 128 * i + 128]
        GT[i, 8:16] = GV[1, :, 128 * i : 128 * i + 128]

    @pl.loop(1, SHARDS)
    def _(k):
        j, dev = shard_dev(k)
        remote(GT.at[pl.ds(SHARD * j // 128, 2)], vr.at[k - 1], es.at[0], er.at[0], dev).start()
        remote(gb, br.at[k - 1], es.at[1], er.at[1], dev).start()

    wait_bytes(vr, er.at[0])
    wait_bytes(vr, es.at[0])
    own = GT[pl.ds(SHARD * me // 128, 2)]
    for k in range(SHARDS - 1):
        own = own + vr[k]
    vr2[7] = own

    @pl.loop(1, 8)
    def _(k):
        remote(vr2.at[7], vr2.at[k - 1], es.at[2], er.at[2], (f, s, (t + k) % 8)).start()

    wait_bytes(br, er.at[1])
    wait_bytes(br, es.at[1])
    sums = gb[...]
    for k in range(SHARDS - 1):
        sums = sums + br[k]
    bout_ref[...] = sums

    for l in (1, 0):
        for p in (2, 1, 0):
            wait_bytes(rsb.at[l, p], rrs.at[l, p])
            wait_bytes(rsb.at[l, p], rss.at[l, p])
            total = dW[l, p, me].astype(F32)
            for k in range(SHARDS - 1):
                total = total + rsb[l, p, k].astype(F32)
            dwo_ref[l, p] = total

    wait_bytes(vr2.at[pl.ds(0, 7)], er.at[2])
    wait_bytes(vr2.at[pl.ds(0, 7)], es.at[2])
    own = vr2[7]
    for k in range(7):
        own = own + vr2[k]
    vout_ref[...] = own
    cp_o.wait()
    cp_g.wait()


def body(
    hidden_in, cotangent, lengths, qkv_weight, qv_bias, out_weight, out_bias,
    up_weight, up_bias, down_weight, down_bias, ln_gain, ln_bias,
):
    seq = lax.axis_index("seq")
    me = lax.axis_index("fsdp") * 2 + seq
    own_pos = seq * ROWS + jnp.arange(ROWS)
    far_pos = (1 - seq) * ROWS + jnp.arange(ROWS)
    keys = jnp.concatenate([own_pos, far_pos])
    live = (keys[None, :] < lengths[:, None]).astype(F32).reshape(MICRO, 1, 2 * ROWS)
    cot = jnp.where((own_pos[None, :] < lengths[:, None])[..., None], cotangent, jnp.zeros((), BF))
    first = jnp.concatenate(
        [qkv_weight[:, 0], qkv_weight[:, 1], qkv_weight[:, 2], jnp.swapaxes(out_weight, 1, 2)], axis=2
    )
    wown = jnp.stack([first, up_weight, jnp.swapaxes(down_weight, 1, 2)], axis=1)
    vectors = jnp.stack(
        [ln_gain[:, 0], ln_gain[:, 1], ln_bias[:, 0], ln_bias[:, 1], out_bias, down_bias], axis=1
    )
    vectors = jnp.pad(vectors, ((0, 0), (0, 2), (0, 0))).reshape(16, SHARD)
    offset = lax.rem(SHARD * me, 128)
    vectors = lax.dynamic_update_slice(jnp.zeros((16, 256), BF), vectors, (0, offset))
    zero = jnp.zeros((2, WIDTH), F32)
    qv = qv_bias.astype(F32)
    bqkv = jnp.concatenate([qv[:, 0], zero, qv[:, 1], zero[:, 0:32]], axis=1).reshape(2, 1, 512)
    bup = up_bias.astype(F32).reshape(2, 1, PART)

    vmem = pl.BlockSpec(memory_space=pltpu.VMEM)
    anys = pl.BlockSpec(memory_space=pl.ANY)
    dma = pltpu.SemaphoreType.DMA
    blocks = (MICRO, 4, 2, 16, D)
    scratch = [
        pltpu.VMEM((2, 3, SHARDS, SHARD, PART), BF),
        pltpu.VMEM((2, 3, SHARDS, SHARD, PART), BF),
        pltpu.VMEM((2, 3, SHARDS - 1, SHARD, PART), BF),
        pltpu.VMEM((5,) + blocks, BF),
        pltpu.VMEM((5,) + blocks, BF),
        pltpu.VMEM((8, MICRO, 4, 16, D), BF),
        pltpu.VMEM((8, MICRO, 3, 16, D), BF),
        pltpu.VMEM(blocks, BF),
        pltpu.VMEM((MICRO, 4, 16, D), BF),
        pltpu.VMEM((2, MICRO, ROWS, 512), BF),
        pltpu.VMEM((2, MICRO, ROWS, 384), BF),
        pltpu.VMEM((2, MICRO, 2 * ROWS, 2 * ROWS), F32),
        pltpu.VMEM((2, MICRO, ROWS, 256), BF),
        pltpu.VMEM((3, MICRO, 16, D), F32),
        pltpu.VMEM((2, MICRO, 16, D), F32),
        pltpu.VMEM((2, MICRO, ROWS, PART), F32),
        pltpu.VMEM((2, MICRO, ROWS, PART), BF),
        pltpu.VMEM((MICRO, ROWS, PART), BF),
        pltpu.VMEM((MICRO, ROWS, 512), F32),
        pltpu.VMEM((MICRO, ROWS, 512), BF),
        pltpu.VMEM((MICRO, ROWS, 384), BF),
        pltpu.VMEM((2, MICRO, ROWS, 384), BF),
        pltpu.VMEM((MICRO, 16, D), F32),
        pltpu.VMEM((MICRO, 16, D), F32),
        pltpu.VMEM((SHARDS, 16, 256), BF),
        pltpu.VMEM((2, 8, 1408), F32),
        pltpu.VMEM((2, 8, 1408), F32),
        pltpu.VMEM((11, 16, 128), F32),
        pltpu.VMEM((SHARDS - 1, 2, 16, 128), F32),
        pltpu.VMEM((8, 2, 16, 128), F32),
        pltpu.VMEM((8, PART), F32),
        pltpu.VMEM((SHARDS - 1, 8, PART), F32),
        dma((2, 3)), dma((2, 3)), dma((2, 3)), dma((2, 3)),
        dma((MICRO,)), dma((8, MICRO)), dma((MICRO,)), dma((8, MICRO)),
        dma((MICRO,)), dma((8, MICRO)), dma((MICRO,)), dma((8, MICRO)),
        dma((2, MICRO)), dma((2, MICRO)), dma((MICRO,)), dma((2, MICRO)),
        dma((1,)), dma((1,)), dma((3,)), dma((3,)), dma((2,)),
    ]
    out, ingrad, dwo, vout, bout = pl.pallas_call(
        kernel,
        name="encoder",
        out_shape=(
            jax.ShapeDtypeStruct(blocks, BF),
            jax.ShapeDtypeStruct(blocks, BF),
            jax.ShapeDtypeStruct((2, 3, SHARD, PART), F32),
            jax.ShapeDtypeStruct((2, 16, 128), F32),
            jax.ShapeDtypeStruct((8, PART), F32),
        ),
        in_specs=[anys, anys, vmem, vmem, vmem, vmem, vmem],
        out_specs=(anys, anys, vmem, vmem, vmem),
        scratch_shapes=scratch,
        compiler_params=pltpu.CompilerParams(
            collective_id=0, has_side_effects=True, vmem_limit_bytes=63 * 1024 * 1024
        ),
    )(hidden_in.reshape(blocks), cot.reshape(blocks), wown, vectors, bqkv, bup, live)

    out_hidden = out.reshape(MICRO, ROWS, D).astype(F32)
    in_grad = ingrad.reshape(MICRO, ROWS, D).astype(F32)
    first = dwo[:, 0]
    qkv_grad = jnp.stack([first[:, :, 0:160], first[:, :, 160:320], first[:, :, 320:480]], axis=1)
    out_grad = jnp.swapaxes(first[:, :, 480:640], 1, 2)
    up_grad = dwo[:, 1]
    down_grad = jnp.swapaxes(dwo[:, 2], 1, 2)
    rows = jnp.swapaxes(vout, 0, 1).reshape(16, 256)
    rows = lax.dynamic_slice(rows, (0, offset), (16, SHARD)).reshape(2, 8, SHARD)
    gain_grad = rows[:, 0:2]
    shift_grad = rows[:, 2:4]
    qv_grad = jnp.stack([bout[0:2, 0:160], bout[0:2, 320:480]], axis=1)
    return (
        out_hidden, in_grad, qkv_grad, qv_grad, out_grad, rows[:, 4], up_grad,
        bout[2:4], down_grad, rows[:, 5], gain_grad, shift_grad,
    )


def solution(mesh):
    placed = (
        P("fsdp", "seq", None),
        P("fsdp", "seq", None),
        P("fsdp"),
        P(None, None, ("fsdp", "seq"), "tp"),
        P(None, None, "tp"),
        P(None, "tp", ("fsdp", "seq")),
        P(None, ("fsdp", "seq")),
        P(None, ("fsdp", "seq"), "tp"),
        P(None, "tp"),
        P(None, "tp", ("fsdp", "seq")),
        P(None, ("fsdp", "seq")),
        P(None, None, ("fsdp", "seq")),
        P(None, None, ("fsdp", "seq")),
    )
    return jax.shard_map(
        body,
        mesh=mesh,
        in_specs=placed,
        out_specs=(
            P("fsdp", "seq", None),
            P("fsdp", "seq", None),
            P(None, None, ("fsdp", "seq"), "tp"),
            P(None, None, "tp"),
            P(None, "tp", ("fsdp", "seq")),
            P(None, ("fsdp", "seq")),
            P(None, ("fsdp", "seq"), "tp"),
            P(None, "tp"),
            P(None, "tp", ("fsdp", "seq")),
            P(None, ("fsdp", "seq")),
            P(None, None, ("fsdp", "seq")),
            P(None, None, ("fsdp", "seq")),
        ),
        check_vma=False,
    )
```

time: 2370 us -> 380 us (0.16)
  waiting for transfers between devices: 1430 us -> 0 us
  blocking collectives: 439 us -> 0 us
  Pallas kernels: 0 us -> 354 us
  local copies, waits for them, and re-layouts: 222 us -> 13 us
  matrix products: 153 us -> 0 us
  other arithmetic: 92.5 us -> 10.9 us
    psum x12 -> x0, waiting for transfers between devices: 618 us -> none  [the longest x6 347 us: input_total(): return lax.psum(partial_sum.astype(jnp.bfloat16), 'tp').astype(jnp.float32)]
    unnamed x57 -> x0, waiting for transfers between devices: 551 us -> none
    pallas_call x0 -> x1, Pallas kernels: none -> 354 us  [body(): pl.pallas_call(kernel, name='encoder', out_shape=(jax.ShapeDtypeStruct(bl...]
    all_gather x18 -> x0, blocking collectives: 330 us -> none  [the longest x2 95.8 us: fetch_layer(): lax.all_gather(out_weight[layer_idx], ('fsdp', 'seq'), axis=1, tiled=True)]
    all_gather x6 -> x0, waiting for transfers between devices: 174 us -> none  [the longest x2 75 us: fetch_layer(): lax.all_gather(down_weight[layer_idx], ('fsdp', 'seq'), axis=1, tiled=True)]
    dot_general x96 -> x0, matrix products: 138 us -> none  [the longest x6 17.8 us: forward_layer(): jnp.dot(activated, w_down, preferred_element_type=jnp.float32)]
    unnamed x837 -> x12, local copies, waits for them, and re-layouts: 100 us -> 3.21 us
    slice x24 -> x4, local copies, waits for them, and re-layouts: 93.5 us -> 2.48 us  [the longest x1 1.32 us: body(): bout[2:4]]
  transfers between devices with their start and end apart: 38 -> 0, of which waited for: 31 -> 0; matrix products, arithmetic and copies ran while one was open for 14% -> 0% of each run, Pallas kernels for 0% -> 0%
where the time goes in v1:
time: 380 us; the launch traced here: 378 us
  Pallas kernels  354 us (93%)
  local copies, waits for them, and re-layouts  13 us (3%)
  other arithmetic  10.9 us (3%)
    pallas_call x1, Pallas kernels, body(): pl.pallas_call(kernel, name='encoder', out_shape=(jax.ShapeDtypeStruct(bl...  354 us

profile of v1, /device:TPU:0, one launch (start us, length us, event | category | flops | bytes accessed | tf_op | source)
XLA Modules:
  0.0 378.3 jit_solution(13688811213482612421)
XLA Ops:
  0.7 0.8 broadcast_compare_fusion
  1.5 0.7 copy.37
  2.2 0.7 copy.38
  2.8 0.1 pad.13.clone
  2.9 0.1 pad.15.clone
  3.0 0.7 fusion.7
  3.7 1.3 compare_convert_fusion.live_ref
  5.0 0.7 copy_convert_fusion
  5.7 0.1 maximum_maximum_fusion
  5.8 0.6 reshape.129.bqkv_ref
  6.4 1.3 reshape.135.bup_ref
  7.6 0.1 dynamic_update_slice.3.vec_ref
  7.8 0.0 copy-start.3
  7.8 1.0 copy.36
  8.7 1.0 slice_bitcast_fusion.9
  9.7 0.2 maximum_bitcast_fusion
  9.9 1.9 pad_maximum_fusion.wown_ref
  11.8 1.1 broadcast_select_fusion
  12.9 353.6 %encoder.1 = (bf16[3,4,2,16,1280]{4,3,2,1,0:T(8,128)(2,1)}, bf16[3,4,2,16,1280]{4,3,2,1,0:T(8,128)(2,1)}, f32[2,3,80,640]{3,2,1,0:T(8,128)}, f32[2,16,128]{2,1,0:T(8,128)}, f32[8,640]{1,0:T(8,128)}) custom-call(bf16[3,4,2,16,1280]{4,3,2,1,0:T(8,128)(2,1)} %bitcast.66, bf16[3,4,2,16,1280]{4,3,2,1,0:T(8,128)(2,1)} %bitcast.65, ...), custom_call_target="tpu_custom_call" | custom-call | tf_op jit(solution)/shard_map/encoder/pallas_call | solution.py:493
  366.6 0.9 slice_bitcast_fusion.13
  367.5 1.3 slice.81
  368.8 0.6 copy.42
  369.4 0.7 copy_bitcast_fusion
  370.1 0.1 dynamic-slice_bitcast_fusion
  370.2 0.6 fusion.9
  370.7 0.6 fusion.8
  371.3 2.6 bitcast_convert_fusion.1
  374.0 1.0 slice_bitcast_fusion
  374.9 0.2 slice_bitcast_fusion.3
  375.1 0.8 copy.43
  376.0 0.8 copy.41
  376.8 1.5 bitcast_convert_fusion
  (15 shorter events, 0.1 us)
Async XLA Ops:
  0.6 11.2 %copy-start.1 = (bf16[3,128,1280]{2,1,0:T(8,128)(2,1)S(1)}, bf16[3,128,1280]{2,1,0:T(8,128)(2,1)}, u32[]{:S(2)}) copy-start(bf16[3,128,1280]{2,1,0:T(8,128)(2,1)} %param.14) | copy-start | bytes 2949124
  7.8 5.2 %copy-start.3 = (bf16[16,256]{1,0:T(8,128)(2,1)}, bf16[16,256]{1,0:T(8,128)(2,1)S(1)}, u32[]{:S(2)}) copy-start(bf16[16,256]{1,0:T(8,128)(2,1)S(1)} %dynamic_update_slice.3.vec_ref) | copy-start | bytes 24580
  366.5 7.4 %copy-start = (f32[2,3,80,640]{3,2,1,0:T(8,128)S(1)}, f32[2,3,80,640]{3,2,1,0:T(8,128)}, u32[]{:S(2)}) copy-start(f32[2,3,80,640]{3,2,1,0:T(8,128)} %get-tuple-element.19) | copy-start | bytes 3686404
  374.9 1.9 copy-start.2

commit v2 on v1

v2 whole, which is shorter than its diff:
```python
from functools import partial
import math

import jax
import jax.numpy as jnp
from jax import lax
from jax.experimental import pallas as pl
from jax.experimental.pallas import tpu as pltpu
from jax.sharding import PartitionSpec as P

HD = 80
EPSILON = 1e-05
MASKED = -1000000000.0
MESH = pl.DeviceIdType.MESH
BF = jnp.bfloat16
F32 = jnp.float32
SCALING = 1.0 / math.sqrt(HD)

D = 1280
MICRO = 3
ROWS = 128
PART = 640
SHARDS = 16
SHARD = 80
WIDTH = 160

PIECES = (
    (0, (256, 512), (0, 256)),
    (0, (512, 640), None),
    (1, (384, 640), (0, 384)),
    (2, (384, 640), (0, 384)),
)
QKV, OUT, UP, DOWN = range(4)


def dot_nn(a, b):
    return lax.dot_general(a, b, (((1,), (0,)), ((), ())), preferred_element_type=F32)


def dot_nt(a, b):
    return lax.dot_general(a, b, (((1,), (1,)), ((), ())), preferred_element_type=F32)


def dot_tn(a, b):
    return lax.dot_general(a, b, (((0,), (0,)), ((), ())), preferred_element_type=F32)


def norm_parts(values):
    row_mean = jnp.mean(values, axis=-1, keepdims=True)
    centred = values - row_mean
    row_var = jnp.mean(centred * centred, axis=-1, keepdims=True)
    inv = lax.rsqrt(row_var + EPSILON)
    return centred * inv, inv


def norm_back(grad, gain, unit, inv):
    scaled = grad * gain
    return inv * (
        scaled
        - jnp.mean(scaled, axis=-1, keepdims=True)
        - unit * jnp.mean(scaled * unit, axis=-1, keepdims=True)
    )


def split_heads(x):
    first = lax.broadcasted_iota(jnp.int32, x.shape, 1) < HD
    return jnp.concatenate([jnp.where(first, x, 0.0), jnp.where(first, 0.0, x)], axis=0)


def kernel(
    hid_ref, cot_ref, wown_ref, vec_ref, bqkv_ref, bup_ref, live_ref,
    out_ref, ingrad_ref, dwo_ref, vout_ref, bout_ref,
    W, dW, rb1, rb2, rc, FB, BB, dr, yr, part, sb,
    qkv, kvo, prob, att, xrow, midrow, slope, act,
    gpre, gkeep, gproj, gks, gkr, gyrow, gmidrow,
    VG, V, GV, GT, vr, vr2, gb, br,
    g1s, g1r, g2s, g2r, q1s, q1r, q2s, q2r,
    s1, r1, s2, r2, s3, r3, s4, r4, ks, kr, gs_s, gs_r, vs, vrs, es, er, lsem,
):
    f, s, t = lax.axis_index("fsdp"), lax.axis_index("seq"), lax.axis_index("tp")
    me = f * 2 + s
    xh, z = f // 4, f % 4
    x = xh * 2 + s
    y, core = t // 2, t % 2
    other = 1 - core

    def shard_dev(k):
        j = (me + k) % SHARDS
        return j, (j // 2, j % 2, t)

    def x_dev(k):
        j = (x + k) % 4
        return j // 2, j % 2, ((j // 2) * 4 + z, j % 2, t)

    def z_dev(k):
        j = (z + k) % 4
        return j, (xh * 4 + j, s, t)

    def y_dev(k):
        j = (y + k) % 4
        return j, (f, s, j * 2 + core)

    core_dev = (f, s, y * 2 + other)
    seq_dev = (f, 1 - s, t)

    def remote(src, dst, ss, rs, dev):
        return pltpu.make_async_remote_copy(
            src_ref=src, dst_ref=dst, send_sem=ss, recv_sem=rs, device_id=dev, device_id_type=MESH
        )

    def wait_bytes(ref, sem):
        pltpu.make_async_copy(ref, ref, sem).wait()

    cp_h = pltpu.make_async_copy(hid_ref, FB.at[0], lsem.at[0])
    cp_c = pltpu.make_async_copy(cot_ref, BB.at[0], lsem.at[1])
    cp_h.start()
    cp_c.start()

    barrier = pltpu.get_barrier_semaphore()

    @pl.loop(1, SHARDS)
    def _(k):
        pl.semaphore_signal(barrier, inc=1, device_id=shard_dev(k)[1], device_id_type=MESH)

    @pl.loop(1, 8)
    def _(k):
        pl.semaphore_signal(barrier, inc=1, device_id=(f, s, (t + k) % 8), device_id_type=MESH)

    pl.semaphore_wait(barrier, 22)

    def piece(l, i):
        part_idx, one, two = PIECES[i]
        both = [(0, slice(*one))] + ([(1, slice(*two))] if two else [])
        return part_idx, both

    def gather_one(l, i):
        p, ways = piece(l, i)
        for way, cols in ways:
            W[l, p, xh, z, s, :, cols] = wown_ref[l, p, :, cols]
            own = W.at[l, p, xh, z, s, :, cols]
            for k in range(1, 4):
                dev = x_dev(k)[2] if way else z_dev(k)[1]
                remote(own, own, g1s.at[l, i, way], g1r.at[l, i, way], dev).start()

    def gather_mid(l, i):
        p, ways = piece(l, i)
        for way, cols in ways:
            three = W.at[l, p, 0, pl.ds(0, 3), 0, :, cols]
            wait_bytes(three, g1r.at[l, i, way])
            wait_bytes(three, g1s.at[l, i, way])

    def gather_two(l, i):
        p, ways = piece(l, i)
        gather_mid(l, i)
        for way, cols in ways:
            four = W.at[l, p, :, z, :, :, cols] if way else W.at[l, p, xh, :, s, :, cols]
            for k in range(1, 4):
                dev = z_dev(k)[1] if way else x_dev(k)[2]
                remote(four, four, g2s.at[l, i, way], g2r.at[l, i, way], dev).start()

    def gather_wait(l, i):
        p, ways = piece(l, i)
        for way, cols in ways:
            twelve = W.at[l, p, :, pl.ds(0, 3), :, :, cols]
            wait_bytes(twelve, g2r.at[l, i, way])
            wait_bytes(twelve, g2s.at[l, i, way])

    def reduce_one(l, i):
        p, ways = piece(l, i)
        for way, cols in ways:
            for k in range(1, 4):
                if way:
                    j, dev = z_dev(k)
                    four = dW.at[l, p, :, j, :, :, cols]
                    buf = rb2.at[l, p, k - 1, :, :, :, 0 : cols.stop - cols.start]
                else:
                    jh, jl, dev = x_dev(k)
                    four = dW.at[l, p, jh, :, jl, :, cols]
                    buf = rb1.at[l, p, k - 1, :, :, cols.start - 256 : cols.stop - 256]
                remote(four, buf, q1s.at[l, i, way], q1r.at[l, i, way], dev).start()

    def reduce_mid(l, i):
        p, ways = piece(l, i)
        for way, cols in ways:
            twelve = dW.at[l, p, :, pl.ds(0, 3), :, :, cols]
            wait_bytes(twelve, q1r.at[l, i, way])
            wait_bytes(twelve, q1s.at[l, i, way])

    def reduce_two(l, i):
        p, ways = piece(l, i)
        reduce_mid(l, i)

        @pl.loop(0, 4)
        def _(n):
            nh, nl = n // 2, n % 2
            for way, cols in ways:
                if way:
                    total = dW[l, p, nh, z, nl, :, cols].astype(F32)
                    for k in range(3):
                        total = total + rb2[l, p, k, nh, nl, :, 0 : cols.stop - cols.start].astype(F32)
                    dW[l, p, nh, z, nl, :, cols] = total.astype(BF)
                else:
                    total = dW[l, p, xh, n, s, :, cols].astype(F32)
                    for k in range(3):
                        total = total + rb1[l, p, k, n, :, cols.start - 256 : cols.stop - 256].astype(F32)
                    dW[l, p, xh, n, s, :, cols] = total.astype(BF)

        for way, cols in ways:
            for k in range(1, 4):
                if way:
                    jh, jl, dev = x_dev(k)
                    one = dW.at[l, p, jh, z, jl, :, cols]
                else:
                    j, dev = z_dev(k)
                    one = dW.at[l, p, xh, j, s, :, cols]
                remote(one, rc.at[l, p, k - 1, :, cols], q2s.at[l, i, way], q2r.at[l, i, way], dev).start()

    def reduce_last(l, i):
        p, ways = piece(l, i)
        for way, cols in ways:
            three = dW.at[l, p, 0, pl.ds(0, 3), 0, :, cols]
            wait_bytes(three, q2r.at[l, i, way])
            wait_bytes(three, q2s.at[l, i, way])

    def reduce_three(l, i):
        p, ways = piece(l, i)
        reduce_last(l, i)
        for way, cols in ways:
            total = dW[l, p, xh, z, s, :, cols].astype(F32)
            for k in range(3):
                total = total + rc[l, p, k, :, cols].astype(F32)
            dwo_ref[l, p, :, cols] = total

    def vec(l, r):
        return V[l, r : r + 1, 0:D]

    def rs_start(a, c, value):
        part[c] = value.astype(BF).reshape(4, 2, 16, D)
        remote(part.at[c, :, other], dr.at[a, c], s1.at[c], r1.at[a, c], core_dev).start()

    def rs_mid(a, c):
        wait_bytes(dr.at[a, c], r1.at[a, c])
        wait_bytes(dr.at[a, c], s1.at[c])
        sb[c] = (part[c, :, core].astype(F32) + dr[a, c].astype(F32)).astype(BF)
        for k in range(1, 4):
            j, dev = y_dev(k)
            remote(sb.at[c, j], yr.at[a, c, k - 1], s2.at[c], r2.at[a, c], dev).start()

    def rs_end(a, c):
        wait_bytes(yr.at[a, c], r2.at[a, c])
        wait_bytes(yr.at[a, c], s2.at[c])
        total = sb[c, y].astype(F32)
        for k in range(3):
            total = total + yr[a, c, k].astype(F32)
        return total

    def ag_start(buf, i, a, c, value):
        buf[i, c, y, core] = value.astype(BF)
        for k in range(1, 4):
            _, dev = y_dev(k)
            remote(buf.at[i, c, y, core], buf.at[i, c, y, core], s3.at[c], r3.at[a, c], dev).start()

    def ag_mid(buf, i, a, c):
        wait_bytes(yr.at[a, c], r3.at[a, c])
        wait_bytes(yr.at[a, c], s3.at[c])
        remote(buf.at[i, c, :, core], buf.at[i, c, :, core], s4.at[c], r4.at[a, c], core_dev).start()

    def ag_end(a, c):
        wait_bytes(dr.at[a, c], r4.at[a, c])
        wait_bytes(dr.at[a, c], s4.at[c])

    def heads_of(l, c):
        own = qkv[l, c].astype(F32)
        far = kvo[l, c].astype(F32)
        q = own[:, 0:160]
        k = jnp.concatenate([own[:, 160:320], far[:, 32:192]], axis=0)
        v = jnp.concatenate([own[:, 320:480], far[:, 192:352]], axis=0)
        return split_heads(q).astype(BF), k, v

    def project(l, c):
        normed = FB[2 * l, c].reshape(ROWS, D)
        proj = dot_nn(normed, W[l, 0, :, :, :, :, 0:512].reshape(D, 512)) + bqkv_ref[l]
        qkv[l, c] = proj.astype(BF)
        remote(qkv.at[l, c, :, 128:512], kvo.at[l, c], ks.at[l, c], kr.at[l, c], seq_dev).start()

    def attend(l, c):
        wait_bytes(kvo.at[l, c], kr.at[l, c])
        wait_bytes(kvo.at[l, c], ks.at[l, c])
        q2, k, v = heads_of(l, c)
        scores = dot_nt(q2, k.astype(BF)) * SCALING
        scores = jnp.where(live_ref[c] > 0.0, scores, MASKED)
        top = jnp.max(scores, axis=-1, keepdims=True)
        powers = jnp.exp(scores - top)
        probs = powers / jnp.sum(powers, axis=-1, keepdims=True)
        prob[l, c] = probs
        low = probs.astype(BF)
        attended = dot_nn(
            jnp.concatenate([low[0:ROWS], low[ROWS:]], axis=1), split_heads(v).astype(BF)
        )
        wide = jnp.concatenate([jnp.zeros((ROWS, 96), F32), attended], axis=1).astype(BF)
        att[l, c] = wide
        rs_start(2 * l, c, dot_nt(wide, W[l, 0, :, :, :, :, 384:640].reshape(D, 256)))

    def attend_rows(l, c):
        a = 2 * l
        middle = xrow[l, c] + rs_end(a, c) + vec(l, 4)
        midrow[l, c] = middle
        unit, _ = norm_parts(middle)
        ag_start(FB, 2 * l + 1, a, c, unit * vec(l, 1) + vec(l, 3))

    def feed(l, c):
        normed = FB[2 * l + 1, c].reshape(ROWS, D)
        pre = dot_nn(normed, W[l, 1].reshape(D, PART)) + bup_ref[l]
        cdf = 0.5 * (1.0 + lax.erf(pre * math.sqrt(0.5)))
        activated = (pre * cdf).astype(BF)
        act[l, c] = activated
        slope[l, c] = cdf + pre * jnp.exp(-0.5 * pre * pre) * (1.0 / math.sqrt(2.0 * math.pi))
        rs_start(2 * l + 1, c, dot_nt(activated, W[l, 2].reshape(D, PART)))

    def feed_rows(l, c):
        a = 2 * l + 1
        hidden = midrow[l, c] + rs_end(a, c) + vec(l, 5)
        if l == 0:
            xrow[1, c] = hidden
            unit, _ = norm_parts(hidden)
            hidden = unit * vec(1, 0) + vec(1, 2)
        ag_start(FB, 2 * l + 2, a, c, hidden)

    def feed_back(l, c):
        grad_act = dot_nn(BB[2 - 2 * l, c].reshape(ROWS, D), W[l, 2].reshape(D, PART))
        grad_pre = (grad_act * slope[l, c]).astype(BF)
        gpre[c] = grad_pre
        gb[2 + l : 3 + l, :] += jnp.sum(grad_pre.astype(F32), axis=0, keepdims=True)
        rs_start(6 - 2 * l, c, dot_nt(grad_pre, W[l, 1].reshape(D, PART)))

    def feed_back_rows(l, c):
        a = 6 - 2 * l
        grad_norm = rs_end(a, c)
        unit, inv = norm_parts(midrow[l, c])
        gy = gyrow[c]
        grad_mid = gy + norm_back(grad_norm, vec(l, 1), unit, inv)
        gmidrow[c] = grad_mid
        ag_start(BB, 3 - 2 * l, a, c, grad_mid)
        GV[l, 1:2, 0:D] += jnp.sum(grad_norm * unit, axis=0, keepdims=True)
        GV[l, 3:4, 0:D] += jnp.sum(grad_norm, axis=0, keepdims=True)
        GV[l, 4:5, 0:D] += jnp.sum(grad_mid, axis=0, keepdims=True)
        GV[l, 5:6, 0:D] += jnp.sum(gy, axis=0, keepdims=True)

    def attend_back(l, c):
        wide = dot_nn(BB[3 - 2 * l, c].reshape(ROWS, D), W[l, 0, :, :, :, :, 384:640].reshape(D, 256))
        ga2 = split_heads(wide[:, 96:256]).astype(BF)
        q2, k, v = heads_of(l, c)
        probs = prob[l, c]
        grad_probs = dot_nt(ga2, v.astype(BF))
        grad_scores = probs * (grad_probs - jnp.sum(probs * grad_probs, axis=-1, keepdims=True))
        low = grad_scores.astype(BF)
        grad_v = dot_tn(probs.astype(BF), ga2)
        grad_k = dot_tn(low, q2) * SCALING
        pad = jnp.zeros((ROWS, 64), F32)
        gks[c] = jnp.concatenate([grad_k[ROWS:], grad_v[ROWS:], pad], axis=1).astype(BF)
        remote(gks.at[c], gkr.at[l, c], gs_s.at[c], gs_r.at[l, c], seq_dev).start()
        grad_q = (
            dot_nn(jnp.concatenate([low[0:ROWS], low[ROWS:]], axis=1), split_heads(k).astype(BF))
            * SCALING
        )
        gkeep[c, :, 0:160] = grad_q
        gkeep[c, :, 160:320] = grad_k[0:ROWS]
        gkeep[c, :, 320:480] = grad_v[0:ROWS]
        gkeep[c, :, 480:512] = jnp.zeros((ROWS, 32), F32)

    def project_back(l, c):
        wait_bytes(gkr.at[l, c], gs_r.at[l, c])
        wait_bytes(gkr.at[l, c], gs_s.at[c])
        far = gkr[l, c].astype(F32)
        gkeep[c, :, 160:480] += far[:, 0:320]
        grads = gkeep[c].astype(BF)
        gproj[c] = grads
        gb[l : l + 1, 0:512] += jnp.sum(grads.astype(F32), axis=0, keepdims=True)
        rs_start(7 - 2 * l, c, dot_nt(grads, W[l, 0, :, :, :, :, 0:512].reshape(D, 512)))

    def project_back_rows(l, c):
        a = 7 - 2 * l
        grad_norm = rs_end(a, c)
        unit, inv = norm_parts(xrow[l, c])
        gy = gmidrow[c] + norm_back(grad_norm, vec(l, 0), unit, inv)
        gyrow[c] = gy
        ag_start(BB, 4 - 2 * l, a, c, gy)
        GV[l, 0:1, 0:D] += jnp.sum(grad_norm * unit, axis=0, keepdims=True)
        GV[l, 2:3, 0:D] += jnp.sum(grad_norm, axis=0, keepdims=True)

    def left_of(buf, i, m):
        return buf[i, :, :, :, :, 640 * m : 640 * m + 640].reshape(MICRO * ROWS, 640)

    def down_grad(l, m):
        right = act[l].reshape(MICRO * ROWS, PART)
        dW[l, 2, m] = dot_tn(left_of(BB, 2 - 2 * l, m), right).astype(BF).reshape(4, 2, SHARD, PART)

    def up_grad(l, m):
        right = gpre[...].reshape(MICRO * ROWS, PART)
        dW[l, 1, m] = dot_tn(left_of(FB, 2 * l + 1, m), right).astype(BF).reshape(4, 2, SHARD, PART)

    def out_grad(l, m):
        grad = dot_tn(left_of(BB, 3 - 2 * l, m), att[l].reshape(MICRO * ROWS, 256))
        dW[l, 0, m, :, :, :, 384:640] = grad.astype(BF).reshape(4, 2, SHARD, 256)

    def qkv_grad(l, m):
        grad = dot_tn(left_of(FB, 2 * l, m), gproj[...].reshape(MICRO * ROWS, 512))
        dW[l, 0, m, :, :, :, 0:384] = grad[:, 0:384].astype(BF).reshape(4, 2, SHARD, 384)
        rest = dW[l, 0, m, :, :, :, 384:512].astype(F32).reshape(640, 128) + grad[:, 384:512]
        dW[l, 0, m, :, :, :, 384:512] = rest.astype(BF).reshape(4, 2, SHARD, 128)

    @pl.loop(1, SHARDS)
    def _(k):
        remote(vec_ref, VG.at[me], vs.at[0], vrs.at[0], shard_dev(k)[1]).start()

    VG[me] = vec_ref[...]
    gather_one(0, QKV)
    V[...] = jnp.zeros_like(V)
    GV[...] = jnp.zeros_like(GV)
    gb[...] = jnp.zeros_like(gb)
    gather_two(0, QKV)
    gather_one(0, OUT)
    gather_one(0, UP)
    wait_bytes(VG.at[pl.ds(0, SHARDS - 1)], vrs.at[0])
    wait_bytes(VG.at[pl.ds(0, SHARDS - 1)], vs.at[0])
    for i in range(SHARDS):
        low = SHARD * i // 128 * 128
        held = VG[i].astype(F32)
        V[0, :, low : low + 256] += held[0:8]
        V[1, :, low : low + 256] += held[8:16]
    cp_h.wait()
    cp_c.wait()
    for c in range(MICRO):
        whole = FB[0, c].reshape(ROWS, D).astype(F32)
        unit, _ = norm_parts(whole)
        xrow[0, c] = FB[0, c, y, core].astype(F32)
        FB[0, c] = (unit * vec(0, 0) + vec(0, 2)).astype(BF).reshape(4, 2, 16, D)
        gyrow[c] = BB[0, c, y, core].astype(F32)
    gather_two(0, OUT)
    gather_wait(0, QKV)
    gather_two(0, UP)
    gather_one(0, DOWN)

    cp_o = pltpu.make_async_copy(FB.at[4], out_ref, lsem.at[0])
    cp_g = pltpu.make_async_copy(BB.at[4], ingrad_ref, lsem.at[1])

    steps = []
    sums = {}
    for l in (0, 1):
        for c in range(MICRO):
            steps.append((partial(project, l, c), None))
        for c in range(MICRO):
            steps.append((partial(attend, l, c), (2 * l, c)))
            sums[2 * l, c] = (partial(attend_rows, l, c), FB, 2 * l + 1)
        for c in range(MICRO):
            steps.append((partial(feed, l, c), (2 * l + 1, c)))
            sums[2 * l + 1, c] = (partial(feed_rows, l, c), FB, 2 * l + 2)
    for l in (1, 0):
        a0, a1 = 6 - 2 * l, 7 - 2 * l
        for c in range(MICRO):
            steps.append((partial(feed_back, l, c), (a0, c)))
            sums[a0, c] = (partial(feed_back_rows, l, c), BB, 3 - 2 * l)
        for c in range(MICRO):
            steps.append((partial(attend_back, l, c), None))
        for c in range(MICRO):
            steps.append((partial(project_back, l, c), (a1, c)))
            sums[a1, c] = (partial(project_back_rows, l, c), BB, 4 - 2 * l)

    g1, g2, g3 = gather_one, gather_two, gather_wait
    d1, d2 = reduce_one, reduce_two
    before = {
        3: [(g3, 0, OUT)],
        6: [(g3, 0, UP), (g3, 0, DOWN)],
        9: [(g3, 1, QKV)],
        12: [(g3, 1, OUT)],
        15: [(g3, 1, UP), (g3, 1, DOWN)],
    }
    between = {
        3: [(g2, 0, DOWN), (g1, 1, QKV), (g1, 1, OUT)],
        5: [(g2, 1, QKV), (g2, 1, OUT), (g1, 1, UP)],
        8: [(g2, 1, UP), (g1, 1, DOWN)],
        11: [(g2, 1, DOWN)],
        18: [(down_grad, 1, 0)],
        19: [(down_grad, 1, 1), (d1, 1, DOWN)],
        21: [(up_grad, 1, 0)],
        22: [(up_grad, 1, 1), (d1, 1, UP)],
        23: [(d2, 1, DOWN)],
        24: [(out_grad, 1, 0)],
        25: [(out_grad, 1, 1), (d1, 1, OUT)],
        26: [(d2, 1, UP)],
        27: [(qkv_grad, 1, 0)],
        28: [(qkv_grad, 1, 1), (d1, 1, QKV)],
        29: [(down_grad, 0, 0), (d2, 1, OUT)],
        30: [(down_grad, 0, 1), (d1, 0, DOWN)],
        31: [(up_grad, 0, 0)],
        32: [(up_grad, 0, 1), (d1, 0, UP)],
        33: [(out_grad, 0, 0), (d2, 1, QKV)],
        34: [(out_grad, 0, 1), (d1, 0, OUT)],
        35: [(d2, 0, DOWN)],
        36: [(qkv_grad, 0, 0), (qkv_grad, 0, 1), (d1, 0, QKV)],
        37: [(d2, 0, UP)],
    }
    for n in range(len(steps) + 2):
        for fn, l, i in before.get(n, ()):
            fn(l, i)
        if n < len(steps):
            steps[n][0]()
        for fn, l, i in between.get(n, ()):
            fn(l, i)
        if n < len(steps) and steps[n][1] is not None:
            rs_mid(*steps[n][1])
        if 1 <= n <= len(steps) and steps[n - 1][1] is not None:
            sums[steps[n - 1][1]][0]()
        if n >= 2 and steps[n - 2][1] is not None:
            a, c = steps[n - 2][1]
            ag_mid(sums[a, c][1], sums[a, c][2], a, c)
            ag_end(a, c)
        if n == 19:
            cp_o.start()

    for i in range(11):
        GT[i, 0:8] = GV[0, :, 128 * i : 128 * i + 128]
        GT[i, 8:16] = GV[1, :, 128 * i : 128 * i + 128]

    @pl.loop(1, SHARDS)
    def _(k):
        j, dev = shard_dev(k)
        remote(GT.at[pl.ds(SHARD * j // 128, 2)], vr.at[k - 1], es.at[0], er.at[0], dev).start()
        remote(gb, br.at[k - 1], es.at[1], er.at[1], dev).start()

    cp_g.start()
    wait_bytes(vr, er.at[0])
    wait_bytes(vr, es.at[0])
    own = GT[pl.ds(SHARD * me // 128, 2)]
    for k in range(SHARDS - 1):
        own = own + vr[k]
    vr2[7] = own

    @pl.loop(1, 8)
    def _(k):
        remote(vr2.at[7], vr2.at[k - 1], es.at[2], er.at[2], (f, s, (t + k) % 8)).start()

    reduce_two(0, OUT)
    reduce_two(0, QKV)
    wait_bytes(br, er.at[1])
    wait_bytes(br, es.at[1])
    totals = gb[...]
    for k in range(SHARDS - 1):
        totals = totals + br[k]
    bout_ref[...] = totals
    for l, i in ((1, DOWN), (1, UP), (1, OUT), (1, QKV), (0, DOWN), (0, UP), (0, OUT)):
        reduce_three(l, i)
    wait_bytes(vr2.at[pl.ds(0, 7)], er.at[2])
    wait_bytes(vr2.at[pl.ds(0, 7)], es.at[2])
    own = vr2[7]
    for k in range(7):
        own = own + vr2[k]
    vout_ref[...] = own
    reduce_three(0, QKV)
    cp_o.wait()
    cp_g.wait()


def body(
    hidden_in, cotangent, lengths, qkv_weight, qv_bias, out_weight, out_bias,
    up_weight, up_bias, down_weight, down_bias, ln_gain, ln_bias,
):
    seq = lax.axis_index("seq")
    me = lax.axis_index("fsdp") * 2 + seq
    own_pos = seq * ROWS + jnp.arange(ROWS)
    far_pos = (1 - seq) * ROWS + jnp.arange(ROWS)
    keys = jnp.concatenate([own_pos, far_pos])
    live = (keys[None, :] < lengths[:, None]).astype(F32).reshape(MICRO, 1, 2 * ROWS)
    cot = jnp.where((own_pos[None, :] < lengths[:, None])[..., None], cotangent, jnp.zeros((), BF))
    first = jnp.concatenate(
        [qkv_weight[:, 0], qkv_weight[:, 1], qkv_weight[:, 2], jnp.swapaxes(out_weight, 1, 2)], axis=2
    )
    wown = jnp.stack([first, up_weight, jnp.swapaxes(down_weight, 1, 2)], axis=1)
    vectors = jnp.stack(
        [ln_gain[:, 0], ln_gain[:, 1], ln_bias[:, 0], ln_bias[:, 1], out_bias, down_bias], axis=1
    )
    vectors = jnp.pad(vectors, ((0, 0), (0, 2), (0, 0))).reshape(16, SHARD)
    offset = lax.rem(SHARD * me, 128)
    vectors = lax.dynamic_update_slice(jnp.zeros((16, 256), BF), vectors, (0, offset))
    zero = jnp.zeros((2, WIDTH), F32)
    qv = qv_bias.astype(F32)
    bqkv = jnp.concatenate([qv[:, 0], zero, qv[:, 1], zero[:, 0:32]], axis=1).reshape(2, 1, 512)
    bup = up_bias.astype(F32).reshape(2, 1, PART)

    vmem = pl.BlockSpec(memory_space=pltpu.VMEM)
    anys = pl.BlockSpec(memory_space=pl.ANY)
    dma = pltpu.SemaphoreType.DMA
    blocks = (MICRO, 4, 2, 16, D)
    scratch = [
        pltpu.VMEM((2, 3, 2, 4, 2, SHARD, PART), BF),
        pltpu.VMEM((2, 3, 2, 4, 2, SHARD, PART), BF),
        pltpu.VMEM((2, 3, 3, 4, SHARD, 384), BF),
        pltpu.VMEM((2, 3, 3, 2, 2, SHARD, 384), BF),
        pltpu.VMEM((2, 3, 3, SHARD, PART), BF),
        pltpu.VMEM((5,) + blocks, BF),
        pltpu.VMEM((5,) + blocks, BF),
        pltpu.VMEM((8, MICRO, 4, 16, D), BF),
        pltpu.VMEM((8, MICRO, 3, 16, D), BF),
        pltpu.VMEM(blocks, BF),
        pltpu.VMEM((MICRO, 4, 16, D), BF),
        pltpu.VMEM((2, MICRO, ROWS, 512), BF),
        pltpu.VMEM((2, MICRO, ROWS, 384), BF),
        pltpu.VMEM((2, MICRO, 2 * ROWS, 2 * ROWS), F32),
        pltpu.VMEM((2, MICRO, ROWS, 256), BF),
        pltpu.VMEM((2, MICRO, 16, D), F32),
        pltpu.VMEM((2, MICRO, 16, D), F32),
        pltpu.VMEM((2, MICRO, ROWS, PART), F32),
        pltpu.VMEM((2, MICRO, ROWS, PART), BF),
        pltpu.VMEM((MICRO, ROWS, PART), BF),
        pltpu.VMEM((MICRO, ROWS, 512), F32),
        pltpu.VMEM((MICRO, ROWS, 512), BF),
        pltpu.VMEM((MICRO, ROWS, 384), BF),
        pltpu.VMEM((2, MICRO, ROWS, 384), BF),
        pltpu.VMEM((MICRO, 16, D), F32),
        pltpu.VMEM((MICRO, 16, D), F32),
        pltpu.VMEM((SHARDS, 16, 256), BF),
        pltpu.VMEM((2, 8, 1408), F32),
        pltpu.VMEM((2, 8, 1408), F32),
        pltpu.VMEM((11, 16, 128), F32),
        pltpu.VMEM((SHARDS - 1, 2, 16, 128), F32),
        pltpu.VMEM((8, 2, 16, 128), F32),
        pltpu.VMEM((8, PART), F32),
        pltpu.VMEM((SHARDS - 1, 8, PART), F32),
        dma((2, 4, 2)), dma((2, 4, 2)), dma((2, 4, 2)), dma((2, 4, 2)),
        dma((2, 4, 2)), dma((2, 4, 2)), dma((2, 4, 2)), dma((2, 4, 2)),
        dma((MICRO,)), dma((8, MICRO)), dma((MICRO,)), dma((8, MICRO)),
        dma((MICRO,)), dma((8, MICRO)), dma((MICRO,)), dma((8, MICRO)),
        dma((2, MICRO)), dma((2, MICRO)), dma((MICRO,)), dma((2, MICRO)),
        dma((1,)), dma((1,)), dma((3,)), dma((3,)), dma((2,)),
    ]
    out, ingrad, dwo, vout, bout = pl.pallas_call(
        kernel,
        name="encoder",
        out_shape=(
            jax.ShapeDtypeStruct(blocks, BF),
            jax.ShapeDtypeStruct(blocks, BF),
            jax.ShapeDtypeStruct((2, 3, SHARD, PART), F32),
            jax.ShapeDtypeStruct((2, 16, 128), F32),
            jax.ShapeDtypeStruct((8, PART), F32),
        ),
        in_specs=[anys, anys, vmem, vmem, vmem, vmem, vmem],
        out_specs=(anys, anys, vmem, vmem, vmem),
        scratch_shapes=scratch,
        compiler_params=pltpu.CompilerParams(
            collective_id=0, has_side_effects=True, vmem_limit_bytes=63 * 1024 * 1024
        ),
    )(hidden_in.reshape(blocks), cot.reshape(blocks), wown, vectors, bqkv, bup, live)

    out_hidden = out.reshape(MICRO, ROWS, D).astype(F32)
    in_grad = ingrad.reshape(MICRO, ROWS, D).astype(F32)
    first = dwo[:, 0]
    qkv_grad = jnp.stack([first[:, :, 0:160], first[:, :, 160:320], first[:, :, 320:480]], axis=1)
    out_grad = jnp.swapaxes(first[:, :, 480:640], 1, 2)
    up_grad = dwo[:, 1]
    down_grad = jnp.swapaxes(dwo[:, 2], 1, 2)
    rows = jnp.swapaxes(vout, 0, 1).reshape(16, 256)
    rows = lax.dynamic_slice(rows, (0, offset), (16, SHARD)).reshape(2, 8, SHARD)
    gain_grad = rows[:, 0:2]
    shift_grad = rows[:, 2:4]
    qv_grad = jnp.stack([bout[0:2, 0:160], bout[0:2, 320:480]], axis=1)
    return (
        out_hidden, in_grad, qkv_grad, qv_grad, out_grad, rows[:, 4], up_grad,
        bout[2:4], down_grad, rows[:, 5], gain_grad, shift_grad,
    )


def solution(mesh):
    placed = (
        P("fsdp", "seq", None),
        P("fsdp", "seq", None),
        P("fsdp"),
        P(None, None, ("fsdp", "seq"), "tp"),
        P(None, None, "tp"),
        P(None, "tp", ("fsdp", "seq")),
        P(None, ("fsdp", "seq")),
        P(None, ("fsdp", "seq"), "tp"),
        P(None, "tp"),
        P(None, "tp", ("fsdp", "seq")),
        P(None, ("fsdp", "seq")),
        P(None, None, ("fsdp", "seq")),
        P(None, None, ("fsdp", "seq")),
    )
    return jax.shard_map(
        body,
        mesh=mesh,
        in_specs=placed,
        out_specs=(
            P("fsdp", "seq", None),
            P("fsdp", "seq", None),
            P(None, None, ("fsdp", "seq"), "tp"),
            P(None, None, "tp"),
            P(None, "tp", ("fsdp", "seq")),
            P(None, ("fsdp", "seq")),
            P(None, ("fsdp", "seq"), "tp"),
            P(None, "tp"),
            P(None, "tp", ("fsdp", "seq")),
            P(None, ("fsdp", "seq")),
            P(None, None, ("fsdp", "seq")),
            P(None, None, ("fsdp", "seq")),
        ),
        check_vma=False,
    )
```

time: 380 us -> 249 us (0.66)
  Pallas kernels: 354 us -> 224 us
    pallas_call x1, Pallas kernels: 354 us -> 224 us  [body(): pl.pallas_call(kernel, name='encoder', out_shape=(jax.ShapeDtypeStruct(bl...]
where the time goes in v2:
time: 249 us
  Pallas kernels  224 us (90%)
  local copies, waits for them, and re-layouts  13 us (5%)
  other arithmetic  10.9 us (4%)
    pallas_call x1, Pallas kernels, body(): pl.pallas_call(kernel, name='encoder', out_shape=(jax.ShapeDtypeStruct(bl...  224 us

profile of v2, /device:TPU:0, one launch (start us, length us, event | category | flops | bytes accessed | tf_op | source)
XLA Modules:
  0.0 248.6 jit_solution(5708703490880364333)
XLA Ops:
  0.7 0.8 broadcast_compare_fusion
  1.5 0.7 copy.37
  2.2 0.7 copy.38
  2.8 0.1 pad.13.clone
  2.9 0.1 pad.15.clone
  3.0 0.7 fusion.7
  3.7 1.3 compare_convert_fusion.live_ref
  5.0 0.7 copy_convert_fusion
  5.7 0.1 maximum_maximum_fusion
  5.8 0.6 reshape.129.bqkv_ref
  6.4 1.3 reshape.135.bup_ref
  7.6 0.1 dynamic_update_slice.3.vec_ref
  7.8 0.0 copy-start.3
  7.8 1.0 copy.36
  8.7 1.0 slice_bitcast_fusion.9
  9.7 0.2 maximum_bitcast_fusion
  9.9 1.9 pad_maximum_fusion.wown_ref
  11.8 1.1 broadcast_select_fusion
  12.9 223.9 %encoder.1 = (bf16[3,4,2,16,1280]{4,3,2,1,0:T(8,128)(2,1)}, bf16[3,4,2,16,1280]{4,3,2,1,0:T(8,128)(2,1)}, f32[2,3,80,640]{3,2,1,0:T(8,128)}, f32[2,16,128]{2,1,0:T(8,128)}, f32[8,640]{1,0:T(8,128)}) custom-call(bf16[3,4,2,16,1280]{4,3,2,1,0:T(8,128)(2,1)} %bitcast.66, bf16[3,4,2,16,1280]{4,3,2,1,0:T(8,128)(2,1)} %bitcast.65, ...), custom_call_target="tpu_custom_call" | custom-call | tf_op jit(solution)/shard_map/encoder/pallas_call | solution.py:636
  236.9 0.9 slice_bitcast_fusion.13
  237.8 1.3 slice.81
  239.1 0.6 copy.42
  239.7 0.7 copy_bitcast_fusion
  240.4 0.1 dynamic-slice_bitcast_fusion
  240.5 0.6 fusion.9
  241.1 0.6 fusion.8
  241.6 2.6 %bitcast_convert_fusion.1 = f32[3,128,1280]{2,1,0:T(8,128)} fusion(bf16[3,4,2,16,1280]{4,3,2,1,0:T(8,128)(2,1)} %get-tuple-element.17), kind=kLoop, calls=%fused_computation.1 | loop fusion | flops 491520 | bytes 2949120 | tf_op jit(solution)/shard_map/convert_element_type | solution.py:654
  244.3 1.0 slice_bitcast_fusion
  245.2 0.2 slice_bitcast_fusion.3
  245.4 0.8 copy.43
  246.3 0.8 copy.41
  247.1 1.5 bitcast_convert_fusion
  (15 shorter events, 0.1 us)
Async XLA Ops:
  0.6 11.2 %copy-start.1 = (bf16[3,128,1280]{2,1,0:T(8,128)(2,1)S(1)}, bf16[3,128,1280]{2,1,0:T(8,128)(2,1)}, u32[]{:S(2)}) copy-start(bf16[3,128,1280]{2,1,0:T(8,128)(2,1)} %param.14) | copy-start | bytes 2949124
  7.8 5.2 %copy-start.3 = (bf16[16,256]{1,0:T(8,128)(2,1)}, bf16[16,256]{1,0:T(8,128)(2,1)S(1)}, u32[]{:S(2)}) copy-start(bf16[16,256]{1,0:T(8,128)(2,1)S(1)} %dynamic_update_slice.3.vec_ref) | copy-start | bytes 24580
  236.9 7.4 %copy-start = (f32[2,3,80,640]{3,2,1,0:T(8,128)S(1)}, f32[2,3,80,640]{3,2,1,0:T(8,128)}, u32[]{:S(2)}) copy-start(f32[2,3,80,640]{3,2,1,0:T(8,128)} %get-tuple-element.19) | copy-start | bytes 3686404
  245.2 1.9 copy-start.2

commit v3 on v2

--- a/solution.py
+++ b/solution.py
@@ -22,7 +22,6 @@
 PART = 640
 SHARDS = 16
 SHARD = 80
-WIDTH = 160
 
 PIECES = (
     (0, (256, 512), (0, 256)),
@@ -31,6 +30,17 @@
     (2, (384, 640), (0, 384)),
 )
 QKV, OUT, UP, DOWN = range(4)
+LOADS = (
+    (0, 0, (256, 512), (0, 256)),
+    (0, 0, (512, 640), None),
+    (0, 1, None, (0, 640)),
+    (0, 2, (0, 256), None),
+    (0, 2, None, (256, 640)),
+    (1, 0, (384, 640), (0, 384)),
+    (1, 1, (384, 640), (0, 384)),
+    (1, 2, (384, 640), (0, 384)),
+)
+QKV0, OUT0, UP0, DOWN0X, DOWN0Z, PROJ1, UP1, DOWN1 = range(8)
 
 
 def dot_nn(a, b):
@@ -68,13 +78,14 @@
 
 
 def kernel(
-    hid_ref, cot_ref, wown_ref, vec_ref, bqkv_ref, bup_ref, live_ref,
-    out_ref, ingrad_ref, dwo_ref, vout_ref, bout_ref,
+    hid_ref, cot_ref, len_ref, wqkv_ref, bqv_ref, wout_ref, bout_ref, wup_ref, bup_ref, wdown_ref, bdown_ref,
+    gain_ref, shift_ref,
+    out_ref, ingrad_ref, dwo_ref, vsum_ref, bsum_ref,
     W, dW, rb1, rb2, rc, FB, BB, dr, yr, part, sb,
     qkv, kvo, prob, att, xrow, midrow, slope, act,
     gpre, gkeep, gproj, gks, gkr, gyrow, gmidrow,
-    VG, V, GV, GT, vr, vr2, gb, br,
-    g1s, g1r, g2s, g2r, q1s, q1r, q2s, q2r,
+    VG, V, GV, GT, vr, vr2, gb, br, vrow, bqkv,
+    g1s, g1r, g2s, g2r, g3s, g3r, q1s, q1r, q2s, q2r,
     s1, r1, s2, r2, s3, r3, s4, r4, ks, kr, gs_s, gs_r, vs, vrs, es, er, lsem,
 ):
     f, s, t = lax.axis_index("fsdp"), lax.axis_index("seq"), lax.axis_index("tp")
@@ -126,44 +137,105 @@
     def _(k):
         pl.semaphore_signal(barrier, inc=1, device_id=(f, s, (t + k) % 8), device_id_type=MESH)
 
+    def pack(l, p):
+        if p == 0:
+            parts = [wqkv_ref[l, i].astype(F32) for i in range(3)] + [wout_ref[l].astype(F32).T]
+            W[l, 0, xh, z, s] = jnp.concatenate(parts, axis=1).astype(BF)
+        elif p == 1:
+            W[l, 1, xh, z, s] = wup_ref[l]
+        else:
+            W[l, 2, xh, z, s] = wdown_ref[l].astype(F32).T.astype(BF)
+
+    vrow[...] = jnp.zeros_like(vrow)
+    for l in range(2):
+        for r in range(2):
+            vrow[8 * l + r : 8 * l + r + 1, 0:SHARD] = gain_ref[l, r : r + 1, :].astype(F32)
+            vrow[8 * l + 2 + r : 8 * l + 3 + r, 0:SHARD] = shift_ref[l, r : r + 1, :].astype(F32)
+        vrow[8 * l + 4 : 8 * l + 5, 0:SHARD] = bout_ref[l : l + 1, :].astype(F32)
+        vrow[8 * l + 5 : 8 * l + 6, 0:SHARD] = bdown_ref[l : l + 1, :].astype(F32)
+    VG[me] = pltpu.roll(vrow[...], (SHARD * me) % 128, 1).astype(BF)
+    pack(0, 0)
     pl.semaphore_wait(barrier, 22)
+
+    def load(n):
+        l, p, one, two = LOADS[n]
+        ways = ([(0, slice(*one))] if one else []) + ([(1, slice(*two))] if two else [])
+        return l, p, ways
+
+    def gather_one(n):
+        l, p, ways = load(n)
+        for way, cols in ways:
+            own = W.at[l, p, xh, z, s, :, cols]
+            for k in range(1, 4):
+                dev = x_dev(k)[2] if way else z_dev(k)[1]
+                remote(own, own, g1s.at[n, way], g1r.at[n, way], dev).start()
+
+    def gather_mid(n):
+        l, p, ways = load(n)
+        for way, cols in ways:
+            three = W.at[l, p, 0, pl.ds(0, 3), 0, :, cols]
+            wait_bytes(three, g1r.at[n, way])
+            wait_bytes(three, g1s.at[n, way])
+
+    def gather_two(n):
+        l, p, ways = load(n)
+        gather_mid(n)
+        for way, cols in ways:
+            four = W.at[l, p, :, z, :, :, cols] if way else W.at[l, p, xh, :, s, :, cols]
+            for k in range(1, 4):
+                dev = z_dev(k)[1] if way else x_dev(k)[2]
+                remote(four, four, g2s.at[n, way], g2r.at[n, way], dev).start()
+
+    def gather_wait(n):
+        l, p, ways = load(n)
+        for way, cols in ways:
+            twelve = W.at[l, p, :, pl.ds(0, 3), :, :, cols]
+            wait_bytes(twelve, g2r.at[n, way])
+            wait_bytes(twelve, g2s.at[n, way])
+
+    def ring_dev(way, k):
+        return z_dev(k)[1] if way else x_dev(k)[2]
+
+    def ring_two(n):
+        l, p, ways = load(n)
+        gather_mid(n)
+        for way, cols in ways:
+            four = W.at[l, p, :, z, :, :, cols] if way else W.at[l, p, xh, :, s, :, cols]
+            for k in (1, 3):
+                remote(four, four, g2s.at[n, way], g2r.at[n, way], ring_dev(way, k)).start()
+
+    def ring_mid(n):
+        l, p, ways = load(n)
+        for way, cols in ways:
+            eight = W.at[l, p, 0, :, :, :, cols]
+            wait_bytes(eight, g2r.at[n, way])
+            wait_bytes(eight, g2s.at[n, way])
+
+    def ring_three(n):
+        l, p, ways = load(n)
+        ring_mid(n)
+        for way, cols in ways:
+            if way:
+                left = W.at[l, p, 0, (z + 3) % 4, :, :, cols]
+                right = W.at[l, p, 1, (z + 1) % 4, :, :, cols]
+            else:
+                il, ir = (x + 3) % 4, (x + 1) % 4
+                left = W.at[l, p, il // 2, pl.ds(0, 2), il % 2, :, cols]
+                right = W.at[l, p, ir // 2, pl.ds(2, 2), ir % 2, :, cols]
+            remote(left, left, g3s.at[n, way], g3r.at[n, way], ring_dev(way, 1)).start()
+            remote(right, right, g3s.at[n, way], g3r.at[n, way], ring_dev(way, 3)).start()
+
+    def ring_wait(n):
+        l, p, ways = load(n)
+        for way, cols in ways:
+            four = W.at[l, p, 0, pl.ds(0, 2), :, :, cols]
+            wait_bytes(four, g3r.at[n, way])
+            wait_bytes(four, g3s.at[n, way])
 
     def piece(l, i):
         part_idx, one, two = PIECES[i]
         both = [(0, slice(*one))] + ([(1, slice(*two))] if two else [])
         return part_idx, both
-
-    def gather_one(l, i):
-        p, ways = piece(l, i)
-        for way, cols in ways:
-            W[l, p, xh, z, s, :, cols] = wown_ref[l, p, :, cols]
-            own = W.at[l, p, xh, z, s, :, cols]
-            for k in range(1, 4):
-                dev = x_dev(k)[2] if way else z_dev(k)[1]
-                remote(own, own, g1s.at[l, i, way], g1r.at[l, i, way], dev).start()
-
-    def gather_mid(l, i):
-        p, ways = piece(l, i)
-        for way, cols in ways:
-            three = W.at[l, p, 0, pl.ds(0, 3), 0, :, cols]
-            wait_bytes(three, g1r.at[l, i, way])
-            wait_bytes(three, g1s.at[l, i, way])
-
-    def gather_two(l, i):
-        p, ways = piece(l, i)
-        gather_mid(l, i)
-        for way, cols in ways:
-            four = W.at[l, p, :, z, :, :, cols] if way else W.at[l, p, xh, :, s, :, cols]
-            for k in range(1, 4):
-                dev = z_dev(k)[1] if way else x_dev(k)[2]
-                remote(four, four, g2s.at[l, i, way], g2r.at[l, i, way], dev).start()
-
-    def gather_wait(l, i):
-        p, ways = piece(l, i)
-        for way, cols in ways:
-            twelve = W.at[l, p, :, pl.ds(0, 3), :, :, cols]
-            wait_bytes(twelve, g2r.at[l, i, way])
-            wait_bytes(twelve, g2s.at[l, i, way])
 
     def reduce_one(l, i):
         p, ways = piece(l, i)
@@ -279,7 +351,7 @@
 
     def project(l, c):
         normed = FB[2 * l, c].reshape(ROWS, D)
-        proj = dot_nn(normed, W[l, 0, :, :, :, :, 0:512].reshape(D, 512)) + bqkv_ref[l]
+        proj = dot_nn(normed, W[l, 0, :, :, :, :, 0:512].reshape(D, 512)) + bqkv[l]
         qkv[l, c] = proj.astype(BF)
         remote(qkv.at[l, c, :, 128:512], kvo.at[l, c], ks.at[l, c], kr.at[l, c], seq_dev).start()
 
@@ -288,7 +360,9 @@
         wait_bytes(kvo.at[l, c], ks.at[l, c])
         q2, k, v = heads_of(l, c)
         scores = dot_nt(q2, k.astype(BF)) * SCALING
-        scores = jnp.where(live_ref[c] > 0.0, scores, MASKED)
+        slot = lax.broadcasted_iota(jnp.int32, (1, 2 * ROWS), 1)
+        slot = jnp.where(slot < ROWS, slot + s * ROWS, slot - s * ROWS)
+        scores = jnp.where(slot < len_ref[c], scores, MASKED)
         top = jnp.max(scores, axis=-1, keepdims=True)
         powers = jnp.exp(scores - top)
         probs = powers / jnp.sum(powers, axis=-1, keepdims=True)
@@ -310,11 +384,16 @@
 
     def feed(l, c):
         normed = FB[2 * l + 1, c].reshape(ROWS, D)
-        pre = dot_nn(normed, W[l, 1].reshape(D, PART)) + bup_ref[l]
+        pre = dot_nn(normed, W[l, 1].reshape(D, PART)) + bup_ref[l : l + 1, :].astype(F32)
         cdf = 0.5 * (1.0 + lax.erf(pre * math.sqrt(0.5)))
         activated = (pre * cdf).astype(BF)
         act[l, c] = activated
         slope[l, c] = cdf + pre * jnp.exp(-0.5 * pre * pre) * (1.0 / math.sqrt(2.0 * math.pi))
+        if c == 0 and l == 0:
+            ring_wait(DOWN0X)
+            ring_wait(DOWN0Z)
+        elif c == 0:
+            ring_wait(DOWN1)
         rs_start(2 * l + 1, c, dot_nt(activated, W[l, 2].reshape(D, PART)))
 
     def feed_rows(l, c):
@@ -411,16 +490,20 @@
 
     @pl.loop(1, SHARDS)
     def _(k):
-        remote(vec_ref, VG.at[me], vs.at[0], vrs.at[0], shard_dev(k)[1]).start()
-
-    VG[me] = vec_ref[...]
-    gather_one(0, QKV)
+        remote(VG.at[me], VG.at[me], vs.at[0], vrs.at[0], shard_dev(k)[1]).start()
+
+    gather_one(QKV0)
+    gather_one(OUT0)
+    pack(0, 1)
+    pack(0, 2)
     V[...] = jnp.zeros_like(V)
     GV[...] = jnp.zeros_like(GV)
     gb[...] = jnp.zeros_like(gb)
-    gather_two(0, QKV)
-    gather_one(0, OUT)
-    gather_one(0, UP)
+    bqkv[...] = jnp.zeros_like(bqkv)
+    for l in range(2):
+        bqkv[l, :, 0:160] = bqv_ref[l, 0:1, :].astype(F32)
+        bqkv[l, :, 320:480] = bqv_ref[l, 1:2, :].astype(F32)
+    gather_two(QKV0)
     wait_bytes(VG.at[pl.ds(0, SHARDS - 1)], vrs.at[0])
     wait_bytes(VG.at[pl.ds(0, SHARDS - 1)], vs.at[0])
     for i in range(SHARDS):
@@ -435,11 +518,23 @@
         unit, _ = norm_parts(whole)
         xrow[0, c] = FB[0, c, y, core].astype(F32)
         FB[0, c] = (unit * vec(0, 0) + vec(0, 2)).astype(BF).reshape(4, 2, 16, D)
-        gyrow[c] = BB[0, c, y, core].astype(F32)
-    gather_two(0, OUT)
-    gather_wait(0, QKV)
-    gather_two(0, UP)
-    gather_one(0, DOWN)
+        if c == 0:
+            gather_one(UP0)
+            gather_one(DOWN0X)
+    gather_two(OUT0)
+    gather_wait(QKV0)
+
+    def mask_grads():
+        row = lax.broadcasted_iota(jnp.int32, (ROWS, 1), 0) + s * ROWS
+        for c in range(MICRO):
+            masked = jnp.where(row < len_ref[c], BB[0, c].reshape(ROWS, D).astype(F32), 0.0)
+            BB[0, c] = masked.astype(BF).reshape(4, 2, 16, D)
+            gyrow[c] = BB[0, c, y, core].astype(F32)
+
+    def bias_sums():
+        @pl.loop(1, SHARDS)
+        def _(k):
+            remote(gb, br.at[k - 1], es.at[1], er.at[1], shard_dev(k)[1]).start()
 
     cp_o = pltpu.make_async_copy(FB.at[4], out_ref, lsem.at[0])
     cp_g = pltpu.make_async_copy(BB.at[4], ingrad_ref, lsem.at[1])
@@ -466,47 +561,48 @@
             steps.append((partial(project_back, l, c), (a1, c)))
             sums[a1, c] = (partial(project_back_rows, l, c), BB, 4 - 2 * l)
 
-    g1, g2, g3 = gather_one, gather_two, gather_wait
+    g1, g2, g3, g4 = gather_one, ring_two, ring_three, ring_wait
     d1, d2 = reduce_one, reduce_two
     before = {
-        3: [(g3, 0, OUT)],
-        6: [(g3, 0, UP), (g3, 0, DOWN)],
-        9: [(g3, 1, QKV)],
-        12: [(g3, 1, OUT)],
-        15: [(g3, 1, UP), (g3, 1, DOWN)],
+        0: [(g2, UP0), (g1, DOWN0Z)],
+        2: [(g2, DOWN0X)],
+        3: [(gather_wait, OUT0), (g2, DOWN0Z)],
+        4: [(g3, UP0), (g1, PROJ1)],
+        5: [(g3, DOWN0X), (g3, DOWN0Z), (g2, PROJ1)],
+        6: [(g4, UP0), (g1, UP1)],
+        7: [(g3, PROJ1), (g2, UP1), (g1, DOWN1)],
+        9: [(g4, PROJ1), (g3, UP1), (g2, DOWN1)],
+        12: [(g3, DOWN1)],
+        15: [(g4, UP1)],
     }
     between = {
-        3: [(g2, 0, DOWN), (g1, 1, QKV), (g1, 1, OUT)],
-        5: [(g2, 1, QKV), (g2, 1, OUT), (g1, 1, UP)],
-        8: [(g2, 1, UP), (g1, 1, DOWN)],
-        11: [(g2, 1, DOWN)],
-        18: [(down_grad, 1, 0)],
-        19: [(down_grad, 1, 1), (d1, 1, DOWN)],
-        21: [(up_grad, 1, 0)],
-        22: [(up_grad, 1, 1), (d1, 1, UP)],
-        23: [(d2, 1, DOWN)],
-        24: [(out_grad, 1, 0)],
-        25: [(out_grad, 1, 1), (d1, 1, OUT)],
-        26: [(d2, 1, UP)],
-        27: [(qkv_grad, 1, 0)],
-        28: [(qkv_grad, 1, 1), (d1, 1, QKV)],
-        29: [(down_grad, 0, 0), (d2, 1, OUT)],
-        30: [(down_grad, 0, 1), (d1, 0, DOWN)],
-        31: [(up_grad, 0, 0)],
-        32: [(up_grad, 0, 1), (d1, 0, UP)],
-        33: [(out_grad, 0, 0), (d2, 1, QKV)],
-        34: [(out_grad, 0, 1), (d1, 0, OUT)],
-        35: [(d2, 0, DOWN)],
-        36: [(qkv_grad, 0, 0), (qkv_grad, 0, 1), (d1, 0, QKV)],
-        37: [(d2, 0, UP)],
+        3: [(pack, 1, 0)],
+        4: [(pack, 1, 1)],
+        5: [(pack, 1, 2)],
+        6: [(mask_grads,)],
+        18: [(down_grad, 1, 0), (down_grad, 1, 1), (d1, 1, DOWN)],
+        21: [(up_grad, 1, 0), (up_grad, 1, 1), (d1, 1, UP)],
+        23: [(out_grad, 1, 0), (out_grad, 1, 1), (d1, 1, OUT)],
+        24: [(d2, 1, DOWN)],
+        25: [(d2, 1, UP)],
+        26: [(qkv_grad, 1, 0), (qkv_grad, 1, 1), (d1, 1, QKV)],
+        27: [(d2, 1, OUT)],
+        29: [(down_grad, 0, 0), (down_grad, 0, 1), (d1, 0, DOWN)],
+        30: [(up_grad, 0, 0), (up_grad, 0, 1), (d1, 0, UP)],
+        31: [(d2, 1, QKV)],
+        32: [(out_grad, 0, 0), (out_grad, 0, 1), (d1, 0, OUT)],
+        33: [(d2, 0, DOWN)],
+        34: [(d2, 0, UP)],
+        35: [(qkv_grad, 0, 0), (qkv_grad, 0, 1), (d1, 0, QKV), (bias_sums,)],
+        36: [(d2, 0, OUT)],
     }
     for n in range(len(steps) + 2):
-        for fn, l, i in before.get(n, ()):
-            fn(l, i)
+        for fn, *where in before.get(n, ()):
+            fn(*where)
         if n < len(steps):
             steps[n][0]()
-        for fn, l, i in between.get(n, ()):
-            fn(l, i)
+        for fn, *where in between.get(n, ()):
+            fn(*where)
         if n < len(steps) and steps[n][1] is not None:
             rs_mid(*steps[n][1])
         if 1 <= n <= len(steps) and steps[n - 1][1] is not None:
@@ -526,7 +622,6 @@
     def _(k):
         j, dev = shard_dev(k)
         remote(GT.at[pl.ds(SHARD * j // 128, 2)], vr.at[k - 1], es.at[0], er.at[0], dev).start()
-        remote(gb, br.at[k - 1], es.at[1], er.at[1], dev).start()
 
     cp_g.start()
     wait_bytes(vr, er.at[0])
@@ -540,14 +635,13 @@
     def _(k):
         remote(vr2.at[7], vr2.at[k - 1], es.at[2], er.at[2], (f, s, (t + k) % 8)).start()
 
-    reduce_two(0, OUT)
     reduce_two(0, QKV)
     wait_bytes(br, er.at[1])
     wait_bytes(br, es.at[1])
     totals = gb[...]
     for k in range(SHARDS - 1):
         totals = totals + br[k]
-    bout_ref[...] = totals
+    bsum_ref[...] = totals
     for l, i in ((1, DOWN), (1, UP), (1, OUT), (1, QKV), (0, DOWN), (0, UP), (0, OUT)):
         reduce_three(l, i)
     wait_bytes(vr2.at[pl.ds(0, 7)], er.at[2])
@@ -555,40 +649,45 @@
     own = vr2[7]
     for k in range(7):
         own = own + vr2[k]
-    vout_ref[...] = own
+    vsum_ref[...] = own
     reduce_three(0, QKV)
     cp_o.wait()
     cp_g.wait()
+
+
+def finish(
+    out_ref, ingrad_ref, dwo_ref, vsum_ref, bsum_ref,
+    hidden_ref, grad_ref, gqkv_ref, gqv_ref, gout_ref, gbout_ref, gup_ref, gbup_ref, gdown_ref, gbdown_ref,
+    ggain_ref, gshift_ref,
+):
+    me = lax.axis_index("fsdp") * 2 + lax.axis_index("seq")
+    hidden_ref[...] = out_ref[...].astype(F32)
+    grad_ref[...] = ingrad_ref[...].astype(F32)
+    rows = jnp.concatenate([vsum_ref[0], vsum_ref[1]], axis=1)
+    rows = pltpu.roll(rows, (256 - (SHARD * me) % 128) % 256, 1)
+    for l in range(2):
+        proj = dwo_ref[l, 0]
+        for i in range(3):
+            gqkv_ref[l, i] = proj[:, 160 * i : 160 * i + 160]
+        gout_ref[l] = proj[:, 480:640].T
+        gup_ref[l] = dwo_ref[l, 1]
+        gdown_ref[l] = dwo_ref[l, 2].T
+        gqv_ref[l, 0:1, :] = bsum_ref[l : l + 1, 0:160]
+        gqv_ref[l, 1:2, :] = bsum_ref[l : l + 1, 320:480]
+        gbup_ref[l : l + 1, :] = bsum_ref[2 + l : 3 + l, :]
+        ggain_ref[l] = rows[8 * l : 8 * l + 2, 0:SHARD]
+        gshift_ref[l] = rows[8 * l + 2 : 8 * l + 4, 0:SHARD]
+        gbout_ref[l : l + 1, :] = rows[8 * l + 4 : 8 * l + 5, 0:SHARD]
+        gbdown_ref[l : l + 1, :] = rows[8 * l + 5 : 8 * l + 6, 0:SHARD]
 
 
 def body(
     hidden_in, cotangent, lengths, qkv_weight, qv_bias, out_weight, out_bias,
     up_weight, up_bias, down_weight, down_bias, ln_gain, ln_bias,
 ):
-    seq = lax.axis_index("seq")
-    me = lax.axis_index("fsdp") * 2 + seq
-    own_pos = seq * ROWS + jnp.arange(ROWS)
-    far_pos = (1 - seq) * ROWS + jnp.arange(ROWS)
-    keys = jnp.concatenate([own_pos, far_pos])
-    live = (keys[None, :] < lengths[:, None]).astype(F32).reshape(MICRO, 1, 2 * ROWS)
-    cot = jnp.where((own_pos[None, :] < lengths[:, None])[..., None], cotangent, jnp.zeros((), BF))
-    first = jnp.concatenate(
-        [qkv_weight[:, 0], qkv_weight[:, 1], qkv_weight[:, 2], jnp.swapaxes(out_weight, 1, 2)], axis=2
-    )
-    wown = jnp.stack([first, up_weight, jnp.swapaxes(down_weight, 1, 2)], axis=1)
-    vectors = jnp.stack(
-        [ln_gain[:, 0], ln_gain[:, 1], ln_bias[:, 0], ln_bias[:, 1], out_bias, down_bias], axis=1
-    )
-    vectors = jnp.pad(vectors, ((0, 0), (0, 2), (0, 0))).reshape(16, SHARD)
-    offset = lax.rem(SHARD * me, 128)
-    vectors = lax.dynamic_update_slice(jnp.zeros((16, 256), BF), vectors, (0, offset))
-    zero = jnp.zeros((2, WIDTH), F32)
-    qv = qv_bias.astype(F32)
-    bqkv = jnp.concatenate([qv[:, 0], zero, qv[:, 1], zero[:, 0:32]], axis=1).reshape(2, 1, 512)
-    bup = up_bias.astype(F32).reshape(2, 1, PART)
-
     vmem = pl.BlockSpec(memory_space=pltpu.VMEM)
     anys = pl.BlockSpec(memory_space=pl.ANY)
+    smem = pl.BlockSpec(memory_space=pltpu.SMEM)
     dma = pltpu.SemaphoreType.DMA
     blocks = (MICRO, 4, 2, 16, D)
     scratch = [
@@ -626,14 +725,16 @@
         pltpu.VMEM((8, 2, 16, 128), F32),
         pltpu.VMEM((8, PART), F32),
         pltpu.VMEM((SHARDS - 1, 8, PART), F32),
-        dma((2, 4, 2)), dma((2, 4, 2)), dma((2, 4, 2)), dma((2, 4, 2)),
+        pltpu.VMEM((16, 256), F32),
+        pltpu.VMEM((2, 1, 512), F32),
+        dma((8, 2)), dma((8, 2)), dma((8, 2)), dma((8, 2)), dma((8, 2)), dma((8, 2)),
         dma((2, 4, 2)), dma((2, 4, 2)), dma((2, 4, 2)), dma((2, 4, 2)),
         dma((MICRO,)), dma((8, MICRO)), dma((MICRO,)), dma((8, MICRO)),
         dma((MICRO,)), dma((8, MICRO)), dma((MICRO,)), dma((8, MICRO)),
         dma((2, MICRO)), dma((2, MICRO)), dma((MICRO,)), dma((2, MICRO)),
         dma((1,)), dma((1,)), dma((3,)), dma((3,)), dma((2,)),
     ]
-    out, ingrad, dwo, vout, bout = pl.pallas_call(
+    out, ingrad, dwo, vsum, bsum = pl.pallas_call(
         kernel,
         name="encoder",
         out_shape=(
@@ -643,30 +744,29 @@
             jax.ShapeDtypeStruct((2, 16, 128), F32),
             jax.ShapeDtypeStruct((8, PART), F32),
         ),
-        in_specs=[anys, anys, vmem, vmem, vmem, vmem, vmem],
+        in_specs=[anys, anys, smem] + [vmem] * 10,
         out_specs=(anys, anys, vmem, vmem, vmem),
         scratch_shapes=scratch,
         compiler_params=pltpu.CompilerParams(
             collective_id=0, has_side_effects=True, vmem_limit_bytes=63 * 1024 * 1024
         ),
-    )(hidden_in.reshape(blocks), cot.reshape(blocks), wown, vectors, bqkv, bup, live)
-
-    out_hidden = out.reshape(MICRO, ROWS, D).astype(F32)
-    in_grad = ingrad.reshape(MICRO, ROWS, D).astype(F32)
-    first = dwo[:, 0]
-    qkv_grad = jnp.stack([first[:, :, 0:160], first[:, :, 160:320], first[:, :, 320:480]], axis=1)
-    out_grad = jnp.swapaxes(first[:, :, 480:640], 1, 2)
-    up_grad = dwo[:, 1]
-    down_grad = jnp.swapaxes(dwo[:, 2], 1, 2)
-    rows = jnp.swapaxes(vout, 0, 1).reshape(16, 256)
-    rows = lax.dynamic_slice(rows, (0, offset), (16, SHARD)).reshape(2, 8, SHARD)
-    gain_grad = rows[:, 0:2]
-    shift_grad = rows[:, 2:4]
-    qv_grad = jnp.stack([bout[0:2, 0:160], bout[0:2, 320:480]], axis=1)
-    return (
-        out_hidden, in_grad, qkv_grad, qv_grad, out_grad, rows[:, 4], up_grad,
-        bout[2:4], down_grad, rows[:, 5], gain_grad, shift_grad,
+    )(
+        hidden_in.reshape(blocks), cotangent.reshape(blocks), lengths, qkv_weight, qv_bias, out_weight,
+        out_bias, up_weight, up_bias, down_weight, down_bias, ln_gain, ln_bias,
     )
+    rows = (MICRO, ROWS, D)
+    shapes = (
+        rows, rows, (2, 3, SHARD, 160), (2, 2, 160), (2, 160, SHARD), (2, SHARD), (2, SHARD, PART),
+        (2, PART), (2, PART, SHARD), (2, SHARD), (2, 2, SHARD), (2, 2, SHARD),
+    )
+    return pl.pallas_call(
+        finish,
+        name="finish",
+        out_shape=tuple(jax.ShapeDtypeStruct(shape, F32) for shape in shapes),
+        in_specs=[vmem] * 5,
+        out_specs=(vmem,) * 12,
+        compiler_params=pltpu.CompilerParams(vmem_limit_bytes=32 * 1024 * 1024),
+    )(out.reshape(rows), ingrad.reshape(rows), dwo, vsum, bsum)
 
 
 def solution(mesh):

time: 249 us -> 230 us (0.924)
  other arithmetic: 10.9 us -> 0 us
  local copies, waits for them, and re-layouts: 13 us -> 7.93 us
  Pallas kernels: 224 us -> 221 us
    convert_element_type x4 -> x0, other arithmetic: 6.1 us -> none  [the longest x1 2.62 us: body(): out_hidden = out.reshape(MICRO, ROWS, D).astype(F32)]
    pallas_call x1, Pallas kernels: 224 us -> 218 us  [body(): pl.pallas_call(kernel, name='encoder', out_shape=(jax.ShapeDtypeStruct(bl...]
    unnamed x12 -> x11, local copies, waits for them, and re-layouts: 3.21 us -> 6.96 us
    pallas_call x0 -> x1, Pallas kernels: none -> 2.8 us  [body(): pl.pallas_call(finish, name='finish', out_shape=tuple((jax.ShapeDtypeStru...]
    reshape x4 -> x0, local copies, waits for them, and re-layouts: 2.67 us -> none  [the longest x1 1.28 us: body(): bup = up_bias.astype(F32).reshape(2, 1, PART)]
where the time goes in v3:
time: 230 us; the launch traced here: 229 us
  Pallas kernels  221 us (96%)
  local copies, waits for them, and re-layouts  7.93 us (3%)
    pallas_call x1, Pallas kernels, body(): pl.pallas_call(kernel, name='encoder', out_shape=(jax.ShapeDtypeStruct(bl...  218 us
    unnamed x11, local copies, waits for them, and re-layouts  6.96 us

profile of v3, /device:TPU:0, one launch (start us, length us, event | category | flops | bytes accessed | tf_op | source)
XLA Modules:
  0.0 229.5 jit_solution(9694847307071712668)
XLA Ops:
  0.6 1.8 copy.25.wdown_ref
  2.5 218.1 %encoder.1 = (bf16[3,4,2,16,1280]{4,3,2,1,0:T(8,128)(2,1)}, bf16[3,4,2,16,1280]{4,3,2,1,0:T(8,128)(2,1)}, f32[2,3,80,640]{3,2,1,0:T(8,128)}, f32[2,16,128]{2,1,0:T(8,128)}, f32[8,640]{1,0:T(8,128)}) custom-call(bf16[3,4,2,16,1280]{4,3,2,1,0:T(8,128)(2,1)} %bitcast.6, bf16[3,4,2,16,1280]{4,3,2,1,0:T(8,128)(2,1)} %bitcast.7, s32[3]{0:T(128)} %len_ref.1, ...), custom_call_target="tpu_custom_call" | custom-call | tf_op jit(solution)/shard_map/encoder/pallas_call | solution.py:737
  220.5 0.0 copy-start
  220.6 1.3 copy-done
  221.8 0.0 copy-start.1
  221.8 1.2 copy-done.1
  223.0 0.0 copy-start.2
  223.0 1.2 copy-done.2
  224.2 0.0 copy-start.3
  224.2 0.7 copy-done.3
  225.0 0.0 copy-start.4
  225.0 0.7 copy-done.4
  225.7 2.8 %finish.1 = (f32[3,128,1280]{2,1,0:T(8,128)}, f32[3,128,1280]{2,1,0:T(8,128)}, f32[2,3,80,160]{3,2,1,0:T(8,128)}, f32[2,2,160]{2,1,0:T(2,128)}, f32[2,160,80]{2,...) custom-call(bf16[3,128,1280]{2,1,0:T(8,128)(2,1)S(1)} %bitcast.4, ...), custom_call_target="tpu_custom_call" | custom-call | tf_op jit(solution)/shard_map/finish/pallas_call | solution.py:762
  228.5 1.0 copy.26
Async XLA Ops:
  220.5 1.3 copy-start
  221.8 1.2 copy-start.1
  223.0 1.2 copy-start.2
  224.2 0.7 copy-start.3
  225.0 0.7 copy-start.4

commit v4 on v3

--- a/solution.py
+++ b/solution.py
@@ -84,9 +84,9 @@
     W, dW, rb1, rb2, rc, FB, BB, dr, yr, part, sb,
     qkv, kvo, prob, att, xrow, midrow, slope, act,
     gpre, gkeep, gproj, gks, gkr, gyrow, gmidrow,
-    VG, V, GV, GT, vr, vr2, gb, br, vrow, bqkv,
+    VG, V, GV, GT, vr, vr2, gb, br, gq, bq, vrow, bqkv, dwo,
     g1s, g1r, g2s, g2r, g3s, g3r, q1s, q1r, q2s, q2r,
-    s1, r1, s2, r2, s3, r3, s4, r4, ks, kr, gs_s, gs_r, vs, vrs, es, er, lsem,
+    s1, r1, s2, r2, s3, r3, s4, r4, ks, kr, gs_s, gs_r, vs, vrs, es, er, lsem, wsem, osem,
 ):
     f, s, t = lax.axis_index("fsdp"), lax.axis_index("seq"), lax.axis_index("tp")
     me = f * 2 + s
@@ -127,6 +127,10 @@
     cp_h.start()
     cp_c.start()
 
+    for l in range(2):
+        for p in range(2):
+            pltpu.make_async_copy((wup_ref, wdown_ref)[p].at[l], W.at[l, p + 1, xh, z, s], wsem.at[l, p]).start()
+
     barrier = pltpu.get_barrier_semaphore()
 
     @pl.loop(1, SHARDS)
@@ -141,10 +145,8 @@
         if p == 0:
             parts = [wqkv_ref[l, i].astype(F32) for i in range(3)] + [wout_ref[l].astype(F32).T]
             W[l, 0, xh, z, s] = jnp.concatenate(parts, axis=1).astype(BF)
-        elif p == 1:
-            W[l, 1, xh, z, s] = wup_ref[l]
         else:
-            W[l, 2, xh, z, s] = wdown_ref[l].astype(F32).T.astype(BF)
+            pltpu.make_async_copy((wup_ref, wdown_ref)[p - 1].at[l], W.at[l, p, xh, z, s], wsem.at[l, p - 1]).wait()
 
     vrow[...] = jnp.zeros_like(vrow)
     for l in range(2):
@@ -301,22 +303,35 @@
             total = dW[l, p, xh, z, s, :, cols].astype(F32)
             for k in range(3):
                 total = total + rc[l, p, k, :, cols].astype(F32)
-            dwo_ref[l, p, :, cols] = total
+            dwo[l, p, :, cols] = total
+            own = dwo.at[l, p, :, cols]
+            pltpu.make_async_copy(own, dwo_ref.at[l, p, :, cols], osem.at[l, i, way]).start()
 
     def vec(l, r):
         return V[l, r : r + 1, 0:D]
 
-    def rs_start(a, c, value):
-        part[c] = value.astype(BF).reshape(4, 2, 16, D)
-        remote(part.at[c, :, other], dr.at[a, c], s1.at[c], r1.at[a, c], core_dev).start()
+    def rs_start(a, c, value_of):
+        for h in range(2):
+            lanes = slice(640 * h, 640 * h + 640)
+            part[c, :, :, :, lanes] = value_of(h).astype(BF).reshape(4, 2, 16, 640)
+            remote(
+                part.at[c, :, other, :, lanes], dr.at[a, c, :, :, lanes], s1.at[c, h], r1.at[a, c, h], core_dev
+            ).start()
 
     def rs_mid(a, c):
-        wait_bytes(dr.at[a, c], r1.at[a, c])
-        wait_bytes(dr.at[a, c], s1.at[c])
-        sb[c] = (part[c, :, core].astype(F32) + dr[a, c].astype(F32)).astype(BF)
-        for k in range(1, 4):
-            j, dev = y_dev(k)
-            remote(sb.at[c, j], yr.at[a, c, k - 1], s2.at[c], r2.at[a, c], dev).start()
+        for h in range(2):
+            lanes = slice(640 * h, 640 * h + 640)
+            half = dr.at[a, c, :, :, lanes]
+            wait_bytes(half, r1.at[a, c, h])
+            wait_bytes(half, s1.at[c, h])
+            sb[c, :, :, lanes] = (
+                part[c, :, core, :, lanes].astype(F32) + dr[a, c, :, :, lanes].astype(F32)
+            ).astype(BF)
+            for k in (2, 1, 3):
+                j, dev = y_dev(k)
+                remote(
+                    sb.at[c, j, :, lanes], yr.at[a, c, k - 1, :, lanes], s2.at[c], r2.at[a, c], dev
+                ).start()
 
     def rs_end(a, c):
         wait_bytes(yr.at[a, c], r2.at[a, c])
@@ -328,7 +343,7 @@
 
     def ag_start(buf, i, a, c, value):
         buf[i, c, y, core] = value.astype(BF)
-        for k in range(1, 4):
+        for k in (2, 1, 3):
             _, dev = y_dev(k)
             remote(buf.at[i, c, y, core], buf.at[i, c, y, core], s3.at[c], r3.at[a, c], dev).start()
 
@@ -373,7 +388,7 @@
         )
         wide = jnp.concatenate([jnp.zeros((ROWS, 96), F32), attended], axis=1).astype(BF)
         att[l, c] = wide
-        rs_start(2 * l, c, dot_nt(wide, W[l, 0, :, :, :, :, 384:640].reshape(D, 256)))
+        rs_start(2 * l, c, lambda h: dot_nt(wide, W[l, 0, h, :, :, :, 384:640].reshape(640, 256)))
 
     def attend_rows(l, c):
         a = 2 * l
@@ -394,7 +409,7 @@
             ring_wait(DOWN0Z)
         elif c == 0:
             ring_wait(DOWN1)
-        rs_start(2 * l + 1, c, dot_nt(activated, W[l, 2].reshape(D, PART)))
+        rs_start(2 * l + 1, c, lambda h: dot_nt(activated, W[l, 2, h].reshape(640, PART)))
 
     def feed_rows(l, c):
         a = 2 * l + 1
@@ -410,7 +425,7 @@
         grad_pre = (grad_act * slope[l, c]).astype(BF)
         gpre[c] = grad_pre
         gb[2 + l : 3 + l, :] += jnp.sum(grad_pre.astype(F32), axis=0, keepdims=True)
-        rs_start(6 - 2 * l, c, dot_nt(grad_pre, W[l, 1].reshape(D, PART)))
+        rs_start(6 - 2 * l, c, lambda h: dot_nt(grad_pre, W[l, 1, h].reshape(640, PART)))
 
     def feed_back_rows(l, c):
         a = 6 - 2 * l
@@ -454,8 +469,13 @@
         gkeep[c, :, 160:480] += far[:, 0:320]
         grads = gkeep[c].astype(BF)
         gproj[c] = grads
-        gb[l : l + 1, 0:512] += jnp.sum(grads.astype(F32), axis=0, keepdims=True)
-        rs_start(7 - 2 * l, c, dot_nt(grads, W[l, 0, :, :, :, :, 0:512].reshape(D, 512)))
+        total = jnp.sum(grads.astype(F32), axis=0, keepdims=True)
+        if l:
+            gb[1:2, 0:512] += total
+        else:
+            for i in range(4):
+                gq[i : i + 1, :] += total[:, 128 * i : 128 * i + 128]
+        rs_start(7 - 2 * l, c, lambda h: dot_nt(grads, W[l, 0, h, :, :, :, 0:512].reshape(640, 512)))
 
     def project_back_rows(l, c):
         a = 7 - 2 * l
@@ -499,6 +519,7 @@
     V[...] = jnp.zeros_like(V)
     GV[...] = jnp.zeros_like(GV)
     gb[...] = jnp.zeros_like(gb)
+    gq[...] = jnp.zeros_like(gq)
     bqkv[...] = jnp.zeros_like(bqkv)
     for l in range(2):
         bqkv[l, :, 0:160] = bqv_ref[l, 0:1, :].astype(F32)
@@ -513,15 +534,16 @@
         V[1, :, low : low + 256] += held[8:16]
     cp_h.wait()
     cp_c.wait()
+    gather_one(UP0)
+    gather_one(DOWN0Z)
+    gather_one(DOWN0X)
     for c in range(MICRO):
         whole = FB[0, c].reshape(ROWS, D).astype(F32)
         unit, _ = norm_parts(whole)
         xrow[0, c] = FB[0, c, y, core].astype(F32)
         FB[0, c] = (unit * vec(0, 0) + vec(0, 2)).astype(BF).reshape(4, 2, 16, D)
-        if c == 0:
-            gather_one(UP0)
-            gather_one(DOWN0X)
     gather_two(OUT0)
+    ring_two(UP0)
     gather_wait(QKV0)
 
     def mask_grads():
@@ -535,6 +557,21 @@
         @pl.loop(1, SHARDS)
         def _(k):
             remote(gb, br.at[k - 1], es.at[1], er.at[1], shard_dev(k)[1]).start()
+
+    def last_sums():
+        @pl.loop(1, SHARDS)
+        def _(k):
+            remote(gq, bq.at[k - 1], es.at[3], er.at[3], shard_dev(k)[1]).start()
+
+    def norm_sums():
+        for i in range(11):
+            GT[i, 0:8] = GV[0, :, 128 * i : 128 * i + 128]
+            GT[i, 8:16] = GV[1, :, 128 * i : 128 * i + 128]
+
+        @pl.loop(1, SHARDS)
+        def _(k):
+            j, dev = shard_dev(k)
+            remote(GT.at[pl.ds(SHARD * j // 128, 2)], vr.at[k - 1], es.at[0], er.at[0], dev).start()
 
     cp_o = pltpu.make_async_copy(FB.at[4], out_ref, lsem.at[0])
     cp_g = pltpu.make_async_copy(BB.at[4], ingrad_ref, lsem.at[1])
@@ -562,16 +599,16 @@
             sums[a1, c] = (partial(project_back_rows, l, c), BB, 4 - 2 * l)
 
     g1, g2, g3, g4 = gather_one, ring_two, ring_three, ring_wait
-    d1, d2 = reduce_one, reduce_two
+    d1, d2, d3 = reduce_one, reduce_two, reduce_three
     before = {
-        0: [(g2, UP0), (g1, DOWN0Z)],
         2: [(g2, DOWN0X)],
-        3: [(gather_wait, OUT0), (g2, DOWN0Z)],
+        3: [(g2, DOWN0Z), (gather_wait, OUT0)],
         4: [(g3, UP0), (g1, PROJ1)],
-        5: [(g3, DOWN0X), (g3, DOWN0Z), (g2, PROJ1)],
-        6: [(g4, UP0), (g1, UP1)],
-        7: [(g3, PROJ1), (g2, UP1), (g1, DOWN1)],
-        9: [(g4, PROJ1), (g3, UP1), (g2, DOWN1)],
+        5: [(g3, DOWN0Z), (g3, DOWN0X)],
+        6: [(g4, UP0), (g2, PROJ1), (g1, UP1)],
+        8: [(g3, PROJ1), (g2, UP1), (g1, DOWN1)],
+        9: [(g4, PROJ1)],
+        10: [(g3, UP1), (g2, DOWN1)],
         12: [(g3, DOWN1)],
         15: [(g4, UP1)],
     }
@@ -580,21 +617,30 @@
         4: [(pack, 1, 1)],
         5: [(pack, 1, 2)],
         6: [(mask_grads,)],
-        18: [(down_grad, 1, 0), (down_grad, 1, 1), (d1, 1, DOWN)],
-        21: [(up_grad, 1, 0), (up_grad, 1, 1), (d1, 1, UP)],
-        23: [(out_grad, 1, 0), (out_grad, 1, 1), (d1, 1, OUT)],
+        18: [(down_grad, 1, 0)],
+        20: [(up_grad, 1, 0)],
+        24: [(out_grad, 1, 0), (out_grad, 1, 1), (d1, 1, OUT)],
+        25: [(d2, 1, UP)],
+        26: [(qkv_grad, 1, 0)],
+        27: [(d2, 1, OUT)],
+        29: [(down_grad, 0, 0)],
+        30: [(up_grad, 0, 0)],
+        31: [(up_grad, 0, 1), (d1, 0, UP), (bias_sums,)],
+        33: [(out_grad, 0, 0), (out_grad, 0, 1), (d1, 0, OUT)],
+        34: [(d2, 0, DOWN)],
+        35: [(qkv_grad, 0, 0), (qkv_grad, 0, 1), (d1, 0, QKV), (last_sums,)],
+        36: [(d2, 0, OUT)],
+    }
+    later = {
+        18: [(down_grad, 1, 1), (d1, 1, DOWN)],
+        20: [(up_grad, 1, 1), (d1, 1, UP)],
         24: [(d2, 1, DOWN)],
-        25: [(d2, 1, UP)],
-        26: [(qkv_grad, 1, 0), (qkv_grad, 1, 1), (d1, 1, QKV)],
-        27: [(d2, 1, OUT)],
-        29: [(down_grad, 0, 0), (down_grad, 0, 1), (d1, 0, DOWN)],
-        30: [(up_grad, 0, 0), (up_grad, 0, 1), (d1, 0, UP)],
-        31: [(d2, 1, QKV)],
-        32: [(out_grad, 0, 0), (out_grad, 0, 1), (d1, 0, OUT)],
-        33: [(d2, 0, DOWN)],
-        34: [(d2, 0, UP)],
-        35: [(qkv_grad, 0, 0), (qkv_grad, 0, 1), (d1, 0, QKV), (bias_sums,)],
-        36: [(d2, 0, OUT)],
+        26: [(qkv_grad, 1, 1), (d1, 1, QKV)],
+        27: [(d3, 1, DOWN)],
+        28: [(d3, 1, UP)],
+        29: [(down_grad, 0, 1), (d1, 0, DOWN)],
+        33: [(d2, 1, QKV)],
+        34: [(d2, 0, UP), (d3, 1, OUT)],
     }
     for n in range(len(steps) + 2):
         for fn, *where in before.get(n, ()):
@@ -607,23 +653,21 @@
             rs_mid(*steps[n][1])
         if 1 <= n <= len(steps) and steps[n - 1][1] is not None:
             sums[steps[n - 1][1]][0]()
+        if n == len(steps):
+            norm_sums()
         if n >= 2 and steps[n - 2][1] is not None:
             a, c = steps[n - 2][1]
             ag_mid(sums[a, c][1], sums[a, c][2], a, c)
-            ag_end(a, c)
+        for fn, *where in later.get(n, ()):
+            fn(*where)
+        if n >= 2 and steps[n - 2][1] is not None:
+            ag_end(*steps[n - 2][1])
         if n == 19:
             cp_o.start()
 
-    for i in range(11):
-        GT[i, 0:8] = GV[0, :, 128 * i : 128 * i + 128]
-        GT[i, 8:16] = GV[1, :, 128 * i : 128 * i + 128]
-
-    @pl.loop(1, SHARDS)
-    def _(k):
-        j, dev = shard_dev(k)
-        remote(GT.at[pl.ds(SHARD * j // 128, 2)], vr.at[k - 1], es.at[0], er.at[0], dev).start()
-
     cp_g.start()
+    for l, i in ((1, QKV), (0, DOWN), (0, UP)):
+        reduce_three(l, i)
     wait_bytes(vr, er.at[0])
     wait_bytes(vr, es.at[0])
     own = GT[pl.ds(SHARD * me // 128, 2)]
@@ -635,14 +679,20 @@
     def _(k):
         remote(vr2.at[7], vr2.at[k - 1], es.at[2], er.at[2], (f, s, (t + k) % 8)).start()
 
-    reduce_two(0, QKV)
     wait_bytes(br, er.at[1])
     wait_bytes(br, es.at[1])
+    wait_bytes(bq, er.at[3])
+    wait_bytes(bq, es.at[3])
     totals = gb[...]
+    lasts = gq[...]
     for k in range(SHARDS - 1):
         totals = totals + br[k]
+        lasts = lasts + bq[k]
     bsum_ref[...] = totals
-    for l, i in ((1, DOWN), (1, UP), (1, OUT), (1, QKV), (0, DOWN), (0, UP), (0, OUT)):
+    for i in range(4):
+        bsum_ref[0:1, 128 * i : 128 * i + 128] = lasts[i : i + 1]
+    reduce_two(0, QKV)
+    for l, i in ((0, OUT),):
         reduce_three(l, i)
     wait_bytes(vr2.at[pl.ds(0, 7)], er.at[2])
     wait_bytes(vr2.at[pl.ds(0, 7)], es.at[2])
@@ -651,6 +701,11 @@
         own = own + vr2[k]
     vsum_ref[...] = own
     reduce_three(0, QKV)
+    for l in range(2):
+        for i in range(4):
+            p, ways = piece(l, i)
+            for way, cols in ways:
+                pltpu.make_async_copy(dwo.at[l, p, :, cols], dwo_ref.at[l, p, :, cols], osem.at[l, i, way]).wait()
     cp_o.wait()
     cp_g.wait()
 
@@ -659,19 +714,38 @@
     out_ref, ingrad_ref, dwo_ref, vsum_ref, bsum_ref,
     hidden_ref, grad_ref, gqkv_ref, gqv_ref, gout_ref, gbout_ref, gup_ref, gbup_ref, gdown_ref, gbdown_ref,
     ggain_ref, gshift_ref,
+    narrow, wide, dwo, in_sem, out_sem, w_sem, g_sem,
 ):
     me = lax.axis_index("fsdp") * 2 + lax.axis_index("seq")
-    hidden_ref[...] = out_ref[...].astype(F32)
-    grad_ref[...] = ingrad_ref[...].astype(F32)
+    tasks = [(a, c) for c in range(MICRO) for a in range(2)]
+    sources, targets = (out_ref, ingrad_ref), (hidden_ref, grad_ref)
+
+    def fetch(a, c):
+        return pltpu.make_async_copy(sources[a].at[c], narrow.at[a, c], in_sem.at[a, c])
+
+    def store(a, c):
+        return pltpu.make_async_copy(wide.at[a, c], targets[a].at[c], out_sem.at[a, c])
+
+    weights = pltpu.make_async_copy(dwo_ref, dwo, w_sem.at[0])
+    for a, c in tasks:
+        fetch(a, c).start()
+    weights.start()
+    ups = pltpu.make_async_copy(dwo.at[:, 1], gup_ref, g_sem.at[0])
+    downs = pltpu.make_async_copy(dwo.at[:, 2], gdown_ref, g_sem.at[1])
+    for a, c in tasks:
+        fetch(a, c).wait()
+        wide[a, c] = narrow[a, c].astype(F32)
+        store(a, c).start()
+    weights.wait()
+    ups.start()
+    downs.start()
     rows = jnp.concatenate([vsum_ref[0], vsum_ref[1]], axis=1)
     rows = pltpu.roll(rows, (256 - (SHARD * me) % 128) % 256, 1)
     for l in range(2):
-        proj = dwo_ref[l, 0]
+        proj = dwo[l, 0]
         for i in range(3):
             gqkv_ref[l, i] = proj[:, 160 * i : 160 * i + 160]
         gout_ref[l] = proj[:, 480:640].T
-        gup_ref[l] = dwo_ref[l, 1]
-        gdown_ref[l] = dwo_ref[l, 2].T
         gqv_ref[l, 0:1, :] = bsum_ref[l : l + 1, 0:160]
         gqv_ref[l, 1:2, :] = bsum_ref[l : l + 1, 320:480]
         gbup_ref[l : l + 1, :] = bsum_ref[2 + l : 3 + l, :]
@@ -679,6 +753,10 @@
         gshift_ref[l] = rows[8 * l + 2 : 8 * l + 4, 0:SHARD]
         gbout_ref[l : l + 1, :] = rows[8 * l + 4 : 8 * l + 5, 0:SHARD]
         gbdown_ref[l : l + 1, :] = rows[8 * l + 5 : 8 * l + 6, 0:SHARD]
+    ups.wait()
+    downs.wait()
+    for a, c in tasks:
+        store(a, c).wait()
 
 
 def body(
@@ -725,14 +803,17 @@
         pltpu.VMEM((8, 2, 16, 128), F32),
         pltpu.VMEM((8, PART), F32),
         pltpu.VMEM((SHARDS - 1, 8, PART), F32),
+        pltpu.VMEM((8, 128), F32),
+        pltpu.VMEM((SHARDS - 1, 8, 128), F32),
         pltpu.VMEM((16, 256), F32),
         pltpu.VMEM((2, 1, 512), F32),
+        pltpu.VMEM((2, 3, SHARD, PART), F32),
         dma((8, 2)), dma((8, 2)), dma((8, 2)), dma((8, 2)), dma((8, 2)), dma((8, 2)),
         dma((2, 4, 2)), dma((2, 4, 2)), dma((2, 4, 2)), dma((2, 4, 2)),
-        dma((MICRO,)), dma((8, MICRO)), dma((MICRO,)), dma((8, MICRO)),
+        dma((MICRO, 2)), dma((8, MICRO, 2)), dma((MICRO,)), dma((8, MICRO)),
         dma((MICRO,)), dma((8, MICRO)), dma((MICRO,)), dma((8, MICRO)),
         dma((2, MICRO)), dma((2, MICRO)), dma((MICRO,)), dma((2, MICRO)),
-        dma((1,)), dma((1,)), dma((3,)), dma((3,)), dma((2,)),
+        dma((1,)), dma((1,)), dma((4,)), dma((4,)), dma((2,)), dma((2, 2)), dma((2, 4, 2)),
     ]
     out, ingrad, dwo, vsum, bsum = pl.pallas_call(
         kernel,
@@ -744,29 +825,36 @@
             jax.ShapeDtypeStruct((2, 16, 128), F32),
             jax.ShapeDtypeStruct((8, PART), F32),
         ),
-        in_specs=[anys, anys, smem] + [vmem] * 10,
-        out_specs=(anys, anys, vmem, vmem, vmem),
+        in_specs=[anys, anys, smem, vmem, vmem, vmem, vmem, anys, vmem, anys, vmem, vmem, vmem],
+        out_specs=(anys, anys, anys, vmem, vmem),
         scratch_shapes=scratch,
         compiler_params=pltpu.CompilerParams(
             collective_id=0, has_side_effects=True, vmem_limit_bytes=63 * 1024 * 1024
         ),
     )(
         hidden_in.reshape(blocks), cotangent.reshape(blocks), lengths, qkv_weight, qv_bias, out_weight,
-        out_bias, up_weight, up_bias, down_weight, down_bias, ln_gain, ln_bias,
+        out_bias, up_weight, up_bias, jnp.swapaxes(down_weight, 1, 2), down_bias, ln_gain, ln_bias,
     )
     rows = (MICRO, ROWS, D)
     shapes = (
         rows, rows, (2, 3, SHARD, 160), (2, 2, 160), (2, 160, SHARD), (2, SHARD), (2, SHARD, PART),
-        (2, PART), (2, PART, SHARD), (2, SHARD), (2, 2, SHARD), (2, 2, SHARD),
+        (2, PART), (2, SHARD, PART), (2, SHARD), (2, 2, SHARD), (2, 2, SHARD),
     )
-    return pl.pallas_call(
+    outs = pl.pallas_call(
         finish,
         name="finish",
         out_shape=tuple(jax.ShapeDtypeStruct(shape, F32) for shape in shapes),
-        in_specs=[vmem] * 5,
-        out_specs=(vmem,) * 12,
+        in_specs=[anys, anys, anys, vmem, vmem],
+        out_specs=(anys, anys, vmem, vmem, vmem, vmem, anys, vmem, anys, vmem, vmem, vmem),
+        scratch_shapes=[
+            pltpu.VMEM((2,) + rows, BF),
+            pltpu.VMEM((2,) + rows, F32),
+            pltpu.VMEM((2, 3, SHARD, PART), F32),
+            dma((2, MICRO)), dma((2, MICRO)), dma((1,)), dma((2,)),
+        ],
         compiler_params=pltpu.CompilerParams(vmem_limit_bytes=32 * 1024 * 1024),
     )(out.reshape(rows), ingrad.reshape(rows), dwo, vsum, bsum)
+    return outs[:8] + (jnp.swapaxes(outs[8], 1, 2),) + outs[9:]
 
 
 def solution(mesh):

time: 230 us -> 239 us (1.039); the launches traced: 229 us -> 234 us
  Pallas kernels: 221 us -> 228 us
  local copies, waits for them, and re-layouts: 7.93 us -> 5.13 us
    pallas_call x1, Pallas kernels: 218 us -> 224 us  [body(): pl.pallas_call(kernel, name='encoder', out_shape=(jax.ShapeDtypeStruct(bl...]
    unnamed x11 -> x10, local copies, waits for them, and re-layouts: 6.96 us -> 5.13 us
where the time goes in v4:
time: 239 us; the launch traced here: 234 us
  Pallas kernels  228 us (95%)
  local copies, waits for them, and re-layouts  5.13 us (2%)
    pallas_call x1, Pallas kernels, body(): pl.pallas_call(kernel, name='encoder', out_shape=(jax.ShapeDtypeStruct(bl...  224 us
    unnamed x10, local copies, waits for them, and re-layouts  5.13 us

profile of v4, /device:TPU:0, one launch (start us, length us, event | category | flops | bytes accessed | tf_op | source)
XLA Modules:
  0.0 234.3 jit_solution(11272140259270436761)
XLA Ops:
  0.6 224.1 %encoder.1 = (bf16[3,4,2,16,1280]{4,3,2,1,0:T(8,128)(2,1)}, bf16[3,4,2,16,1280]{4,3,2,1,0:T(8,128)(2,1)}, f32[2,3,80,640]{3,2,1,0:T(8,128)}, f32[2,16,128]{2,1,0:T(8,128)}, f32[8,640]{1,0:T(8,128)}) custom-call(bf16[3,4,2,16,1280]{4,3,2,1,0:T(8,128)(2,1)} %bitcast.8, bf16[3,4,2,16,1280]{4,3,2,1,0:T(8,128)(2,1)} %bitcast.9, s32[3]{0:T(128)} %len_ref.1, ...), custom_call_target="tpu_custom_call" | custom-call | tf_op jit(solution)/shard_map/encoder/pallas_call | solution.py:818
  224.8 0.0 copy-start
  224.8 1.3 copy-done
  226.1 0.0 copy-start.1
  226.1 1.2 copy-done.1
  227.3 0.0 copy-start.2
  227.3 1.2 copy-done.2
  228.5 0.0 copy-start.3
  228.5 0.7 copy-done.3
  229.2 0.0 copy-start.4
  229.2 0.7 copy-done.4
  229.9 4.2 %finish.1 = (f32[3,128,1280]{2,1,0:T(8,128)}, f32[3,128,1280]{2,1,0:T(8,128)}, f32[2,3,80,160]{3,2,1,0:T(8,128)}, f32[2,2,160]{2,1,0:T(2,128)}, f32[2,160,80]{2,...) custom-call(bf16[3,128,1280]{2,1,0:T(8,128)(2,1)S(1)} %bitcast.6, ...), custom_call_target="tpu_custom_call" | custom-call | tf_op jit(solution)/shard_map/finish/pallas_call | solution.py:843
Async XLA Ops:
  224.8 1.3 copy-start
  226.1 1.2 copy-start.1
  227.3 1.2 copy-start.2
  228.5 0.7 copy-start.3
  229.2 0.7 copy-start.4

commit v5 on v4

--- a/solution.py
+++ b/solution.py
@@ -714,38 +714,19 @@
     out_ref, ingrad_ref, dwo_ref, vsum_ref, bsum_ref,
     hidden_ref, grad_ref, gqkv_ref, gqv_ref, gout_ref, gbout_ref, gup_ref, gbup_ref, gdown_ref, gbdown_ref,
     ggain_ref, gshift_ref,
-    narrow, wide, dwo, in_sem, out_sem, w_sem, g_sem,
 ):
     me = lax.axis_index("fsdp") * 2 + lax.axis_index("seq")
-    tasks = [(a, c) for c in range(MICRO) for a in range(2)]
-    sources, targets = (out_ref, ingrad_ref), (hidden_ref, grad_ref)
-
-    def fetch(a, c):
-        return pltpu.make_async_copy(sources[a].at[c], narrow.at[a, c], in_sem.at[a, c])
-
-    def store(a, c):
-        return pltpu.make_async_copy(wide.at[a, c], targets[a].at[c], out_sem.at[a, c])
-
-    weights = pltpu.make_async_copy(dwo_ref, dwo, w_sem.at[0])
-    for a, c in tasks:
-        fetch(a, c).start()
-    weights.start()
-    ups = pltpu.make_async_copy(dwo.at[:, 1], gup_ref, g_sem.at[0])
-    downs = pltpu.make_async_copy(dwo.at[:, 2], gdown_ref, g_sem.at[1])
-    for a, c in tasks:
-        fetch(a, c).wait()
-        wide[a, c] = narrow[a, c].astype(F32)
-        store(a, c).start()
-    weights.wait()
-    ups.start()
-    downs.start()
+    hidden_ref[...] = out_ref[...].astype(F32)
+    grad_ref[...] = ingrad_ref[...].astype(F32)
     rows = jnp.concatenate([vsum_ref[0], vsum_ref[1]], axis=1)
     rows = pltpu.roll(rows, (256 - (SHARD * me) % 128) % 256, 1)
     for l in range(2):
-        proj = dwo[l, 0]
+        proj = dwo_ref[l, 0]
         for i in range(3):
             gqkv_ref[l, i] = proj[:, 160 * i : 160 * i + 160]
         gout_ref[l] = proj[:, 480:640].T
+        gup_ref[l] = dwo_ref[l, 1]
+        gdown_ref[l] = dwo_ref[l, 2]
         gqv_ref[l, 0:1, :] = bsum_ref[l : l + 1, 0:160]
         gqv_ref[l, 1:2, :] = bsum_ref[l : l + 1, 320:480]
         gbup_ref[l : l + 1, :] = bsum_ref[2 + l : 3 + l, :]
@@ -753,10 +734,6 @@
         gshift_ref[l] = rows[8 * l + 2 : 8 * l + 4, 0:SHARD]
         gbout_ref[l : l + 1, :] = rows[8 * l + 4 : 8 * l + 5, 0:SHARD]
         gbdown_ref[l : l + 1, :] = rows[8 * l + 5 : 8 * l + 6, 0:SHARD]
-    ups.wait()
-    downs.wait()
-    for a, c in tasks:
-        store(a, c).wait()
 
 
 def body(
@@ -844,15 +821,9 @@
         finish,
         name="finish",
         out_shape=tuple(jax.ShapeDtypeStruct(shape, F32) for shape in shapes),
-        in_specs=[anys, anys, anys, vmem, vmem],
-        out_specs=(anys, anys, vmem, vmem, vmem, vmem, anys, vmem, anys, vmem, vmem, vmem),
-        scratch_shapes=[
-            pltpu.VMEM((2,) + rows, BF),
-            pltpu.VMEM((2,) + rows, F32),
-            pltpu.VMEM((2, 3, SHARD, PART), F32),
-            dma((2, MICRO)), dma((2, MICRO)), dma((1,)), dma((2,)),
-        ],
-        compiler_params=pltpu.CompilerParams(vmem_limit_bytes=32 * 1024 * 1024),
+        in_specs=[vmem] * 5,
+        out_specs=(vmem,) * 12,
+        compiler_params=pltpu.CompilerParams(vmem_limit_bytes=63 * 1024 * 1024),
     )(out.reshape(rows), ingrad.reshape(rows), dwo, vsum, bsum)
     return outs[:8] + (jnp.swapaxes(outs[8], 1, 2),) + outs[9:]
 

time: 239 us -> 234 us (0.979)
  local copies, waits for them, and re-layouts: 5.13 us -> 0 us
    unnamed x10 -> x0, local copies, waits for them, and re-layouts: 5.13 us -> none
where the time goes in v5:
time: 234 us; the launch traced here: 230 us
  Pallas kernels  229 us (98%)
    pallas_call x1, Pallas kernels, body(): pl.pallas_call(kernel, name='encoder', out_shape=(jax.ShapeDtypeStruct(bl...  224 us

profile of v5, /device:TPU:0, one launch (start us, length us, event | category | flops | bytes accessed | tf_op | source)
XLA Modules:
  0.0 229.5 jit_solution(3235698898657588183)
XLA Ops:
  0.6 224.0 %encoder.1 = (bf16[3,4,2,16,1280]{4,3,2,1,0:T(8,128)(2,1)}, bf16[3,4,2,16,1280]{4,3,2,1,0:T(8,128)(2,1)}, f32[2,3,80,640]{3,2,1,0:T(8,128)}, f32[2,16,128]{2,1,0:T(8,128)}, f32[8,640]{1,0:T(8,128)}) custom-call(bf16[3,4,2,16,1280]{4,3,2,1,0:T(8,128)(2,1)} %bitcast.6, bf16[3,4,2,16,1280]{4,3,2,1,0:T(8,128)(2,1)} %bitcast.7, s32[3]{0:T(128)} %len_ref.1, ...), custom_call_target="tpu_custom_call" | custom-call | tf_op jit(solution)/shard_map/encoder/pallas_call | solution.py:795
  224.6 4.7 %finish.1 = (f32[3,128,1280]{2,1,0:T(8,128)}, f32[3,128,1280]{2,1,0:T(8,128)}, f32[2,3,80,160]{3,2,1,0:T(8,128)}, f32[2,2,160]{2,1,0:T(2,128)}, f32[2,160,80]{2,...) custom-call(bf16[3,128,1280]{2,1,0:T(8,128)(2,1)} %bitcast.8, ...), custom_call_target="tpu_custom_call" | custom-call | tf_op jit(solution)/shard_map/finish/pallas_call | solution.py:820

commit v6 on v5

--- a/solution.py
+++ b/solution.py
@@ -488,25 +488,34 @@
         GV[l, 2:3, 0:D] += jnp.sum(grad_norm, axis=0, keepdims=True)
 
     def left_of(buf, i, m):
-        return buf[i, :, :, :, :, 640 * m : 640 * m + 640].reshape(MICRO * ROWS, 640)
-
-    def down_grad(l, m):
-        right = act[l].reshape(MICRO * ROWS, PART)
-        dW[l, 2, m] = dot_tn(left_of(BB, 2 - 2 * l, m), right).astype(BF).reshape(4, 2, SHARD, PART)
-
-    def up_grad(l, m):
-        right = gpre[...].reshape(MICRO * ROWS, PART)
-        dW[l, 1, m] = dot_tn(left_of(FB, 2 * l + 1, m), right).astype(BF).reshape(4, 2, SHARD, PART)
-
-    def out_grad(l, m):
-        grad = dot_tn(left_of(BB, 3 - 2 * l, m), att[l].reshape(MICRO * ROWS, 256))
-        dW[l, 0, m, :, :, :, 384:640] = grad.astype(BF).reshape(4, 2, SHARD, 256)
-
-    def qkv_grad(l, m):
-        grad = dot_tn(left_of(FB, 2 * l, m), gproj[...].reshape(MICRO * ROWS, 512))
-        dW[l, 0, m, :, :, :, 0:384] = grad[:, 0:384].astype(BF).reshape(4, 2, SHARD, 384)
-        rest = dW[l, 0, m, :, :, :, 384:512].astype(F32).reshape(640, 128) + grad[:, 384:512]
-        dW[l, 0, m, :, :, :, 384:512] = rest.astype(BF).reshape(4, 2, SHARD, 128)
+        lanes = pl.ds(pl.multiple_of(m * 640, 128), 640)
+        return buf[i, :, :, :, :, lanes].reshape(MICRO * ROWS, 640)
+
+    def down_grad(l):
+        @pl.loop(0, 2)
+        def _(m):
+            right = act[l].reshape(MICRO * ROWS, PART)
+            dW[l, 2, m] = dot_tn(left_of(BB, 2 - 2 * l, m), right).astype(BF).reshape(4, 2, SHARD, PART)
+
+    def up_grad(l):
+        @pl.loop(0, 2)
+        def _(m):
+            right = gpre[...].reshape(MICRO * ROWS, PART)
+            dW[l, 1, m] = dot_tn(left_of(FB, 2 * l + 1, m), right).astype(BF).reshape(4, 2, SHARD, PART)
+
+    def out_grad(l):
+        @pl.loop(0, 2)
+        def _(m):
+            grad = dot_tn(left_of(BB, 3 - 2 * l, m), att[l].reshape(MICRO * ROWS, 256))
+            dW[l, 0, m, :, :, :, 384:640] = grad.astype(BF).reshape(4, 2, SHARD, 256)
+
+    def qkv_grad(l):
+        @pl.loop(0, 2)
+        def _(m):
+            grad = dot_tn(left_of(FB, 2 * l, m), gproj[...].reshape(MICRO * ROWS, 512))
+            dW[l, 0, m, :, :, :, 0:384] = grad[:, 0:384].astype(BF).reshape(4, 2, SHARD, 384)
+            rest = dW[l, 0, m, :, :, :, 384:512].astype(F32).reshape(640, 128) + grad[:, 384:512]
+            dW[l, 0, m, :, :, :, 384:512] = rest.astype(BF).reshape(4, 2, SHARD, 128)
 
     @pl.loop(1, SHARDS)
     def _(k):
@@ -617,28 +626,24 @@
         4: [(pack, 1, 1)],
         5: [(pack, 1, 2)],
         6: [(mask_grads,)],
-        18: [(down_grad, 1, 0)],
-        20: [(up_grad, 1, 0)],
-        24: [(out_grad, 1, 0), (out_grad, 1, 1), (d1, 1, OUT)],
+        18: [(down_grad, 1), (d1, 1, DOWN)],
+        20: [(up_grad, 1), (d1, 1, UP)],
+        24: [(out_grad, 1), (d1, 1, OUT)],
         25: [(d2, 1, UP)],
-        26: [(qkv_grad, 1, 0)],
+        26: [(qkv_grad, 1), (d1, 1, QKV)],
         27: [(d2, 1, OUT)],
-        29: [(down_grad, 0, 0)],
-        30: [(up_grad, 0, 0)],
-        31: [(up_grad, 0, 1), (d1, 0, UP), (bias_sums,)],
-        33: [(out_grad, 0, 0), (out_grad, 0, 1), (d1, 0, OUT)],
+        29: [(down_grad, 0), (d1, 0, DOWN)],
+        30: [(up_grad, 0), (d1, 0, UP)],
+        31: [(bias_sums,)],
+        33: [(out_grad, 0), (d1, 0, OUT)],
         34: [(d2, 0, DOWN)],
-        35: [(qkv_grad, 0, 0), (qkv_grad, 0, 1), (d1, 0, QKV), (last_sums,)],
+        35: [(qkv_grad, 0), (d1, 0, QKV), (last_sums,)],
         36: [(d2, 0, OUT)],
     }
     later = {
-        18: [(down_grad, 1, 1), (d1, 1, DOWN)],
-        20: [(up_grad, 1, 1), (d1, 1, UP)],
         24: [(d2, 1, DOWN)],
-        26: [(qkv_grad, 1, 1), (d1, 1, QKV)],
         27: [(d3, 1, DOWN)],
         28: [(d3, 1, UP)],
-        29: [(down_grad, 0, 1), (d1, 0, DOWN)],
         33: [(d2, 1, QKV)],
         34: [(d2, 0, UP), (d3, 1, OUT)],
     }

time: 234 us -> 218 us (0.932); the launches traced: 230 us -> 218 us
  Pallas kernels: 229 us -> 218 us
    pallas_call x1, Pallas kernels: 224 us -> 213 us  [body(): pl.pallas_call(kernel, name='encoder', out_shape=(jax.ShapeDtypeStruct(bl...]
where the time goes in v6:
time: 218 us
  Pallas kernels  218 us (100%)
    pallas_call x1, Pallas kernels, body(): pl.pallas_call(kernel, name='encoder', out_shape=(jax.ShapeDtypeStruct(bl...  213 us
    pallas_call x1, Pallas kernels, body(): pl.pallas_call(finish, name='finish', out_shape=tuple((jax.ShapeDtypeStru...  4.66 us

profile of v6, /device:TPU:0, one launch (start us, length us, event | category | flops | bytes accessed | tf_op | source)
XLA Modules:
  0.0 218.3 jit_solution(15406856711720337643)
XLA Ops:
  0.6 212.8 %encoder.1 = (bf16[3,4,2,16,1280]{4,3,2,1,0:T(8,128)(2,1)}, bf16[3,4,2,16,1280]{4,3,2,1,0:T(8,128)(2,1)}, f32[2,3,80,640]{3,2,1,0:T(8,128)}, f32[2,16,128]{2,1,0:T(8,128)}, f32[8,640]{1,0:T(8,128)}) custom-call(bf16[3,4,2,16,1280]{4,3,2,1,0:T(8,128)(2,1)} %bitcast.6, bf16[3,4,2,16,1280]{4,3,2,1,0:T(8,128)(2,1)} %bitcast.7, s32[3]{0:T(128)} %len_ref.1, ...), custom_call_target="tpu_custom_call" | custom-call | tf_op jit(solution)/shard_map/encoder/pallas_call | solution.py:800
  213.5 4.7 %finish.1 = (f32[3,128,1280]{2,1,0:T(8,128)}, f32[3,128,1280]{2,1,0:T(8,128)}, f32[2,3,80,160]{3,2,1,0:T(8,128)}, f32[2,2,160]{2,1,0:T(2,128)}, f32[2,160,80]{2,...) custom-call(bf16[3,128,1280]{2,1,0:T(8,128)(2,1)} %bitcast.8, ...), custom_call_target="tpu_custom_call" | custom-call | tf_op jit(solution)/shard_map/finish/pallas_call | solution.py:825

commit v7 on v6

--- a/solution.py
+++ b/solution.py
@@ -33,14 +33,13 @@
 LOADS = (
     (0, 0, (256, 512), (0, 256)),
     (0, 0, (512, 640), None),
-    (0, 1, None, (0, 640)),
-    (0, 2, (0, 256), None),
-    (0, 2, None, (256, 640)),
+    (0, 1, (384, 640), (0, 384)),
+    (0, 2, (384, 640), (0, 384)),
     (1, 0, (384, 640), (0, 384)),
     (1, 1, (384, 640), (0, 384)),
     (1, 2, (384, 640), (0, 384)),
 )
-QKV0, OUT0, UP0, DOWN0X, DOWN0Z, PROJ1, UP1, DOWN1 = range(8)
+QKV0, OUT0, UP0, DOWN0, PROJ1, UP1, DOWN1 = range(7)
 
 
 def dot_nn(a, b):
@@ -122,6 +121,16 @@
     def wait_bytes(ref, sem):
         pltpu.make_async_copy(ref, ref, sem).wait()
 
+    barrier = pltpu.get_barrier_semaphore()
+
+    @pl.loop(1, SHARDS)
+    def _(k):
+        pl.semaphore_signal(barrier, inc=1, device_id=shard_dev(k)[1], device_id_type=MESH)
+
+    @pl.loop(1, 8)
+    def _(k):
+        pl.semaphore_signal(barrier, inc=1, device_id=(f, s, (t + k) % 8), device_id_type=MESH)
+
     cp_h = pltpu.make_async_copy(hid_ref, FB.at[0], lsem.at[0])
     cp_c = pltpu.make_async_copy(cot_ref, BB.at[0], lsem.at[1])
     cp_h.start()
@@ -130,16 +139,6 @@
     for l in range(2):
         for p in range(2):
             pltpu.make_async_copy((wup_ref, wdown_ref)[p].at[l], W.at[l, p + 1, xh, z, s], wsem.at[l, p]).start()
-
-    barrier = pltpu.get_barrier_semaphore()
-
-    @pl.loop(1, SHARDS)
-    def _(k):
-        pl.semaphore_signal(barrier, inc=1, device_id=shard_dev(k)[1], device_id_type=MESH)
-
-    @pl.loop(1, 8)
-    def _(k):
-        pl.semaphore_signal(barrier, inc=1, device_id=(f, s, (t + k) % 8), device_id_type=MESH)
 
     def pack(l, p):
         if p == 0:
@@ -168,7 +167,7 @@
         l, p, ways = load(n)
         for way, cols in ways:
             own = W.at[l, p, xh, z, s, :, cols]
-            for k in range(1, 4):
+            for k in (2, 1, 3):
                 dev = x_dev(k)[2] if way else z_dev(k)[1]
                 remote(own, own, g1s.at[n, way], g1r.at[n, way], dev).start()
 
@@ -184,7 +183,7 @@
         gather_mid(n)
         for way, cols in ways:
             four = W.at[l, p, :, z, :, :, cols] if way else W.at[l, p, xh, :, s, :, cols]
-            for k in range(1, 4):
+            for k in (2, 1, 3):
                 dev = z_dev(k)[1] if way else x_dev(k)[2]
                 remote(four, four, g2s.at[n, way], g2r.at[n, way], dev).start()
 
@@ -242,7 +241,7 @@
     def reduce_one(l, i):
         p, ways = piece(l, i)
         for way, cols in ways:
-            for k in range(1, 4):
+            for k in (2, 1, 3):
                 if way:
                     j, dev = z_dev(k)
                     four = dW.at[l, p, :, j, :, :, cols]
@@ -280,7 +279,7 @@
                     dW[l, p, xh, n, s, :, cols] = total.astype(BF)
 
         for way, cols in ways:
-            for k in range(1, 4):
+            for k in (2, 1, 3):
                 if way:
                     jh, jl, dev = x_dev(k)
                     one = dW.at[l, p, jh, z, jl, :, cols]
@@ -403,13 +402,10 @@
         cdf = 0.5 * (1.0 + lax.erf(pre * math.sqrt(0.5)))
         activated = (pre * cdf).astype(BF)
         act[l, c] = activated
+        if c == 0:
+            ring_wait(DOWN1 if l else DOWN0)
+        rs_start(2 * l + 1, c, lambda h: dot_nt(activated, W[l, 2, h].reshape(640, PART)))
         slope[l, c] = cdf + pre * jnp.exp(-0.5 * pre * pre) * (1.0 / math.sqrt(2.0 * math.pi))
-        if c == 0 and l == 0:
-            ring_wait(DOWN0X)
-            ring_wait(DOWN0Z)
-        elif c == 0:
-            ring_wait(DOWN1)
-        rs_start(2 * l + 1, c, lambda h: dot_nt(activated, W[l, 2, h].reshape(640, PART)))
 
     def feed_rows(l, c):
         a = 2 * l + 1
@@ -424,8 +420,8 @@
         grad_act = dot_nn(BB[2 - 2 * l, c].reshape(ROWS, D), W[l, 2].reshape(D, PART))
         grad_pre = (grad_act * slope[l, c]).astype(BF)
         gpre[c] = grad_pre
+        rs_start(6 - 2 * l, c, lambda h: dot_nt(grad_pre, W[l, 1, h].reshape(640, PART)))
         gb[2 + l : 3 + l, :] += jnp.sum(grad_pre.astype(F32), axis=0, keepdims=True)
-        rs_start(6 - 2 * l, c, lambda h: dot_nt(grad_pre, W[l, 1, h].reshape(640, PART)))
 
     def feed_back_rows(l, c):
         a = 6 - 2 * l
@@ -469,13 +465,13 @@
         gkeep[c, :, 160:480] += far[:, 0:320]
         grads = gkeep[c].astype(BF)
         gproj[c] = grads
+        rs_start(7 - 2 * l, c, lambda h: dot_nt(grads, W[l, 0, h, :, :, :, 0:512].reshape(640, 512)))
         total = jnp.sum(grads.astype(F32), axis=0, keepdims=True)
         if l:
             gb[1:2, 0:512] += total
         else:
             for i in range(4):
                 gq[i : i + 1, :] += total[:, 128 * i : 128 * i + 128]
-        rs_start(7 - 2 * l, c, lambda h: dot_nt(grads, W[l, 0, h, :, :, :, 0:512].reshape(640, 512)))
 
     def project_back_rows(l, c):
         a = 7 - 2 * l
@@ -517,11 +513,12 @@
             rest = dW[l, 0, m, :, :, :, 384:512].astype(F32).reshape(640, 128) + grad[:, 384:512]
             dW[l, 0, m, :, :, :, 384:512] = rest.astype(BF).reshape(4, 2, SHARD, 128)
 
+    gather_one(QKV0)
+
     @pl.loop(1, SHARDS)
     def _(k):
         remote(VG.at[me], VG.at[me], vs.at[0], vrs.at[0], shard_dev(k)[1]).start()
 
-    gather_one(QKV0)
     gather_one(OUT0)
     pack(0, 1)
     pack(0, 2)
@@ -544,8 +541,7 @@
     cp_h.wait()
     cp_c.wait()
     gather_one(UP0)
-    gather_one(DOWN0Z)
-    gather_one(DOWN0X)
+    gather_one(DOWN0)
     for c in range(MICRO):
         whole = FB[0, c].reshape(ROWS, D).astype(F32)
         unit, _ = norm_parts(whole)
@@ -574,8 +570,8 @@
 
     def norm_sums():
         for i in range(11):
-            GT[i, 0:8] = GV[0, :, 128 * i : 128 * i + 128]
-            GT[i, 8:16] = GV[1, :, 128 * i : 128 * i + 128]
+            lanes = slice(128 * i, 128 * i + 128)
+            GT[i] = jnp.concatenate([GV[0, :, lanes], GV[1, :, lanes]], axis=0).astype(BF)
 
         @pl.loop(1, SHARDS)
         def _(k):
@@ -610,42 +606,37 @@
     g1, g2, g3, g4 = gather_one, ring_two, ring_three, ring_wait
     d1, d2, d3 = reduce_one, reduce_two, reduce_three
     before = {
-        2: [(g2, DOWN0X)],
-        3: [(g2, DOWN0Z), (gather_wait, OUT0)],
-        4: [(g3, UP0), (g1, PROJ1)],
-        5: [(g3, DOWN0Z), (g3, DOWN0X)],
-        6: [(g4, UP0), (g2, PROJ1), (g1, UP1)],
-        8: [(g3, PROJ1), (g2, UP1), (g1, DOWN1)],
-        9: [(g4, PROJ1)],
-        10: [(g3, UP1), (g2, DOWN1)],
+        3: [(g2, DOWN0), (gather_wait, OUT0)],
+        4: [(g1, PROJ1)],
+        5: [(g3, DOWN0), (g2, PROJ1)],
+        6: [(g4, UP0), (g1, UP1)],
+        7: [(g3, PROJ1), (g2, UP1), (g1, DOWN1)],
+        9: [(g4, PROJ1), (g3, UP1), (g2, DOWN1)],
         12: [(g3, DOWN1)],
         15: [(g4, UP1)],
     }
     between = {
-        3: [(pack, 1, 0)],
+        3: [(g3, UP0), (pack, 1, 0)],
         4: [(pack, 1, 1)],
         5: [(pack, 1, 2)],
         6: [(mask_grads,)],
         18: [(down_grad, 1), (d1, 1, DOWN)],
         20: [(up_grad, 1), (d1, 1, UP)],
+        22: [(d2, 1, DOWN)],
         24: [(out_grad, 1), (d1, 1, OUT)],
-        25: [(d2, 1, UP)],
         26: [(qkv_grad, 1), (d1, 1, QKV)],
         27: [(d2, 1, OUT)],
         29: [(down_grad, 0), (d1, 0, DOWN)],
         30: [(up_grad, 0), (d1, 0, UP)],
-        31: [(bias_sums,)],
+        31: [(d2, 1, QKV), (bias_sums,)],
         33: [(out_grad, 0), (d1, 0, OUT)],
         34: [(d2, 0, DOWN)],
         35: [(qkv_grad, 0), (d1, 0, QKV), (last_sums,)],
         36: [(d2, 0, OUT)],
     }
     later = {
-        24: [(d2, 1, DOWN)],
-        27: [(d3, 1, DOWN)],
-        28: [(d3, 1, UP)],
-        33: [(d2, 1, QKV)],
-        34: [(d2, 0, UP), (d3, 1, OUT)],
+        25: [(d2, 1, UP)],
+        34: [(d2, 0, UP)],
     }
     for n in range(len(steps) + 2):
         for fn, *where in before.get(n, ()):
@@ -660,6 +651,8 @@
             sums[steps[n - 1][1]][0]()
         if n == len(steps):
             norm_sums()
+        if n == len(steps) + 1:
+            reduce_two(0, QKV)
         if n >= 2 and steps[n - 2][1] is not None:
             a, c = steps[n - 2][1]
             ag_mid(sums[a, c][1], sums[a, c][2], a, c)
@@ -671,13 +664,13 @@
             cp_o.start()
 
     cp_g.start()
-    for l, i in ((1, QKV), (0, DOWN), (0, UP)):
+    for l, i in ((1, DOWN), (1, UP), (1, OUT), (1, QKV)):
         reduce_three(l, i)
     wait_bytes(vr, er.at[0])
     wait_bytes(vr, es.at[0])
-    own = GT[pl.ds(SHARD * me // 128, 2)]
+    own = GT[pl.ds(SHARD * me // 128, 2)].astype(F32)
     for k in range(SHARDS - 1):
-        own = own + vr[k]
+        own = own + vr[k].astype(F32)
     vr2[7] = own
 
     @pl.loop(1, 8)
@@ -696,8 +689,7 @@
     bsum_ref[...] = totals
     for i in range(4):
         bsum_ref[0:1, 128 * i : 128 * i + 128] = lasts[i : i + 1]
-    reduce_two(0, QKV)
-    for l, i in ((0, OUT),):
+    for l, i in ((0, DOWN), (0, UP), (0, OUT)):
         reduce_three(l, i)
     wait_bytes(vr2.at[pl.ds(0, 7)], er.at[2])
     wait_bytes(vr2.at[pl.ds(0, 7)], es.at[2])
@@ -780,8 +772,8 @@
         pltpu.VMEM((SHARDS, 16, 256), BF),
         pltpu.VMEM((2, 8, 1408), F32),
         pltpu.VMEM((2, 8, 1408), F32),
-        pltpu.VMEM((11, 16, 128), F32),
-        pltpu.VMEM((SHARDS - 1, 2, 16, 128), F32),
+        pltpu.VMEM((11, 16, 128), BF),
+        pltpu.VMEM((SHARDS - 1, 2, 16, 128), BF),
         pltpu.VMEM((8, 2, 16, 128), F32),
         pltpu.VMEM((8, PART), F32),
         pltpu.VMEM((SHARDS - 1, 8, PART), F32),

time: 218 us -> 214 us (0.982)
  Pallas kernels: 218 us -> 212 us
    pallas_call x1, Pallas kernels: 213 us -> 207 us  [body(): pl.pallas_call(kernel, name='encoder', out_shape=(jax.ShapeDtypeStruct(bl...]
where the time goes in v7:
time: 214 us; the launch traced here: 213 us
  Pallas kernels  212 us (99%)
    pallas_call x1, Pallas kernels, body(): pl.pallas_call(kernel, name='encoder', out_shape=(jax.ShapeDtypeStruct(bl...  207 us
    pallas_call x1, Pallas kernels, body(): pl.pallas_call(finish, name='finish', out_shape=tuple((jax.ShapeDtypeStru...  4.66 us

profile of v7, /device:TPU:0, one launch (start us, length us, event | category | flops | bytes accessed | tf_op | source)
XLA Modules:
  0.0 212.9 jit_solution(1514048171779205610)
XLA Ops:
  0.6 207.4 %encoder.1 = (bf16[3,4,2,16,1280]{4,3,2,1,0:T(8,128)(2,1)}, bf16[3,4,2,16,1280]{4,3,2,1,0:T(8,128)(2,1)}, f32[2,3,80,640]{3,2,1,0:T(8,128)}, f32[2,16,128]{2,1,0:T(8,128)}, f32[8,640]{1,0:T(8,128)}) custom-call(bf16[3,4,2,16,1280]{4,3,2,1,0:T(8,128)(2,1)} %bitcast.6, bf16[3,4,2,16,1280]{4,3,2,1,0:T(8,128)(2,1)} %bitcast.7, s32[3]{0:T(128)} %len_ref.1, ...), custom_call_target="tpu_custom_call" | custom-call | tf_op jit(solution)/shard_map/encoder/pallas_call | solution.py:792
  208.0 4.7 %finish.1 = (f32[3,128,1280]{2,1,0:T(8,128)}, f32[3,128,1280]{2,1,0:T(8,128)}, f32[2,3,80,160]{3,2,1,0:T(8,128)}, f32[2,2,160]{2,1,0:T(2,128)}, f32[2,160,80]{2,...) custom-call(bf16[3,128,1280]{2,1,0:T(8,128)(2,1)} %bitcast.8, ...), custom_call_target="tpu_custom_call" | custom-call | tf_op jit(solution)/shard_map/finish/pallas_call | solution.py:817

commit v8 on v7

--- a/solution.py
+++ b/solution.py
@@ -317,25 +317,29 @@
                 part.at[c, :, other, :, lanes], dr.at[a, c, :, :, lanes], s1.at[c, h], r1.at[a, c, h], core_dev
             ).start()
 
+    def place(a, c):
+        return c + MICRO if a == 3 else c
+
     def rs_mid(a, c):
+        q = place(a, c)
         for h in range(2):
             lanes = slice(640 * h, 640 * h + 640)
             half = dr.at[a, c, :, :, lanes]
             wait_bytes(half, r1.at[a, c, h])
             wait_bytes(half, s1.at[c, h])
-            sb[c, :, :, lanes] = (
+            sb[q, :, :, lanes] = (
                 part[c, :, core, :, lanes].astype(F32) + dr[a, c, :, :, lanes].astype(F32)
             ).astype(BF)
             for k in (2, 1, 3):
                 j, dev = y_dev(k)
                 remote(
-                    sb.at[c, j, :, lanes], yr.at[a, c, k - 1, :, lanes], s2.at[c], r2.at[a, c], dev
+                    sb.at[q, j, :, lanes], yr.at[a, c, k - 1, :, lanes], s2.at[q], r2.at[a, c], dev
                 ).start()
 
     def rs_end(a, c):
         wait_bytes(yr.at[a, c], r2.at[a, c])
-        wait_bytes(yr.at[a, c], s2.at[c])
-        total = sb[c, y].astype(F32)
+        wait_bytes(yr.at[a, c], s2.at[place(a, c)])
+        total = sb[place(a, c), y].astype(F32)
         for k in range(3):
             total = total + yr[a, c, k].astype(F32)
         return total
@@ -344,16 +348,16 @@
         buf[i, c, y, core] = value.astype(BF)
         for k in (2, 1, 3):
             _, dev = y_dev(k)
-            remote(buf.at[i, c, y, core], buf.at[i, c, y, core], s3.at[c], r3.at[a, c], dev).start()
+            remote(buf.at[i, c, y, core], buf.at[i, c, y, core], s3.at[place(a, c)], r3.at[a, c], dev).start()
 
     def ag_mid(buf, i, a, c):
         wait_bytes(yr.at[a, c], r3.at[a, c])
-        wait_bytes(yr.at[a, c], s3.at[c])
-        remote(buf.at[i, c, :, core], buf.at[i, c, :, core], s4.at[c], r4.at[a, c], core_dev).start()
+        wait_bytes(yr.at[a, c], s3.at[place(a, c)])
+        remote(buf.at[i, c, :, core], buf.at[i, c, :, core], s4.at[place(a, c)], r4.at[a, c], core_dev).start()
 
     def ag_end(a, c):
         wait_bytes(dr.at[a, c], r4.at[a, c])
-        wait_bytes(dr.at[a, c], s4.at[c])
+        wait_bytes(dr.at[a, c], s4.at[place(a, c)])
 
     def heads_of(l, c):
         own = qkv[l, c].astype(F32)
@@ -620,7 +624,7 @@
         4: [(pack, 1, 1)],
         5: [(pack, 1, 2)],
         6: [(mask_grads,)],
-        18: [(down_grad, 1), (d1, 1, DOWN)],
+        17: [(down_grad, 1), (d1, 1, DOWN)],
         20: [(up_grad, 1), (d1, 1, UP)],
         22: [(d2, 1, DOWN)],
         24: [(out_grad, 1), (d1, 1, OUT)],
@@ -647,20 +651,29 @@
             fn(*where)
         if n < len(steps) and steps[n][1] is not None:
             rs_mid(*steps[n][1])
-        if 1 <= n <= len(steps) and steps[n - 1][1] is not None:
-            sums[steps[n - 1][1]][0]()
+        if n == 18:
+            for c in range(MICRO):
+                sums[3, c][0]()
+        one = steps[n - 1][1] if 1 <= n <= len(steps) else None
+        two = steps[n - 2][1] if n >= 2 else None
+        if one is not None and one[0] != 3:
+            sums[one][0]()
         if n == len(steps):
             norm_sums()
         if n == len(steps) + 1:
             reduce_two(0, QKV)
-        if n >= 2 and steps[n - 2][1] is not None:
-            a, c = steps[n - 2][1]
-            ag_mid(sums[a, c][1], sums[a, c][2], a, c)
+        if n == 22:
+            for c in range(MICRO):
+                ag_mid(FB, 4, 3, c)
+        if two is not None and two[0] != 3:
+            ag_mid(sums[two][1], sums[two][2], *two)
         for fn, *where in later.get(n, ()):
             fn(*where)
-        if n >= 2 and steps[n - 2][1] is not None:
-            ag_end(*steps[n - 2][1])
-        if n == 19:
+        if two is not None and two[0] != 3:
+            ag_end(*two)
+        if n == 22:
+            for c in range(MICRO):
+                ag_end(3, c)
             cp_o.start()
 
     cp_g.start()
@@ -753,7 +766,7 @@
         pltpu.VMEM((8, MICRO, 4, 16, D), BF),
         pltpu.VMEM((8, MICRO, 3, 16, D), BF),
         pltpu.VMEM(blocks, BF),
-        pltpu.VMEM((MICRO, 4, 16, D), BF),
+        pltpu.VMEM((2 * MICRO, 4, 16, D), BF),
         pltpu.VMEM((2, MICRO, ROWS, 512), BF),
         pltpu.VMEM((2, MICRO, ROWS, 384), BF),
         pltpu.VMEM((2, MICRO, 2 * ROWS, 2 * ROWS), F32),
@@ -784,8 +797,8 @@
         pltpu.VMEM((2, 3, SHARD, PART), F32),
         dma((8, 2)), dma((8, 2)), dma((8, 2)), dma((8, 2)), dma((8, 2)), dma((8, 2)),
         dma((2, 4, 2)), dma((2, 4, 2)), dma((2, 4, 2)), dma((2, 4, 2)),
-        dma((MICRO, 2)), dma((8, MICRO, 2)), dma((MICRO,)), dma((8, MICRO)),
-        dma((MICRO,)), dma((8, MICRO)), dma((MICRO,)), dma((8, MICRO)),
+        dma((MICRO, 2)), dma((8, MICRO, 2)), dma((2 * MICRO,)), dma((8, MICRO)),
+        dma((2 * MICRO,)), dma((8, MICRO)), dma((2 * MICRO,)), dma((8, MICRO)),
         dma((2, MICRO)), dma((2, MICRO)), dma((MICRO,)), dma((2, MICRO)),
         dma((1,)), dma((1,)), dma((4,)), dma((4,)), dma((2,)), dma((2, 2)), dma((2, 4, 2)),
     ]

time: 214 us -> 213 us (level)
  no operation moved by 1% of the time
where the time goes in v8:
time: 213 us; the launch traced here: 212 us
  Pallas kernels  211 us (99%)
    pallas_call x1, Pallas kernels, body(): pl.pallas_call(kernel, name='encoder', out_shape=(jax.ShapeDtypeStruct(bl...  206 us
    pallas_call x1, Pallas kernels, body(): pl.pallas_call(finish, name='finish', out_shape=tuple((jax.ShapeDtypeStru...  4.66 us

profile of v8, /device:TPU:0, one launch (start us, length us, event | category | flops | bytes accessed | tf_op | source)
XLA Modules:
  0.0 211.7 jit_solution(16213455128588397620)
XLA Ops:
  0.6 206.2 %encoder.1 = (bf16[3,4,2,16,1280]{4,3,2,1,0:T(8,128)(2,1)}, bf16[3,4,2,16,1280]{4,3,2,1,0:T(8,128)(2,1)}, f32[2,3,80,640]{3,2,1,0:T(8,128)}, f32[2,16,128]{2,1,0:T(8,128)}, f32[8,640]{1,0:T(8,128)}) custom-call(bf16[3,4,2,16,1280]{4,3,2,1,0:T(8,128)(2,1)} %bitcast.6, bf16[3,4,2,16,1280]{4,3,2,1,0:T(8,128)(2,1)} %bitcast.7, s32[3]{0:T(128)} %len_ref.1, ...), custom_call_target="tpu_custom_call" | custom-call | tf_op jit(solution)/shard_map/encoder/pallas_call | solution.py:805
  206.9 4.7 %finish.1 = (f32[3,128,1280]{2,1,0:T(8,128)}, f32[3,128,1280]{2,1,0:T(8,128)}, f32[2,3,80,160]{3,2,1,0:T(8,128)}, f32[2,2,160]{2,1,0:T(2,128)}, f32[2,160,80]{2,...) custom-call(bf16[3,128,1280]{2,1,0:T(8,128)(2,1)} %bitcast.8, ...), custom_call_target="tpu_custom_call" | custom-call | tf_op jit(solution)/shard_map/finish/pallas_call | solution.py:830
